TPU v7x, 32 devices: a whole 2x2x4 slice. The times are simulated.
32 devices in a mesh: dp: 4 (over y, core), expert: 4 (over z), seq: 2 (over x).
Axes of the slice: x: 2, y: 2, z: 4, core: 2. Of those that a mesh axis runs over, the one named last changes fastest.
Arguments:
- inputs: bfloat16 [8, 1024, 2048], P('dp', ('expert', 'seq')), may hold values from -6 to 6
- lengths: int32 [8], P('dp'), may hold values from 256 to 1024, as said below
- attn_routes: int32 [8, 1024, 2], P('dp', ('expert', 'seq')), may hold values from 0 to 3, all different within a row
- mlp_routes: int32 [8, 1024, 2], P('dp', ('expert', 'seq')), may hold values from 0 to 3, all different within a row
- slot_order: int32 [4, 8, 256], P('dp', ('expert', 'seq')), may hold values from 0 to 255, each once within a row
- gain_attn: bfloat16 [2048], P(('dp', 'seq')), may hold values from 0.099609375 to 1.8984375
- router_attn: bfloat16 [2048, 4], P(('dp', 'seq')), may hold values from -0.09375 to 0.09375
- w_key: bfloat16 [2048, 2048], P(('dp', 'seq')), may hold values from -0.125 to 0.125
- w_value: bfloat16 [2048, 2048], P(('dp', 'seq')), may hold values from -0.125 to 0.125
- w_query: bfloat16 [4, 2048, 2048], P('expert', ('dp', 'seq')), may hold values from -0.125 to 0.125
- w_out: bfloat16 [4, 2048, 2048], P('expert', ('dp', 'seq')), may hold values from -1.5 to 1.5
- gain_mlp: bfloat16 [2048], P(('dp', 'seq')), may hold values from 0.099609375 to 1.8984375
- router_mlp: bfloat16 [2048, 4], P(('dp', 'seq')), may hold values from -0.09375 to 0.09375
- w_gate: bfloat16 [4, 2048, 5632], P('expert', None, ('dp', 'seq')), may hold values from -0.125 to 0.125
- w_up: bfloat16 [4, 2048, 5632], P('expert', None, ('dp', 'seq')), may hold values from -0.125 to 0.125
- w_down: bfloat16 [4, 5632, 2048], P('expert', ('dp', 'seq')), may hold values from -0.109375 to 0.109375
- d_out: bfloat16 [8, 1024, 2048], P('dp', ('expert', 'seq')), may hold values from -6 to 6
Outputs:
- block_out: bfloat16 [8, 1024, 2048], P('dp', ('expert', 'seq'))
- grad_x: bfloat16 [8, 1024, 2048], P('dp', ('expert', 'seq'))
- grad_gain_attn: float32 [2048], P(('dp', 'seq'))
- grad_router_attn: float32 [2048, 4], P(('dp', 'seq'))
- grad_w_key: float32 [2048, 2048], P(('dp', 'seq'))
- grad_w_value: float32 [2048, 2048], P(('dp', 'seq'))
- grad_w_query: float32 [4, 2048, 2048], P('expert', ('dp', 'seq'))
- grad_w_out: float32 [4, 2048, 2048], P('expert', ('dp', 'seq'))
- grad_gain_mlp: float32 [2048], P(('dp', 'seq'))
- grad_router_mlp: float32 [2048, 4], P(('dp', 'seq'))
- grad_w_gate: float32 [4, 2048, 5632], P('expert', None, ('dp', 'seq'))
- grad_w_up: float32 [4, 2048, 5632], P('expert', None, ('dp', 'seq'))
- grad_w_down: float32 [4, 5632, 2048], P('expert', ('dp', 'seq'))
Inputs may be any that keep to these rules, and one draw needn't show every extreme that they name: `lengths`: in each group of 2 consecutive sequences one has exactly 1024 valid slots. `attn_routes`: each slot names 2 different experts; every expert is named by some slot. `mlp_routes`: each slot names 2 different experts; every expert is named by some slot. `slot_order`: the 256 values of each row are a permutation.
All inputs are finite; a program needn't handle non-finite values.
Results may differ from a plain program's by a relative error of at most 0.025.
Values may be sent and summed in bfloat16 or wider, within the bound.
No kernel may reach another device: no remote copies, remote signals or barrier semaphores. Data moves between devices by JAX's collectives and lax.ppermute only.
A program may use at most 384 MiB of HBM per device.

v0:
```python
import jax
import jax.numpy as jnp
from jax import lax
from jax.sharding import PartitionSpec as P

HEAD = 128


EPS = 1e-06
NEG = -1e30
HIGH = lax.Precision.HIGHEST


def route_pairs(routes, order, is_valid, experts, capacity):
    tokens_here, top_count = routes.shape
    pairs = tokens_here * top_count
    target = routes.reshape(pairs)
    second = lax.broadcasted_iota(jnp.int32, routes.shape, 1)
    priority = (order[:, None] * top_count + second).reshape(pairs)
    living = jnp.broadcast_to(is_valid[:, None], routes.shape).reshape(pairs)
    earlier = (
        (target[:, None] == target[None, :])
        & (priority[None, :] < priority[:, None])
        & living[None, :]
    )
    slot_index = jnp.sum(earlier.astype(jnp.int32), axis=1, dtype=jnp.int32)
    kept_pair = living & (slot_index < capacity)
    expert_ids = lax.broadcasted_iota(jnp.int32, (1, experts, 1), 1)
    slot_ids = lax.broadcasted_iota(jnp.int32, (1, 1, capacity), 2)
    table = (
        kept_pair[:, None, None]
        & (target[:, None, None] == expert_ids)
        & (slot_index[:, None, None] == slot_ids)
    )
    pair_ids = lax.broadcasted_iota(jnp.int32, (pairs, 1, 1), 0)
    source_pair = jnp.sum(jnp.where(table, pair_ids, 0), axis=0, dtype=jnp.int32)
    filled = jnp.any(table, axis=0)
    flat_slot = target * capacity + jnp.minimum(slot_index, capacity - 1)
    return (kept_pair.reshape(routes.shape), source_pair, filled, flat_slot)


def rms_norm(values, gain):
    return values * lax.rsqrt(jnp.mean(values * values, axis=1, keepdims=True) + EPS) * gain


def norm_back(values, gain, grad):
    factor = lax.rsqrt(jnp.mean(values * values, axis=1, keepdims=True) + EPS)
    unit = values * factor
    gain_grad = jnp.sum(grad * unit, axis=0)
    scaled = grad * gain
    return (factor * (scaled - unit * jnp.mean(scaled * unit, axis=1, keepdims=True)), gain_grad)


def gate_values(normed, router, routes):
    logits = jnp.dot(normed, router, preferred_element_type=jnp.float32)
    chosen = jnp.take_along_axis(logits, routes, axis=1)
    top = jnp.max(chosen, axis=1, keepdims=True)
    expo = jnp.exp(chosen - top)
    return expo / jnp.sum(expo, axis=1, keepdims=True)


def gate_grads(normed, router, routes, gates, gate_grad):
    chosen = gates * (gate_grad - jnp.sum(gates * gate_grad, axis=1, keepdims=True))
    expert_ids = lax.broadcasted_iota(jnp.int32, (1, 1, router.shape[1]), 2)
    logit_grad = jnp.sum(
        jnp.where(routes[:, :, None] == expert_ids, chosen[:, :, None], 0.0), axis=1
    )
    router_grad = jnp.dot(normed.astype(jnp.float32).T, logit_grad, precision=HIGH)
    input_grad = jnp.dot(logit_grad, router.astype(jnp.float32).T, precision=HIGH)
    return (router_grad, input_grad)


def head_split(matrix, groups):
    rows = matrix.shape[0]
    return matrix.reshape(rows, groups, matrix.shape[1] // groups).transpose(1, 0, 2)


def head_join(stacked):
    groups, rows, piece = stacked.shape
    return stacked.transpose(1, 0, 2).reshape(rows, groups * piece)


def visibility(row_codes, key_limit, seq_len):
    key_codes = lax.broadcasted_iota(jnp.int32, (1, key_limit.shape[0]), 1)
    same_seq = key_codes // seq_len == row_codes[:, None] // seq_len
    return same_seq & (key_codes <= row_codes[:, None]) & (key_codes % seq_len < key_limit[None, :])


def attention_forward(query, keys, values, visible):
    groups = min(4, query.shape[1] // HEAD)
    scale = HEAD ** (-0.5)

    def one_group(parts):
        part_q, part_k, part_v = parts
        rows = part_q.shape[0]
        q_four = part_q.reshape(rows, -1, HEAD)
        k_four = part_k.reshape(part_k.shape[0], -1, HEAD)
        v_four = part_v.reshape(part_v.shape[0], -1, HEAD)
        scores = (
            jnp.einsum("rhd,khd->hrk", q_four, k_four, preferred_element_type=jnp.float32) * scale
        )
        scores = jnp.where(visible[None], scores, NEG)
        top = jnp.max(scores, axis=2, keepdims=True)
        expo = jnp.exp(scores - top)
        total = jnp.sum(expo, axis=2, keepdims=True)
        probs = (expo / total).astype(jnp.bfloat16)
        mixed = jnp.einsum("hrk,khd->rhd", probs, v_four, preferred_element_type=jnp.float32)
        return (
            mixed.reshape(rows, -1).astype(jnp.bfloat16),
            jnp.transpose((top + jnp.log(total))[:, :, 0]),
        )

    mixed, log_total = lax.map(
        one_group, (head_split(query, groups), head_split(keys, groups), head_split(values, groups))
    )
    return (head_join(mixed), head_join(log_total))


def attention_backward(query, keys, values, visible, log_total, mixed_grad):
    groups = min(4, query.shape[1] // HEAD)
    scale = HEAD ** (-0.5)

    def one_group(parts):
        part_q, part_k, part_v, part_l, part_g = parts
        rows = part_q.shape[0]
        count = part_k.shape[0]
        q_four = part_q.reshape(rows, -1, HEAD)
        k_four = part_k.reshape(count, -1, HEAD)
        v_four = part_v.reshape(count, -1, HEAD)
        g_four = part_g.reshape(rows, -1, HEAD)
        scores = (
            jnp.einsum("rhd,khd->hrk", q_four, k_four, preferred_element_type=jnp.float32) * scale
        )
        scores = jnp.where(visible[None], scores, NEG)
        probs = jnp.exp(scores - jnp.transpose(part_l)[:, :, None])
        prob_grad = jnp.einsum("rhd,khd->hrk", g_four, v_four, preferred_element_type=jnp.float32)
        center = jnp.sum(probs * prob_grad, axis=2, keepdims=True)
        score_grad = (probs * (prob_grad - center)).astype(jnp.bfloat16)
        query_grad = (
            jnp.einsum("hrk,khd->rhd", score_grad, k_four, preferred_element_type=jnp.float32)
            * scale
        ).astype(jnp.bfloat16)
        key_grad = (
            jnp.einsum("hrk,rhd->khd", score_grad, q_four, preferred_element_type=jnp.float32)
            * scale
        )
        value_grad = jnp.einsum(
            "hrk,rhd->khd", probs.astype(jnp.bfloat16), g_four, preferred_element_type=jnp.float32
        )
        return (
            query_grad.reshape(rows, -1),
            key_grad.reshape(count, -1),
            value_grad.reshape(count, -1),
        )

    parts = (
        head_split(query, groups),
        head_split(keys, groups),
        head_split(values, groups),
        head_split(log_total, groups),
        head_split(mixed_grad, groups),
    )
    query_grad, key_grad, value_grad = lax.map(one_group, parts)
    return (head_join(query_grad), head_join(key_grad), head_join(value_grad))


def body(
    inputs,
    lengths,
    attn_routes,
    mlp_routes,
    slot_order,
    gain_attn,
    router_attn,
    w_key,
    w_value,
    w_query,
    w_out,
    gain_mlp,
    router_mlp,
    w_gate,
    w_up,
    w_down,
    d_out,
):
    seq_count, stretch, width = inputs.shape
    tok_rows = seq_count * stretch
    top_count = attn_routes.shape[2]
    experts = router_attn.shape[1]
    capacity = top_count * tok_rows // experts
    seq_len = stretch * lax.axis_size(("expert", "seq"))
    block = lax.axis_index(("expert", "seq"))
    column = lax.broadcasted_iota(jnp.int32, (seq_count, stretch), 1)
    seq_row = lax.broadcasted_iota(jnp.int32, (seq_count, stretch), 0)
    place = block * stretch + column
    is_valid = (place < lengths[:, None]).reshape(tok_rows)
    row_codes = (seq_row * seq_len + place).reshape(tok_rows)
    order = slot_order.reshape(tok_rows)
    attn_idx = attn_routes.reshape(tok_rows, top_count)
    mlp_idx = mlp_routes.reshape(tok_rows, top_count)
    attn_kept, attn_pair, attn_filled, attn_flat = route_pairs(
        attn_idx, order, is_valid, experts, capacity
    )
    mlp_kept, mlp_pair, mlp_filled, mlp_flat = route_pairs(
        mlp_idx, order, is_valid, experts, capacity
    )
    attn_keep = attn_kept.astype(jnp.float32)
    mlp_keep = mlp_kept.astype(jnp.float32)
    gate_w = w_gate[0]
    up_w = w_up[0]
    down_w = w_down[0]
    norm_one, route_one, key_w, value_w, query_full, out_full, norm_two, route_two = (
        lax.all_gather(gain_attn, ("dp", "seq"), axis=0, tiled=True),
        lax.all_gather(router_attn, ("dp", "seq"), axis=0, tiled=True),
        lax.all_gather(w_key, ("dp", "seq"), axis=0, tiled=True),
        lax.all_gather(w_value, ("dp", "seq"), axis=0, tiled=True),
        lax.all_gather(w_query, ("dp", "seq"), axis=1, tiled=True),
        lax.all_gather(w_out, ("dp", "seq"), axis=1, tiled=True),
        lax.all_gather(gain_mlp, ("dp", "seq"), axis=0, tiled=True),
        lax.all_gather(router_mlp, ("dp", "seq"), axis=0, tiled=True),
    )
    query_w = query_full[0]
    out_w = out_full[0]
    x_in = inputs.astype(jnp.float32).reshape(tok_rows, width)
    normed_one = rms_norm(x_in, norm_one.astype(jnp.float32)).astype(jnp.bfloat16)
    attn_gates = gate_values(normed_one, route_one, attn_idx)
    keys_here = jnp.dot(normed_one, key_w, preferred_element_type=jnp.float32).astype(jnp.bfloat16)
    values_here = jnp.dot(normed_one, value_w, preferred_element_type=jnp.float32).astype(
        jnp.bfloat16
    )
    keys_seq, values_seq = (
        lax.all_gather(
            keys_here.reshape(seq_count, stretch, -1), ("expert", "seq"), axis=1, tiled=True
        ),
        lax.all_gather(
            values_here.reshape(seq_count, stretch, -1), ("expert", "seq"), axis=1, tiled=True
        ),
    )
    keys_all = keys_seq.reshape(seq_count * seq_len, -1)
    values_all = values_seq.reshape(seq_count * seq_len, -1)
    key_owner = lax.broadcasted_iota(jnp.int32, (seq_count, seq_count * seq_len), 1) // seq_len
    seq_ids = lax.broadcasted_iota(jnp.int32, (seq_count, seq_count * seq_len), 0)
    key_limit = jnp.sum(
        jnp.where(key_owner == seq_ids, lengths[:, None], 0), axis=0, dtype=jnp.int32
    )
    attn_token = attn_pair // top_count
    attn_send = jnp.where(
        attn_filled[:, :, None], normed_one[attn_token], jnp.zeros((), jnp.bfloat16)
    )
    attn_codes = jnp.where(attn_filled, row_codes[attn_token], 0)
    rows_in = lax.all_to_all(attn_send, "expert", split_axis=0, concat_axis=0, tiled=True)
    codes_in = lax.all_to_all(attn_codes, "expert", split_axis=0, concat_axis=0, tiled=True)
    senders, count = codes_in.shape
    flat_rows = rows_in.reshape(senders * count, width)
    query = jnp.dot(flat_rows, query_w, preferred_element_type=jnp.float32).astype(jnp.bfloat16)
    visible = visibility(codes_in.reshape(-1), key_limit, seq_len)
    mixed, log_total = attention_forward(query, keys_all, values_all, visible)
    result = jnp.dot(mixed, out_w, preferred_element_type=jnp.float32).astype(jnp.bfloat16)
    returned = lax.all_to_all(
        result.reshape(senders, count, width), "expert", split_axis=0, concat_axis=0, tiled=True
    )
    attn_rows = rows_in
    attn_query = query.reshape(senders, count, -1)
    attn_mixed = mixed.reshape(senders, count, -1)
    attn_lse = log_total.reshape(senders, count, -1)
    attn_pairs = (
        returned.reshape(experts * capacity, width)[attn_flat]
        .astype(jnp.float32)
        .reshape(tok_rows, top_count, width)
    )
    attn_weight = attn_gates * attn_keep
    hidden_in = x_in + jnp.sum(attn_weight[:, :, None] * attn_pairs, axis=1)
    normed_two = rms_norm(hidden_in, norm_two.astype(jnp.float32)).astype(jnp.bfloat16)
    mlp_gates = gate_values(normed_two, route_two, mlp_idx)
    mlp_weight = mlp_gates * mlp_keep
    grad_out = d_out.astype(jnp.float32).reshape(tok_rows, width)
    mlp_pair_grad = (
        (mlp_weight[:, :, None] * grad_out[:, None, :])
        .astype(jnp.bfloat16)
        .reshape(tok_rows * top_count, width)
    )
    mlp_send = jnp.where(
        mlp_filled[:, :, None], normed_two[mlp_pair // top_count], jnp.zeros((), jnp.bfloat16)
    )
    mlp_grad_send = jnp.where(
        mlp_filled[:, :, None], mlp_pair_grad[mlp_pair], jnp.zeros((), jnp.bfloat16)
    )
    rows_in = lax.all_to_all(mlp_send, "expert", split_axis=0, concat_axis=0, tiled=True)
    grads_in = lax.all_to_all(mlp_grad_send, "expert", split_axis=0, concat_axis=0, tiled=True)
    senders, count, _ = rows_in.shape
    gathered_rows = lax.all_gather(rows_in, ("dp", "seq"), axis=0, tiled=True)
    gathered_grads = lax.all_gather(grads_in, ("dp", "seq"), axis=0, tiled=True)
    everyone = gathered_rows.shape[0]
    flat_rows = gathered_rows.reshape(everyone * count, width)
    flat_grads = gathered_grads.reshape(everyone * count, width)
    gate_pre = jnp.dot(flat_rows, gate_w, preferred_element_type=jnp.float32)
    up_pre = jnp.dot(flat_rows, up_w, preferred_element_type=jnp.float32)
    sigma = jax.nn.sigmoid(gate_pre)
    activated = gate_pre * sigma
    hidden_act = (activated * up_pre).astype(jnp.bfloat16)
    partial_out = jnp.dot(hidden_act, down_w, preferred_element_type=jnp.float32)
    hidden_grad = jnp.dot(flat_grads, down_w.T, preferred_element_type=jnp.float32)
    gate_grad = (hidden_grad * up_pre * sigma * (1.0 + gate_pre * (1.0 - sigma))).astype(
        jnp.bfloat16
    )
    up_grad = (hidden_grad * activated).astype(jnp.bfloat16)
    partial_in = jnp.dot(gate_grad, gate_w.T, preferred_element_type=jnp.float32) + jnp.dot(
        up_grad, up_w.T, preferred_element_type=jnp.float32
    )
    out_sum = lax.psum_scatter(
        partial_out.reshape(everyone, count, width).astype(jnp.bfloat16),
        ("dp", "seq"),
        scatter_dimension=0,
        tiled=True,
    )
    in_sum = lax.psum_scatter(
        partial_in.reshape(everyone, count, width).astype(jnp.bfloat16),
        ("dp", "seq"),
        scatter_dimension=0,
        tiled=True,
    )
    returned_out = lax.all_to_all(out_sum, "expert", split_axis=0, concat_axis=0, tiled=True)
    returned_in = lax.all_to_all(in_sum, "expert", split_axis=0, concat_axis=0, tiled=True)
    act_kept = hidden_act.reshape(everyone, count, -1)
    gate_grad_kept = gate_grad.reshape(everyone, count, -1)
    up_grad_kept = up_grad.reshape(everyone, count, -1)
    mlp_pairs = (
        returned_out.reshape(experts * capacity, width)[mlp_flat]
        .astype(jnp.float32)
        .reshape(tok_rows, top_count, width)
    )
    output = hidden_in + jnp.sum(mlp_weight[:, :, None] * mlp_pairs, axis=1)
    result_out = output.astype(jnp.bfloat16).reshape(seq_count, stretch, width)
    rows_flat = gathered_rows.reshape(-1, width)
    grads_flat = gathered_grads.reshape(-1, width)
    act_flat = act_kept.reshape(rows_flat.shape[0], -1)
    gate_grad_flat = gate_grad_kept.reshape(rows_flat.shape[0], -1)
    up_grad_flat = up_grad_kept.reshape(rows_flat.shape[0], -1)
    grad_gate = jnp.dot(rows_flat.T, gate_grad_flat, preferred_element_type=jnp.float32)
    grad_up = jnp.dot(rows_flat.T, up_grad_flat, preferred_element_type=jnp.float32)
    grad_down = jnp.dot(act_flat.T, grads_flat, preferred_element_type=jnp.float32)
    norm_one, route_one, key_w, value_w, query_full, out_full, norm_two, route_two = (
        lax.all_gather(gain_attn, ("dp", "seq"), axis=0, tiled=True),
        lax.all_gather(router_attn, ("dp", "seq"), axis=0, tiled=True),
        lax.all_gather(w_key, ("dp", "seq"), axis=0, tiled=True),
        lax.all_gather(w_value, ("dp", "seq"), axis=0, tiled=True),
        lax.all_gather(w_query, ("dp", "seq"), axis=1, tiled=True),
        lax.all_gather(w_out, ("dp", "seq"), axis=1, tiled=True),
        lax.all_gather(gain_mlp, ("dp", "seq"), axis=0, tiled=True),
        lax.all_gather(router_mlp, ("dp", "seq"), axis=0, tiled=True),
    )
    query_w = query_full[0]
    out_w = out_full[0]
    mlp_gate_grad = mlp_keep * jnp.sum(grad_out[:, None, :] * mlp_pairs, axis=2)
    back_pairs = (
        returned_in.reshape(experts * capacity, width)[mlp_flat]
        .astype(jnp.float32)
        .reshape(tok_rows, top_count, width)
    )
    router_two_grad, router_two_input = gate_grads(
        normed_two, route_two, mlp_idx, mlp_gates, mlp_gate_grad
    )
    normed_two_grad = jnp.sum(mlp_keep[:, :, None] * back_pairs, axis=1) + router_two_input
    residual_grad, norm_two_grad = norm_back(
        hidden_in, norm_two.astype(jnp.float32), normed_two_grad
    )
    hidden_total = grad_out + residual_grad
    attn_pair_grad = (
        (attn_weight[:, :, None] * hidden_total[:, None, :])
        .astype(jnp.bfloat16)
        .reshape(tok_rows * top_count, width)
    )
    attn_gate_grad = attn_keep * jnp.sum(hidden_total[:, None, :] * attn_pairs, axis=2)
    attn_grad_send = jnp.where(
        attn_filled[:, :, None], attn_pair_grad[attn_pair], jnp.zeros((), jnp.bfloat16)
    )
    attn_grad_rows = lax.all_to_all(
        attn_grad_send, "expert", split_axis=0, concat_axis=0, tiled=True
    ).reshape(experts * capacity, width)
    mixed_rows = attn_mixed.reshape(experts * capacity, -1)
    grad_out_w = jnp.dot(mixed_rows.T, attn_grad_rows, preferred_element_type=jnp.float32)
    mixed_grad = jnp.dot(attn_grad_rows, out_w.T, preferred_element_type=jnp.float32).astype(
        jnp.bfloat16
    )
    visible = visibility(codes_in.reshape(-1), key_limit, seq_len)
    query_grad, key_grad, value_grad = attention_backward(
        attn_query.reshape(experts * capacity, -1),
        keys_all,
        values_all,
        visible,
        attn_lse.reshape(experts * capacity, -1),
        mixed_grad,
    )
    rows_one = attn_rows.reshape(experts * capacity, width)
    grad_query = jnp.dot(rows_one.T, query_grad, preferred_element_type=jnp.float32)
    rows_one_grad = jnp.dot(query_grad, query_w.T, preferred_element_type=jnp.float32).astype(
        jnp.bfloat16
    )
    attn_grad_back = lax.all_to_all(
        rows_one_grad.reshape(experts, capacity, width),
        "expert",
        split_axis=0,
        concat_axis=0,
        tiled=True,
    )
    key_part, value_part = (
        lax.psum_scatter(
            key_grad.reshape(seq_count, seq_len, -1).astype(jnp.bfloat16),
            ("expert", "seq"),
            scatter_dimension=1,
            tiled=True,
        ).astype(jnp.float32),
        lax.psum_scatter(
            value_grad.reshape(seq_count, seq_len, -1).astype(jnp.bfloat16),
            ("expert", "seq"),
            scatter_dimension=1,
            tiled=True,
        ).astype(jnp.float32),
    )
    key_low = key_part.reshape(tok_rows, -1).astype(jnp.bfloat16)
    value_low = value_part.reshape(tok_rows, -1).astype(jnp.bfloat16)
    grad_key = jnp.dot(normed_one.T, key_low, preferred_element_type=jnp.float32)
    grad_value = jnp.dot(normed_one.T, value_low, preferred_element_type=jnp.float32)
    back_one = (
        attn_grad_back.reshape(experts * capacity, width)[attn_flat]
        .astype(jnp.float32)
        .reshape(tok_rows, top_count, width)
    )
    router_one_grad, router_one_input = gate_grads(
        normed_one, route_one, attn_idx, attn_gates, attn_gate_grad
    )
    normed_one_grad = jnp.sum(attn_keep[:, :, None] * back_one, axis=1) + router_one_input
    normed_one_grad = (
        normed_one_grad
        + jnp.dot(key_low, key_w.T, preferred_element_type=jnp.float32)
        + jnp.dot(value_low, value_w.T, preferred_element_type=jnp.float32)
    )
    input_grad, norm_one_grad = norm_back(x_in, norm_one.astype(jnp.float32), normed_one_grad)
    grad_x = (hidden_total + input_grad).astype(jnp.bfloat16).reshape(seq_count, stretch, width)
    summed = (
        lax.psum_scatter(
            norm_one_grad.astype(jnp.bfloat16), ("dp", "seq"), scatter_dimension=0, tiled=True
        ).astype(jnp.float32),
        lax.psum_scatter(
            router_one_grad.astype(jnp.bfloat16), ("dp", "seq"), scatter_dimension=0, tiled=True
        ).astype(jnp.float32),
        lax.psum_scatter(
            grad_key.astype(jnp.bfloat16), ("dp", "seq"), scatter_dimension=0, tiled=True
        ).astype(jnp.float32),
        lax.psum_scatter(
            grad_value.astype(jnp.bfloat16), ("dp", "seq"), scatter_dimension=0, tiled=True
        ).astype(jnp.float32),
        lax.psum_scatter(
            norm_two_grad.astype(jnp.bfloat16), ("dp", "seq"), scatter_dimension=0, tiled=True
        ).astype(jnp.float32),
        lax.psum_scatter(
            router_two_grad.astype(jnp.bfloat16), ("dp", "seq"), scatter_dimension=0, tiled=True
        ).astype(jnp.float32),
        lax.psum_scatter(
            grad_query[None].astype(jnp.bfloat16), ("dp", "seq"), scatter_dimension=1, tiled=True
        ).astype(jnp.float32),
        lax.psum_scatter(
            grad_out_w[None].astype(jnp.bfloat16), ("dp", "seq"), scatter_dimension=1, tiled=True
        ).astype(jnp.float32),
    )
    shared = (
        lax.psum(summed[0].astype(jnp.bfloat16), "expert").astype(jnp.float32),
        lax.psum(summed[1].astype(jnp.bfloat16), "expert").astype(jnp.float32),
        lax.psum(summed[2].astype(jnp.bfloat16), "expert").astype(jnp.float32),
        lax.psum(summed[3].astype(jnp.bfloat16), "expert").astype(jnp.float32),
        lax.psum(summed[4].astype(jnp.bfloat16), "expert").astype(jnp.float32),
        lax.psum(summed[5].astype(jnp.bfloat16), "expert").astype(jnp.float32),
    )
    return (
        result_out,
        grad_x,
        shared[0],
        shared[1],
        shared[2],
        shared[3],
        summed[6],
        summed[7],
        shared[4],
        shared[5],
        grad_gate[None],
        grad_up[None],
        grad_down[None],
    )


def solution(mesh):
    in_specs = (
        P("dp", ("expert", "seq"), None),
        P("dp"),
        P("dp", ("expert", "seq"), None),
        P("dp", ("expert", "seq"), None),
        P("dp", ("expert", "seq"), None),
        P(("dp", "seq")),
        P(("dp", "seq"), None),
        P(("dp", "seq"), None),
        P(("dp", "seq"), None),
        P("expert", ("dp", "seq"), None),
        P("expert", ("dp", "seq"), None),
        P(("dp", "seq")),
        P(("dp", "seq"), None),
        P("expert", None, ("dp", "seq")),
        P("expert", None, ("dp", "seq")),
        P("expert", ("dp", "seq"), None),
        P("dp", ("expert", "seq"), None),
    )
    out_specs = (
        P("dp", ("expert", "seq"), None),
        P("dp", ("expert", "seq"), None),
        P(("dp", "seq")),
        P(("dp", "seq"), None),
        P(("dp", "seq"), None),
        P(("dp", "seq"), None),
        P("expert", ("dp", "seq"), None),
        P("expert", ("dp", "seq"), None),
        P(("dp", "seq")),
        P(("dp", "seq"), None),
        P("expert", None, ("dp", "seq")),
        P("expert", None, ("dp", "seq")),
        P("expert", ("dp", "seq"), None),
    )
    return jax.shard_map(body, mesh=mesh, in_specs=in_specs, out_specs=out_specs, check_vma=False)
```

profile of v0, /device:TPU:0, one launch (start us, length us, event | category | flops | bytes accessed | tf_op | source)
XLA Modules:
  0.0 2432.6 jit_solution(1223203499186843237)
XLA Ops:
  9.5 13.6 all-gather
  28.3 38.8 %all-gather.17.cloned.1.call-done = bf16[2048,2048]{1,0:T(8,128)(2,1)} async-done(((bf16[256,2048]{1,0:T(8,128)(2,1)}), bf16[2048,2048]{1,0:T(8,128)(2,1)}) %all-gather.17.cloned.1.call-update) | async-done | bytes 8388624 | tf_op jit(solution)/shard_map/all_gather | solution.py:215
  74.2 49.2 %all-gather.11.cloned.1.call-done = bf16[2048,2048]{1,0:T(8,128)(2,1)} async-done(((bf16[256,2048]{1,0:T(8,128)(2,1)}), bf16[2048,2048]{1,0:T(8,128)(2,1)}) %all-gather.11.cloned.1.call-update) | async-done | bytes 8388624 | tf_op jit(solution)/shard_map/all_gather | solution.py:216
  160.5 75.8 %all-to-all-done.1 = bf16[4,128,2048]{2,1,0:T(8,128)(2,1)} async-done(((bf16[4,128,2048]{2,1,0:T(8,128)(2,1)}), bf16[4,128,2048]{2,1,0:T(8,128)(2,1)}, u32[]{:S(2)}, u32[]{:S(2)}) %all-to-all-start.1) | async-done | bytes 2097184 | tf_op jit(solution)/shard_map/all_to_all | solution.py:251
  236.3 9.9 fusion.32
  250.3 69.1 %all-gather.19.cloned.1.call-done = bf16[2,1024,2048]{2,1,0:T(8,128)(2,1)} async-done(((bf16[2,128,2048]{2,1,0:T(8,128)(2,1)}), bf16[2,1024,2048]{2,1,0:T(8,128)(2,1)}) %all-gather.19.cloned.1.call-update) | async-done | bytes 8388624 | tf_op jit(solution)/shard_map/all_gather | solution.py:232
  319.4 14.7 reshape_reshape.5
  334.1 13.7 copy.112
  347.9 97.3 %all-gather.13.cloned.1.call-done = bf16[2,1024,2048]{2,1,0:T(8,128)(2,1)} async-done(((bf16[2,128,2048]{2,1,0:T(8,128)(2,1)}), bf16[2,1024,2048]{2,1,0:T(8,128)(2,1)}) %all-gather.13.cloned.1.call-update) | async-done | bytes 8388624 | tf_op jit(solution)/shard_map/all_gather | solution.py:235
  445.1 14.7 reshape_reshape.4
  459.9 13.8 copy.111
  475.1 99.2 %while.28 = (s32[]{:T(128)}, bf16[4,512,512]{1,2,0:T(8,128)(2,1)}, f32[4,512,4]{1,2,0:T(4,128)}, bf16[4,2048,512]{1,2,0:T(8,128)(2,1)}, bf16[4,512,512]{1,2,0:T(...) while((s32[]{:T(128)}, bf16[4,512,512]{1,2,0:T(8,128)(2,1)}, ...), condition=%wide.region_10.12_spmd.clone, body=%wide.region_7.11_spmd.clone.sunk | while | flops 2202269696 | bytes 70334592 | solution.py:113
  574.4 9.9 fusion.38
  589.1 12.5 all-gather.1
  603.0 15.9 all_gather.45
  637.0 15.1 all_gather.53
  667.6 9.0 multiply_reduce_fusion.6
  707.1 54.4 %all_to_all.46 = bf16[4,128,2048]{2,1,0:T(8,128)(2,1)} all-to-all(bf16[4,128,2048]{2,1,0:T(8,128)(2,1)S(1)} %get-tuple-element.338), channel_id=1, replica_groups=mesh['dp'=4,'expert'=4,'seq'=2] {'expert'}, dimensions={0} | all-to-all | bytes 4194304 | tf_op jit(solution)/shard_map/all_to_all | solution.py:288
  761.6 53.1 %all_to_all.47 = bf16[4,128,2048]{2,1,0:T(8,128)(2,1)} all-to-all(bf16[4,128,2048]{2,1,0:T(8,128)(2,1)} %get-tuple-element.337), channel_id=1, replica_groups=mesh['dp'=4,'expert'=4,'seq'=2] {'expert'}, dimensions={0} | all-to-all | bytes 4194304 | tf_op jit(solution)/shard_map/all_to_all | solution.py:289
  814.7 34.6 %all-gather.23.cloned.1.call-done = bf16[32,128,2048]{2,1,0:T(8,128)(2,1)} async-done(((bf16[4,128,2048]{2,1,0:T(8,128)(2,1)}), bf16[32,128,2048]{2,1,0:T(8,128)(2,1)}) %all-gather.23.cloned.1.call-update) | async-done | bytes 16777232 | tf_op jit(solution)/shard_map/all_gather | solution.py:291
  849.3 20.1 fusion.48
  869.4 14.8 fusion.52
  884.3 56.8 %all-gather.25.cloned.1.call-done = bf16[32,128,2048]{2,1,0:T(8,128)(2,1)} async-done(((bf16[4,128,2048]{2,1,0:T(8,128)(2,1)}), bf16[32,128,2048]{2,1,0:T(8,128)(2,1)}) %all-gather.25.cloned.1.call-update) | async-done | bytes 16777232 | tf_op jit(solution)/shard_map/all_gather | solution.py:292
  941.1 35.0 %multiply_convert_fusion.1 = (bf16[4096,704]{0,1:T(8,128)(2,1)}, bf16[4096,704]{0,1:T(8,128)(2,1)}, bf16[4096,704]{0,1:T(8,128)(2,1)}) fusion(f32[4096,704]{0,1:T(8,128)} %fusion.52, f32[4096,704]{0,1:T(8,128)} %fusion.48, bf16[4096,2048]{1,0:T(8,128)(2,1)} %bitcast.420, bf16[1,704,2048]{2,1,0:T(8,128)(2,1)S(1)} %copy-done), kind=kOutput, calls=%fused_computation.56 | convolution fusion | flops 11854413824 | bytes 60030976 | tf_op jit(solution)/shard_map/dot_general | solution.py:302
  976.1 18.8 convolution_convert_fusion
  996.7 24.5 %fusion.50 = f32[4096,2048]{1,0:T(8,128)} fusion(bf16[4096,704]{0,1:T(8,128)(2,1)} %get-tuple-element.327, bf16[1,2048,704]{1,2,0:T(8,128)(2,1)S(1)} %copy-done.92), kind=kOutput, calls=%fused_computation.96 | convolution fusion | flops 11811160064 | bytes 42205184 | tf_op jit(solution)/shard_map/dot_general | solution.py:307
  1021.2 26.5 %add_convert_fusion = bf16[4096,2048]{1,0:T(8,128)(2,1)} fusion(f32[4096,2048]{1,0:T(8,128)} %fusion.50, bf16[4096,704]{0,1:T(8,128)(2,1)} %get-tuple-element.326, bf16[1,2048,704]{1,2,0:T(8,128)(2,1)} %param.37), kind=kOutput, calls=%fused_computation.52 | convolution fusion | flops 11827937280 | bytes 58982400 | tf_op jit(solution)/shard_map/dot_general | solution.py:307
  1047.8 63.2 %reduce-scatter.15.cloned.1.call-done = bf16[4,128,2048]{2,1,0:T(8,128)(2,1)} async-done(((bf16[32,128,2048]{2,1,0:T(8,128)(2,1)}), bf16[4,128,2048]{2,1,0:T(8,128)(2,1)}) %reduce-scatter.15.cloned.1.call-update) | async-done | bytes 2097168 | tf_op jit(solution)/shard_map/reduce_scatter | solution.py:310
  1115.7 114.8 %reduce-scatter.17.cloned.1.call-done = bf16[4,128,2048]{2,1,0:T(8,128)(2,1)} async-done(((bf16[32,128,2048]{2,1,0:T(8,128)(2,1)}), bf16[4,128,2048]{2,1,0:T(8,128)(2,1)}) %reduce-scatter.17.cloned.1.call-update) | async-done | bytes 2097168 | tf_op jit(solution)/shard_map/reduce_scatter | solution.py:316
  1253.3 10.9 multiply_reduce_fusion.3
  1264.6 20.2 all-to-all-done.6
  1293.9 9.0 multiply_reduce_fusion.4
  1330.6 47.6 %all-to-all-done.7 = bf16[4,128,2048]{2,1,0:T(8,128)(2,1)S(1)} async-done(((bf16[4,128,2048]{2,1,0:T(8,128)(2,1)}), bf16[4,128,2048]{2,1,0:T(8,128)(2,1)S(1)}, u32[]{:S(2)}, u32[]{:S(2)}) %all-to-all-start.7) | async-done | bytes 2097184 | tf_op jit(solution)/shard_map/all_to_all | solution.py:377
  1378.2 9.9 fusion.41
  1393.6 228.9 %while.29 = (s32[]{:T(128)}, bf16[4,512,512]{1,2,0:T(8,128)(2,1)}, bf16[4,2048,512]{1,2,0:T(8,128)(2,1)}, bf16[4,2048,512]{1,2,0:T(8,128)(2,1)}, bf16[4,2048,512...) while((s32[]{:T(128)}, bf16[4,512,512]{1,2,0:T(8,128)(2,1)}, ...), condition=%wide.region_28.30_spmd.clone, body=%wide.region_26.29_spmd.clone.sunk | while | flops 5438437376 | bytes 163125424 | solution.py:163
  1418.5 12.8 multiply_reduce_fusion.13
  1431.2 12.1 multiply_convert_fusion.8
  1475.5 12.8 multiply_reduce_fusion.13
  1488.3 12.1 multiply_convert_fusion.8
  1523.8 8.8 fusion.213
  1532.6 12.8 multiply_reduce_fusion.13
  1545.3 12.1 multiply_convert_fusion.8
  1580.9 8.8 fusion.213
  1589.7 12.8 multiply_reduce_fusion.13
  1602.4 12.1 multiply_convert_fusion.8
  1622.4 14.4 convert_element_type.298
  1636.9 21.2 copy.126
  1658.1 14.6 convert_element_type.294
  1672.7 21.3 copy.125
  1704.0 10.2 convert_bitcast_fusion.1
  1724.3 81.1 %reduce-scatter.21.cloned.1.call-done = bf16[2,128,2048]{2,1,0:T(8,128)(2,1)} async-done(((bf16[2,1024,2048]{2,1,0:T(8,128)(2,1)}), bf16[2,128,2048]{2,1,0:T(8,128)(2,1)}) %reduce-scatter.21.cloned.1.call-update) | async-done | bytes 1048592 | tf_op jit(solution)/shard_map/reduce_scatter | solution.py:413
  1814.3 143.1 %reduce-scatter.19.cloned.1.call-done = bf16[2,128,2048]{2,1,0:T(8,128)(2,1)} async-done(((bf16[2,1024,2048]{2,1,0:T(8,128)(2,1)}), bf16[2,128,2048]{2,1,0:T(8,128)(2,1)}) %reduce-scatter.19.cloned.1.call-update) | async-done | bytes 1048592 | tf_op jit(solution)/shard_map/reduce_scatter | solution.py:407
  1964.4 19.2 convolution_bitcast_fusion.2
  1983.6 19.0 convolution_bitcast_fusion
  2012.2 19.2 convolution_bitcast_fusion.1
  2034.7 25.8 %all-to-all-done.8 = bf16[4,128,2048]{2,1,0:T(8,128)(2,1)S(1)} async-done(((bf16[4,128,2048]{2,1,0:T(8,128)(2,1)}), bf16[4,128,2048]{2,1,0:T(8,128)(2,1)S(1)}, u32[]{:S(2)}, u32[]{:S(2)}) %all-to-all-start.8) | async-done | bytes 2097184 | tf_op jit(solution)/shard_map/all_to_all | solution.py:399
  2069.9 10.1 multiply_reduce_fusion.2
  2080.0 26.8 %reduce-scatter.27.cloned.1.call-done = bf16[1,256,2048]{2,1,0:T(8,128)(2,1)} async-done(((bf16[1,2048,2048]{2,1,0:T(8,128)(2,1)}), bf16[1,256,2048]{2,1,0:T(8,128)(2,1)}) %reduce-scatter.27.cloned.1.call-update) | async-done | bytes 1048592 | tf_op jit(solution)/shard_map/reduce_scatter | solution.py:459
  2109.6 72.2 %reduce-scatter.29.cloned.1.call-done = bf16[1,256,2048]{2,1,0:T(8,128)(2,1)} async-done(((bf16[1,2048,2048]{2,1,0:T(8,128)(2,1)}), bf16[1,256,2048]{2,1,0:T(8,128)(2,1)}) %reduce-scatter.29.cloned.1.call-update) | async-done | bytes 1048592 | tf_op jit(solution)/shard_map/reduce_scatter | solution.py:462
  2184.6 71.8 %reduce-scatter.25.cloned.1.call-done = bf16[256,2048]{1,0:T(8,128)(2,1)} async-done(((bf16[2048,2048]{1,0:T(8,128)(2,1)}), bf16[256,2048]{1,0:T(8,128)(2,1)}) %reduce-scatter.25.cloned.1.call-update) | async-done | bytes 1048592 | tf_op jit(solution)/shard_map/reduce_scatter | solution.py:450
  2256.4 75.0 %reduce-scatter.23.cloned.1.call-done = bf16[256,2048]{1,0:T(8,128)(2,1)} async-done(((bf16[2048,2048]{1,0:T(8,128)(2,1)}), bf16[256,2048]{1,0:T(8,128)(2,1)}) %reduce-scatter.23.cloned.1.call-update) | async-done | bytes 1048592 | tf_op jit(solution)/shard_map/reduce_scatter | solution.py:447
  2346.9 14.4 all-reduce.2
  2361.5 12.9 all-reduce.3
  2380.5 40.8 %all-reduce.7.cloned.1.call-done = (bf16[256,2048]{1,0:T(8,128)(2,1)}, bf16[256,2048]{1,0:T(8,128)(2,1)}) async-done(((bf16[256,2048]{1,0:T(8,128)(2,1)}, bf16[256,2048]{1,0:T(8,128)(2,1)}), (bf16[256,2048]{1,0:T(8,128)(2,1)}, bf16[256,2048]{1,0:T(8,128)(2,1)})) %all-reduce.7.cloned.1.call-update) | async-done | bytes 2097168 | tf_op jit(solution)/shard_map/psum | solution.py:469
  (476 shorter events, 498.2 us)
Async XLA Ops:
  7.2 933.9 %copy-start = (bf16[1,704,2048]{2,1,0:T(8,128)(2,1)S(1)}, bf16[1,704,2048]{2,1,0:T(8,128)(2,1)}, u32[]{:S(2)}) copy-start(bf16[1,704,2048]{2,1,0:T(8,128)(2,1)} %param.38) | copy-start | bytes 8650756
  7.2 59.8 %all-gather.17.cloned.1.call-start = ((), (), s32[]{:S(2)}) async-start(), calls=%async_computation.22 | async-start | bytes 9437184 | tf_op jit(solution)/shard_map/all_gather | solution.py:215
  7.9 115.4 %all-gather.11.cloned.1.call-start = ((), (), s32[]{:S(2)}) async-start(), calls=%async_computation.19 | async-start | bytes 9437184 | tf_op jit(solution)/shard_map/all_gather | solution.py:216
  8.7 227.6 %all-gather.15.cloned.1.call-start = ((), (), s32[]{:S(2)}) async-start(), calls=%async_computation.21 | async-start | bytes 9437184 | tf_op jit(solution)/shard_map/all_gather | solution.py:217
  9.4 310.0 %all-gather.19.cloned.1.call-start = ((), (), s32[]{:S(2)}) async-start(), calls=%async_computation.23 | async-start | bytes 9437184 | tf_op jit(solution)/shard_map/all_gather | solution.py:232
  74.1 56.3 %copy-start.89 = (s32[2]{0:T(128)S(1)}, s32[2]{0:T(128)}, u32[]{:S(2)}) copy-start(s32[2]{0:T(128)} %param.24) | copy-start | bytes 28
  74.1 57.2 %copy-start.88 = (s32[1,1,256]{2,1,0:T(1,128)S(1)}, s32[1,1,256]{2,1,0:T(1,128)}, u32[]{:S(2)}) copy-start(s32[1,1,256]{2,1,0:T(1,128)} %param.27) | copy-start | bytes 3076
  74.1 57.5 %copy-start.64 = (s32[2,128,2]{1,2,0:T(2,128)S(1)}, s32[2,128,2]{1,2,0:T(2,128)}, u32[]{:S(2)}) copy-start(s32[2,128,2]{1,2,0:T(2,128)} %param.25) | copy-start | bytes 6148
  74.1 57.8 %copy-start.61 = (s32[2,128,2]{1,2,0:T(2,128)S(1)}, s32[2,128,2]{1,2,0:T(2,128)}, u32[]{:S(2)}) copy-start(s32[2,128,2]{1,2,0:T(2,128)} %param.26) | copy-start | bytes 6148
  74.1 371.0 %all-gather.13.cloned.1.call-start = ((), (), s32[]{:S(2)}) async-start(), calls=%async_computation.20 | async-start | bytes 9437184 | tf_op jit(solution)/shard_map/all_gather | solution.py:235
  140.4 14.3 all-to-all-start
  154.7 81.6 %all-to-all-start.1 = ((bf16[4,128,2048]{2,1,0:T(8,128)(2,1)}), bf16[4,128,2048]{2,1,0:T(8,128)(2,1)}, u32[]{:S(2)}, u32[]{:S(2)}) async-start(bf16[4,128,2048]{2,1,0:T(8,128)(2,1)} %broadcast_select_fusion.3), calls=%async_computation.1 | async-start | bytes 4194304 | tf_op jit(solution)/shard_map/all_to_all | solution.py:251
  159.8 414.6 %all-gather.21.cloned.1.call-start = ((), (), s32[]{:S(2)}) async-start(), calls=%async_computation.24 | async-start | bytes 9437184 | tf_op jit(solution)/shard_map/all_gather | solution.py:218
  584.4 18.2 copy-start.85
  584.4 18.4 copy-start.84
  584.4 18.6 copy-start.86
  584.4 70.2 %all-to-all-start.2 = ((bf16[4,128,2048]{2,1,0:T(8,128)(2,1)}), bf16[4,128,2048]{2,1,0:T(8,128)(2,1)}, u32[]{:S(2)}, u32[]{:S(2)}) async-start(bf16[4,128,2048]{2,1,0:T(8,128)(2,1)} %bitcast.390), calls=%async_computation.2 | async-start | bytes 4194304 | tf_op jit(solution)/shard_map/all_to_all | solution.py:259
  589.0 260.3 %all-gather.23.cloned.1.call-start = ((), (), s32[]{:S(2)}) async-start(), calls=%async_computation.25 | async-start | bytes 18874368 | tf_op jit(solution)/shard_map/all_gather | solution.py:291
  601.6 75.4 %copy-start.51 = (f32[8,1,256]{2,1,0:T(1,128)}, f32[8,1,256]{2,1,0:T(1,128)S(1)}, u32[]{:S(2)}) copy-start(f32[8,1,256]{2,1,0:T(1,128)S(1)} %convert_element_type.325) | copy-start | bytes 24580
  602.8 81.8 %copy-start.35 = (pred[256,2]{1,0:T(8,128)(4,1)}, pred[256,2]{1,0:T(8,128)(4,1)S(1)}, u32[]{:S(2)}) copy-start(pred[256,2]{1,0:T(8,128)(4,1)S(1)} %lt.154) | copy-start | bytes 1540
  603.0 50.8 %copy-start.32 = (pred[256,2]{1,0:T(8,128)(4,1)}, pred[256,2]{1,0:T(8,128)(4,1)S(1)}, u32[]{:S(2)}) copy-start(pred[256,2]{1,0:T(8,128)(4,1)S(1)} %lt.148) | copy-start | bytes 1540
  630.9 21.2 copy-start.68
  630.9 21.2 copy-start.70
  630.9 21.8 copy-start.39
  630.9 21.8 copy-start.72
  630.9 22.9 copy-start.58
  652.1 25.2 %copy-start.49 = (bf16[2048,4]{0,1:T(4,128)(2,1)}, bf16[2048,4]{0,1:T(4,128)(2,1)S(1)}, u32[]{:S(2)}) copy-start(bf16[2048,4]{0,1:T(4,128)(2,1)S(1)} %all_gather.53) | copy-start | bytes 49156
  761.5 179.6 %all-gather.25.cloned.1.call-start = ((), (), s32[]{:S(2)}) async-start(), calls=%async_computation.27 | async-start | bytes 18874368 | tf_op jit(solution)/shard_map/all_gather | solution.py:292
  814.7 296.4 %reduce-scatter.15.cloned.1.call-start = ((), (), s32[]{:S(2)}) async-start(), calls=%async_computation.26 | async-start | bytes 18874368 | tf_op jit(solution)/shard_map/reduce_scatter | solution.py:310
  849.3 20.1 copy-start.90
  849.3 20.1 copy-start.91
  994.9 235.5 %reduce-scatter.17.cloned.1.call-start = ((), (), s32[]{:S(2)}) async-start(), calls=%async_computation.28 | async-start | bytes 18874368 | tf_op jit(solution)/shard_map/reduce_scatter | solution.py:316
  1111.0 119.4 %all-to-all-start.4 = ((bf16[4,128,2048]{2,1,0:T(8,128)(2,1)}), bf16[4,128,2048]{2,1,0:T(8,128)(2,1)S(1)}, u32[]{:S(2)}, u32[]{:S(2)}) async-start(bf16[4,128,2048]{2,1,0:T(8,128)(2,1)} %reduce-scatter.15.cloned.1.call-done), calls=%async_computation.5 | async-start | bytes 4194304 | tf_op jit(solution)/shard_map/all_to_all | solution.py:322
  1115.6 120.9 %copy-start.24 = (f32[256,2]{1,0:T(8,128)S(1)}, f32[256,2]{1,0:T(8,128)}, u32[]{:S(2)}) copy-start(f32[256,2]{1,0:T(8,128)} %copy-done.23) | copy-start | bytes 6148
  1115.7 123.9 %copy-start.63 = (s32[2,128,2]{1,2,0:T(2,128)S(1)}, s32[2,128,2]{1,2,0:T(2,128)}, u32[]{:S(2)}) copy-start(s32[2,128,2]{1,2,0:T(2,128)} %param.26) | copy-start | bytes 6148
  1115.7 124.2 %copy-start.83 = (s32[512]{0:T(512)S(1)}, s32[512]{0:T(512)}, u32[]{:S(2)}) copy-start(s32[512]{0:T(512)} %get-tuple-element.345) | copy-start | bytes 6148
  1115.7 124.2 %copy-start.82 = (s32[512]{0:T(512)S(1)}, s32[512]{0:T(512)}, u32[]{:S(2)}) copy-start(s32[512]{0:T(512)} %get-tuple-element.329) | copy-start | bytes 6148
  1115.7 124.3 %copy-start.33 = (pred[256,2]{1,0:T(8,128)(4,1)S(1)}, pred[256,2]{1,0:T(8,128)(4,1)}, u32[]{:S(2)}) copy-start(pred[256,2]{1,0:T(8,128)(4,1)} %copy-done.32) | copy-start | bytes 1540
  1115.7 124.3 %copy-start.36 = (pred[256,2]{1,0:T(8,128)(4,1)S(1)}, pred[256,2]{1,0:T(8,128)(4,1)}, u32[]{:S(2)}) copy-start(pred[256,2]{1,0:T(8,128)(4,1)} %copy-done.35) | copy-start | bytes 1540
  1115.7 124.3 %copy-start.59 = (pred[256]{0:T(512)(128)(4,1)S(1)}, pred[256]{0:T(512)(128)(4,1)}, u32[]{:S(2)}) copy-start(pred[256]{0:T(512)(128)(4,1)} %copy-done.57) | copy-start | bytes 772
  1231.8 52.9 %all-to-all-start.6 = ((bf16[4,128,2048]{2,1,0:T(8,128)(2,1)}), bf16[4,128,2048]{2,1,0:T(8,128)(2,1)S(1)}, u32[]{:S(2)}, u32[]{:S(2)}) async-start(bf16[4,128,2048]{2,1,0:T(8,128)(2,1)} %reduce-scatter.17.cloned.1.call-done), calls=%async_computation.8 | async-start | bytes 4194304 | tf_op jit(solution)/shard_map/all_to_all | solution.py:323
  1264.5 38.4 %copy-start.55 = (f32[256,4]{0,1:T(4,128)}, f32[256,4]{0,1:T(4,128)S(1)}, u32[]{:S(2)}) copy-start(f32[256,4]{0,1:T(4,128)S(1)} %select_reduce_fusion.1) | copy-start | bytes 12292
  1326.9 51.3 %all-to-all-start.7 = ((bf16[4,128,2048]{2,1,0:T(8,128)(2,1)}), bf16[4,128,2048]{2,1,0:T(8,128)(2,1)S(1)}, u32[]{:S(2)}, u32[]{:S(2)}) async-start(bf16[4,128,2048]{2,1,0:T(8,128)(2,1)} %broadcast_select_fusion.2), calls=%async_computation.9 | async-start | bytes 4194304 | tf_op jit(solution)/shard_map/all_to_all | solution.py:377
  1330.5 474.9 %reduce-scatter.21.cloned.1.call-start = ((), (), s32[]{:S(2)}) async-start(), calls=%async_computation.30 | async-start | bytes 9437184 | tf_op jit(solution)/shard_map/reduce_scatter | solution.py:413
  1658.1 299.3 %reduce-scatter.19.cloned.1.call-start = ((), (), s32[]{:S(2)}) async-start(), calls=%async_computation.29 | async-start | bytes 9437184 | tf_op jit(solution)/shard_map/reduce_scatter | solution.py:407
  1694.0 338.9 %reduce-scatter.33.cloned.1.call-start = ((), (), s32[]{:S(2)}) async-start(), calls=%async_computation.36 | async-start | bytes 589824
  1702.3 331.5 %reduce-scatter.31.cloned.1.call-start = ((), (), s32[]{:S(2)}) async-start(), calls=%async_computation.35 | async-start | bytes 589824
  1704.0 402.8 %reduce-scatter.27.cloned.1.call-start = ((), (), s32[]{:S(2)}) async-start(), calls=%async_computation.33 | async-start | bytes 9437184 | tf_op jit(solution)/shard_map/reduce_scatter | solution.py:459
  1714.2 467.6 %reduce-scatter.29.cloned.1.call-start = ((), (), s32[]{:S(2)}) async-start(), calls=%async_computation.34 | async-start | bytes 9437184 | tf_op jit(solution)/shard_map/reduce_scatter | solution.py:462
  1724.0 81.4 %copy-start.8 = (bf16[2,128,2048]{2,1,0:T(8,128)(2,1)S(1)}, bf16[2,128,2048]{2,1,0:T(8,128)(2,1)}, u32[]{:S(2)}) copy-start(bf16[2,128,2048]{2,1,0:T(8,128)(2,1)} %param.23) | copy-start | bytes 3145732
  1724.1 81.4 %copy-start.38 = (f32[8,1,256]{2,1,0:T(1,128)S(1)}, f32[8,1,256]{2,1,0:T(1,128)}, u32[]{:S(2)}) copy-start(f32[8,1,256]{2,1,0:T(1,128)} %copy-done.37) | copy-start | bytes 24580
  1724.1 81.4 %copy-start.71 = (f32[2,128]{1,0:T(2,128)S(1)}, f32[2,128]{1,0:T(2,128)}, u32[]{:S(2)}) copy-start(f32[2,128]{1,0:T(2,128)} %get-tuple-element.333) | copy-start | bytes 3076
  1724.1 532.3 %reduce-scatter.25.cloned.1.call-start = ((), (), s32[]{:S(2)}) async-start(), calls=%async_computation.32 | async-start | bytes 9437184 | tf_op jit(solution)/shard_map/reduce_scatter | solution.py:450
  1812.4 518.9 %reduce-scatter.23.cloned.1.call-start = ((), (), s32[]{:S(2)}) async-start(), calls=%async_computation.31 | async-start | bytes 9437184 | tf_op jit(solution)/shard_map/reduce_scatter | solution.py:447
  1964.4 38.2 %slice-start = ((s8[8388608]{0:T(1024)(128)(4,1)}), s8[4194304]{0:T(1024)(128)(4,1)S(1)}, s32[]{:S(2)}) async-start(s8[8388608]{0:T(1024)(128)(4,1)} %bitcast.422), calls=%async_computation.38 | async-start | bytes 8388608
  1983.6 19.0 copy-start.18
  1983.6 19.0 slice-start.1
  2008.5 52.1 %all-to-all-start.8 = ((bf16[4,128,2048]{2,1,0:T(8,128)(2,1)}), bf16[4,128,2048]{2,1,0:T(8,128)(2,1)S(1)}, u32[]{:S(2)}, u32[]{:S(2)}) async-start(bf16[4,128,2048]{2,1,0:T(8,128)(2,1)} %bitcast.391), calls=%async_computation.10 | async-start | bytes 4194304 | tf_op jit(solution)/shard_map/all_to_all | solution.py:399
  2012.1 409.3 %all-reduce.7.cloned.1.call-start = ((), (), s32[]{:S(2)}) async-start(), calls=%async_computation.37 | async-start | bytes 4194304 | tf_op jit(solution)/shard_map/psum | solution.py:469
  2012.1 19.2 copy-start.9
  2012.1 19.2 copy-start.13
  2012.2 19.2 copy-start.16
  2031.4 29.2 %copy-start.74 = (s32[1024]{0:T(1024)S(1)}, s32[1024]{0:T(1024)}, u32[]{:S(2)}) copy-start(s32[1024]{0:T(1024)} %copy-done.73) | copy-start | bytes 12292
  2109.6 221.9 %copy-start.28 = (bf16[2,128,2048]{2,1,0:T(8,128)(2,1)S(1)}, bf16[2,128,2048]{2,1,0:T(8,128)(2,1)}, u32[]{:S(2)}) copy-start(bf16[2,128,2048]{2,1,0:T(8,128)(2,1)} %reduce-scatter.21.cloned.1.call-done) | copy-start | bytes 3145732
  (60 other events, 352.9 us)
Sparse Core Ops, SparseCore 0:
  9.9 57.0 all-gather.16
  68.9 54.3 all-gather.10
  125.2 54.3 all-gather.14
  182.3 137.0 all-gather.18
  322.0 123.0 all-gather.12
  446.9 52.5 all-gather.20
  761.6 87.6 all-gather.22
  851.2 89.8 all-gather.24
  995.0 115.9 reduce-scatter.14
  1114.5 115.9 reduce-scatter.16
  1658.2 147.1 reduce-scatter.20
  1809.3 148.0 reduce-scatter.18
  1961.0 33.0 reduce-scatter.32
  1998.0 34.0 reduce-scatter.30
  2035.4 71.2 reduce-scatter.26
  2110.5 71.2 reduce-scatter.28
  2185.1 71.2 reduce-scatter.24
  2260.1 71.2 reduce-scatter.22
  2333.8 87.4 all-reduce.6
where the time goes:
time: 2450 us; the launch traced here: 2430 us
  waiting for transfers between devices  1210 us (49%)
  matrix products  481 us (20%)
  local copies, waits for them, and re-layouts  327 us (13%)
  blocking collectives  192 us (8%)
  other arithmetic  177 us (7%)
  starting transfers between devices  32.3 us (1%)
    reduce_scatter x1, waiting for transfers between devices, body(): lax.psum_scatter(key_grad.reshape(seq_count, seq_len, -1).astype(jnp.bflo...  143 us
    reduce_scatter x1, waiting for transfers between devices, body(): lax.psum_scatter(partial_in.reshape(everyone, count, width).astype(jnp.bf...  115 us
    all_gather x1, waiting for transfers between devices, body(): lax.all_gather(values_here.reshape(seq_count, stretch, -1), ('expert', 's...  97.3 us
    reduce_scatter x1, waiting for transfers between devices, body(): lax.psum_scatter(value_grad.reshape(seq_count, seq_len, -1).astype(jnp.bf...  81.1 us
    all_to_all x1, waiting for transfers between devices, body(): lax.all_to_all(attn_send, 'expert', split_axis=0, concat_axis=0, tiled=True)  75.8 us
    reduce_scatter x1, waiting for transfers between devices, body(): lax.psum_scatter(grad_key.astype(jnp.bfloat16), ('dp', 'seq'), scatter_di...  75 us
    reduce_scatter x1, waiting for transfers between devices, body(): lax.psum_scatter(grad_out_w[None].astype(jnp.bfloat16), ('dp', 'seq'), sc...  72.2 us
    reduce_scatter x1, waiting for transfers between devices, body(): lax.psum_scatter(grad_value.astype(jnp.bfloat16), ('dp', 'seq'), scatter_...  71.8 us
  transfers between devices with their start and end apart: 26, of which 19 were waited for; matrix products, arithmetic and copies ran while one was open for 22% of the time, Pallas kernels for 0%

commit v1 on v0

v1 whole, which is shorter than its diff:
```python
import functools

import jax
import jax.numpy as jnp
from jax import lax
from jax.experimental import pallas as pl
from jax.experimental.pallas import tpu as pltpu
from jax.sharding import PartitionSpec as P

HEAD = 128
EPS = 1e-06
NEG = -1e30
HIGH = lax.Precision.HIGHEST
BF = jnp.bfloat16
F32 = jnp.float32
LOG2E = 1.4426950408889634


def dot(left, right):
    return jnp.dot(left, right, preferred_element_type=F32)


def dot_t(left, right):
    return lax.dot_general(left, right, (((1,), (1,)), ((), ())), preferred_element_type=F32)


def t_dot(left, right):
    return lax.dot_general(left, right, (((0,), (0,)), ((), ())), preferred_element_type=F32)


def ring(count, shift):
    return [(j, (j + shift) % count) for j in range(count)]


def flip(count, bit):
    return [(j, j ^ bit) for j in range(count)]


def swap_x(value):
    return lax.ppermute(value, "seq", flip(2, 1))


def swap_core(value):
    return lax.ppermute(value, "dp", flip(lax.axis_size("dp"), 1))


def swap_y(value):
    return lax.ppermute(value, "dp", flip(4, 2))


def z_rounds(pieces, sign):
    count = lax.axis_size("expert")
    return [pieces[0]] + [
        lax.ppermute(pieces[r], "expert", ring(count, sign * r)) for r in range(1, count)
    ]


def is_small():
    return lax.axis_size("dp") == 4 and lax.axis_size("expert") == 4


def add_low(*terms):
    total = terms[0].astype(F32)
    for term in terms[1:]:
        total = total + term.astype(F32)
    return total.astype(terms[0].dtype)


def square_gather(piece):
    if not is_small():
        every = lax.all_gather(piece, ("dp", "seq"), axis=0, tiled=False)
        return [every[j] for j in range(every.shape[0])]
    half = piece.shape[0] // 2
    along_x = swap_x(piece)
    along_y = swap_y(piece)
    corner = jnp.concatenate([swap_y(along_x[:half]), swap_x(along_y[half:])], axis=0)
    own = [piece, along_x, along_y, corner]
    return own + [swap_core(part) for part in own]


def square_scatter(parts):
    if not is_small():
        return lax.psum_scatter(
            jnp.stack(parts), ("dp", "seq"), scatter_dimension=0, tiled=False
        )
    half = parts[0].shape[0] // 2
    corner = add_low(parts[3], swap_core(parts[7]))
    for_x = add_low(parts[1], swap_core(parts[5]))
    for_y = add_low(parts[2], swap_core(parts[6]))
    own = add_low(parts[0], swap_core(parts[4]))
    via_x = swap_x(corner[:half])
    via_y = swap_y(corner[half:])
    from_x = [swap_x(for_x[:half]), swap_x(add_low(for_x[half:], via_y))]
    from_y = [swap_y(for_y[half:]), swap_y(add_low(for_y[:half], via_x))]
    low = add_low(own[:half], from_x[0], from_y[1])
    high = add_low(own[half:], from_x[1], from_y[0])
    return jnp.concatenate([low, high], axis=0)


def group_gather(block):
    count = lax.axis_size("expert")
    if is_small():
        half = block.shape[0] // 2
        up = lax.ppermute(block, "expert", ring(count, -1))
        down = lax.ppermute(block, "expert", ring(count, 1))
        far = jnp.concatenate(
            [
                lax.ppermute(down[:half], "expert", ring(count, 1)),
                lax.ppermute(up[half:], "expert", ring(count, -1)),
            ],
            axis=0,
        )
        own = [block, up, far, down]
        return own + [swap_x(part) for part in own]
    e_at, s_at = lax.axis_index("expert"), lax.axis_index("seq")
    every = lax.all_gather(block, ("expert", "seq"), axis=0, tiled=False)
    wanted = [
        (lax.rem(e_at + r, count)) * 2 + lax.rem(s_at + sp, 2)
        for sp in range(2)
        for r in range(count)
    ]
    return [lax.dynamic_index_in_dim(every, at, 0, keepdims=False) for at in wanted]


def group_scatter(parts):
    count = lax.axis_size("expert")
    if not is_small():
        e_at, s_at = lax.axis_index("expert"), lax.axis_index("seq")
        stacked = jnp.stack(parts)
        spots = [
            (lax.rem(s_at + b % 2, 2)) * count + lax.rem(b // 2 - e_at + count, count)
            for b in range(2 * count)
        ]
        ordered = jnp.stack(
            [lax.dynamic_index_in_dim(stacked, at, 0, keepdims=False) for at in spots]
        )
        return lax.psum_scatter(ordered, ("expert", "seq"), scatter_dimension=0, tiled=False)
    half = parts[0].shape[0] // 2
    far = add_low(parts[2], swap_x(parts[6]))
    up = add_low(parts[1], swap_x(parts[5]))
    down = add_low(parts[3], swap_x(parts[7]))
    own = add_low(parts[0], swap_x(parts[4]))
    far_up = lax.ppermute(far[:half], "expert", ring(count, 1))
    far_down = lax.ppermute(far[half:], "expert", ring(count, -1))
    up_low = lax.ppermute(add_low(up[:half], far_up), "expert", ring(count, 1))
    up_high = lax.ppermute(up[half:], "expert", ring(count, 1))
    down_high = lax.ppermute(add_low(down[half:], far_down), "expert", ring(count, -1))
    down_low = lax.ppermute(down[:half], "expert", ring(count, -1))
    return jnp.concatenate(
        [add_low(own[:half], up_low, down_low), add_low(own[half:], up_high, down_high)], axis=0
    )


def dp_gather(piece):
    if not is_small():
        return lax.all_gather(piece, "dp", axis=0, tiled=True)
    at = lax.axis_index("dp")
    core, row = at % 2, at // 2
    along_y = swap_y(piece)
    beside, across = swap_core(piece), swap_core(along_y)
    here = jnp.where(
        core == 0,
        jnp.concatenate([piece, beside], axis=0),
        jnp.concatenate([beside, piece], axis=0),
    )
    there = jnp.where(
        core == 0,
        jnp.concatenate([along_y, across], axis=0),
        jnp.concatenate([across, along_y], axis=0),
    )
    return jnp.where(
        row == 0,
        jnp.concatenate([here, there], axis=0),
        jnp.concatenate([there, here], axis=0),
    )


def dp_scatter(part_of):
    count = lax.axis_size("dp")
    at = lax.axis_index("dp")
    if count != 4:
        parts = jnp.stack([part_of(jnp.int32(d)) for d in range(count)])
        return lax.psum_scatter(parts, "dp", scatter_dimension=0, tiled=False)
    beside, across = part_of(at ^ 1), part_of(at ^ 3)
    far, own = part_of(at ^ 2), part_of(at)
    far = add_low(far, swap_core(across))
    own = add_low(own, swap_core(beside))
    return add_low(own, swap_y(far))


def route_pairs(routes, order, is_valid, capacity):
    tokens_here, top_count = routes.shape
    pairs = tokens_here * top_count
    target = routes.reshape(pairs)
    second = lax.broadcasted_iota(jnp.int32, routes.shape, 1)
    priority = (order[:, None] * top_count + second).reshape(pairs)
    living = jnp.broadcast_to(is_valid[:, None], routes.shape).reshape(pairs)
    earlier = (
        (target[:, None] == target[None, :])
        & (priority[None, :] < priority[:, None])
        & living[None, :]
    )
    slot_index = jnp.sum(earlier.astype(jnp.int32), axis=1, dtype=jnp.int32)
    kept_pair = living & (slot_index < capacity)
    return (kept_pair.reshape(routes.shape), slot_index.reshape(routes.shape))


def spots(routes, kept, slot_index, experts, capacity):
    away = lax.rem(lax.axis_index("expert") - routes + experts, experts)
    flat = jnp.where(kept, away * capacity + slot_index, -1)
    slots = lax.broadcasted_iota(jnp.int32, (1, experts * capacity), 1)
    return [flat[:, k : k + 1] == slots for k in range(routes.shape[1])]


def weigh(hot, weight):
    return sum(jnp.where(hot[k], weight[:, k : k + 1], 0.0) for k in range(len(hot)))


def in_two(value):
    high = lax.reduce_precision(value, 8, 7)
    return high.astype(BF), (value - high).astype(BF)


def rms_norm(values, gain):
    return values * lax.rsqrt(jnp.mean(values * values, axis=-1, keepdims=True) + EPS) * gain


def norm_back(values, gain, grad):
    factor = lax.rsqrt(jnp.mean(values * values, axis=1, keepdims=True) + EPS)
    unit = values * factor
    gain_grad = jnp.sum(grad * unit, axis=0)
    scaled = grad * gain
    return (factor * (scaled - unit * jnp.mean(scaled * unit, axis=1, keepdims=True)), gain_grad)


def gate_values(normed, router, routes):
    logits = dot(normed, router)
    experts = lax.broadcasted_iota(jnp.int32, logits.shape, 1)
    chosen = jnp.concatenate(
        [
            jnp.sum(jnp.where(routes[:, k : k + 1] == experts, logits, 0.0), axis=1, keepdims=True)
            for k in range(routes.shape[1])
        ],
        axis=1,
    )
    top = jnp.max(chosen, axis=1, keepdims=True)
    expo = jnp.exp(chosen - top)
    return expo / jnp.sum(expo, axis=1, keepdims=True)


def gate_grads(normed, router, routes, gates, gate_grad):
    chosen = gates * (gate_grad - jnp.sum(gates * gate_grad, axis=1, keepdims=True))
    experts = lax.broadcasted_iota(jnp.int32, (1, 1, router.shape[1]), 2)
    logit_grad = jnp.sum(jnp.where(routes[:, :, None] == experts, chosen[:, :, None], 0.0), axis=1)
    router_grad = jnp.dot(normed.astype(F32).T, logit_grad, precision=HIGH)
    input_grad = jnp.dot(logit_grad, router.astype(F32).T, precision=HIGH)
    return (router_grad, input_grad)


def tile_bias(info, tile, blocks, tokens):
    stretch = tokens // 2
    row_seq, row_place = info[:, 0:1], info[:, 1:2]
    rows = info.shape[0]
    col = lax.broadcasted_iota(jnp.int32, (rows, tokens), 1)
    same = (col // stretch) == row_seq
    near = jnp.where(same, 0.0, NEG)
    place = lax.rem(col, stretch)
    diagonal = [
        jnp.where(same & (place + (tile * blocks + j) * stretch <= row_place), 0.0, NEG)
        for j in range(blocks)
    ]
    return jnp.concatenate([near] * (tile * blocks) + diagonal, axis=1)


def picked(ref, index, at, count):
    return jnp.concatenate([ref[index[at + j]] for j in range(count)], axis=0)


def attend_kernel(index, info, query, keys, values, mixed, logs, *, blocks):
    head = pl.program_id(0)
    total, capacity, _ = query.shape
    tokens = keys.shape[1]
    rate = HEAD ** (-0.5) * LOG2E
    lane = lax.broadcasted_iota(jnp.int32, (capacity, logs.shape[2]), 1)
    for tile in range(total // blocks):
        first = tile * blocks
        q = picked(query, index, first, blocks)
        k = picked(keys, index, 0, first + blocks)
        v = picked(values, index, 0, first + blocks)
        bias = tile_bias(picked(info, index, first, blocks), tile, blocks, tokens)
        scores = dot_t(q, k) + bias
        top = jnp.max(scores, axis=1, keepdims=True)
        expo = jnp.exp2((scores - top) * rate)
        norm = jnp.sum(expo, axis=1, keepdims=True)
        out = (dot(expo.astype(BF), v) / norm).astype(BF)
        log = top * rate + jnp.log2(norm)
        for j in range(blocks):
            rows = slice(j * capacity, (j + 1) * capacity)
            mixed[index[first + j]] = out[rows]
            held = logs[index[first + j]]
            logs[index[first + j]] = jnp.where(lane == head, log[rows], held)


def attend_back_kernel(
    index, info, query, keys, values, logs, mixed_grad, q_grad, k_grad, v_grad, k_sum, v_sum, *, blocks
):
    head = pl.program_id(0)
    total, capacity, _ = query.shape
    tokens = keys.shape[1]
    scale = HEAD ** (-0.5)
    rate = scale * LOG2E
    k_sum[...] = jnp.zeros_like(k_sum)
    v_sum[...] = jnp.zeros_like(v_sum)
    for tile in range(total // blocks):
        first = tile * blocks
        q = picked(query, index, first, blocks)
        k = picked(keys, index, 0, first + blocks)
        v = picked(values, index, 0, first + blocks)
        g = picked(mixed_grad, index, first, blocks)
        log = picked(logs, index, first, blocks)
        lane = lax.broadcasted_iota(jnp.int32, log.shape, 1)
        log = jnp.sum(jnp.where(lane == head, log, 0.0), axis=1, keepdims=True)
        bias = tile_bias(picked(info, index, first, blocks), tile, blocks, tokens)
        probs = jnp.exp2((dot_t(q, k) + bias) * rate - log)
        prob_grad = dot_t(g, v)
        center = jnp.sum(probs * prob_grad, axis=1, keepdims=True)
        score_grad = (probs * (prob_grad - center)).astype(BF)
        out = (dot(score_grad, k) * scale).astype(BF)
        for j in range(blocks):
            q_grad[index[first + j]] = out[j * capacity : (j + 1) * capacity]
        k_part = t_dot(score_grad, q)
        v_part = t_dot(probs.astype(BF), g)
        for j in range(first + blocks):
            rows = slice(j * tokens, (j + 1) * tokens)
            k_sum[index[j]] += k_part[rows]
            v_sum[index[j]] += v_part[rows]
    k_grad[...] = (k_sum[...] * scale).astype(BF)
    v_grad[...] = v_sum[...].astype(BF)


def head_spec(shape, skip=0):
    return pl.BlockSpec((shape[0], shape[1], HEAD), lambda h, index: (0, 0, h + skip))


def flat_spec(shape):
    return pl.BlockSpec(shape, lambda h, index: (0, 0, 0))


def attend(index, info, query, both):
    total, capacity, width = query.shape
    tokens = both.shape[1]
    heads = width // HEAD
    blocks = max(1, 256 // capacity)
    log_shape = (total, capacity, 128)
    flops = 4 * total * capacity * total * tokens * width
    return pl.pallas_call(
        functools.partial(attend_kernel, blocks=blocks),
        grid_spec=pltpu.PrefetchScalarGridSpec(
            num_scalar_prefetch=1,
            grid=(heads,),
            in_specs=[
                flat_spec(info.shape),
                head_spec(query.shape),
                head_spec(both.shape),
                head_spec(both.shape, heads),
            ],
            out_specs=[head_spec(query.shape), flat_spec(log_shape)],
        ),
        out_shape=[
            jax.ShapeDtypeStruct(query.shape, BF),
            jax.ShapeDtypeStruct(log_shape, F32),
        ],
        compiler_params=pltpu.CompilerParams(vmem_limit_bytes=50 << 20),
        cost_estimate=pl.CostEstimate(
            flops=flops, bytes_accessed=16 << 20, transcendentals=flops // 512
        ),
    )(index, info, query, both, both)


def attend_back(index, info, query, both, logs, mixed_grad):
    total, capacity, width = query.shape
    tokens = both.shape[1]
    heads = width // HEAD
    blocks = max(1, 256 // capacity)
    flops = 10 * total * capacity * total * tokens * width
    key_shape = (total, tokens, width)
    return pl.pallas_call(
        functools.partial(attend_back_kernel, blocks=blocks),
        grid_spec=pltpu.PrefetchScalarGridSpec(
            num_scalar_prefetch=1,
            grid=(heads,),
            in_specs=[
                flat_spec(info.shape),
                head_spec(query.shape),
                head_spec(both.shape),
                head_spec(both.shape, heads),
                flat_spec(logs.shape),
                head_spec(mixed_grad.shape),
            ],
            out_specs=[head_spec(query.shape), head_spec(key_shape), head_spec(key_shape)],
            scratch_shapes=[
                pltpu.VMEM((total, tokens, HEAD), F32),
                pltpu.VMEM((total, tokens, HEAD), F32),
            ],
        ),
        out_shape=[
            jax.ShapeDtypeStruct(query.shape, BF),
            jax.ShapeDtypeStruct(key_shape, BF),
            jax.ShapeDtypeStruct(key_shape, BF),
        ],
        compiler_params=pltpu.CompilerParams(vmem_limit_bytes=50 << 20),
        cost_estimate=pl.CostEstimate(
            flops=flops, bytes_accessed=32 << 20, transcendentals=flops // 1280
        ),
    )(index, info, query, both, both, logs, mixed_grad)


def body(
    inputs,
    lengths,
    attn_routes,
    mlp_routes,
    slot_order,
    gain_attn,
    router_attn,
    w_key,
    w_value,
    w_query,
    w_out,
    gain_mlp,
    router_mlp,
    w_gate,
    w_up,
    w_down,
    d_out,
):
    seq_count, stretch, width = inputs.shape
    tok = seq_count * stretch
    top_count = attn_routes.shape[2]
    experts = router_attn.shape[1]
    cap = top_count * tok // experts
    slots = experts * cap
    dps, seqs = lax.axis_size("dp"), lax.axis_size("seq")
    total = experts * seqs
    e_at, s_at, d_at = lax.axis_index("expert"), lax.axis_index("seq"), lax.axis_index("dp")
    block = e_at * seqs + s_at
    rows_own = w_key.shape[0]
    inner = w_key.shape[1]
    half = inner // seqs

    absolute = lax.broadcasted_iota(jnp.int32, (total,), 0)
    index = lax.rem(absolute % seqs - s_at + seqs, seqs) * experts + lax.rem(
        absolute // seqs - e_at + experts, experts
    )
    block_of = lax.rem(absolute % experts + e_at, experts) * seqs + lax.rem(
        absolute // experts + s_at, seqs
    )

    x_low = inputs.reshape(tok, width)
    x_blocks = group_gather(x_low)

    def halves(weight):
        split = weight.reshape(rows_own, dps, seqs, inner // (dps * seqs))
        return (
            lax.dynamic_index_in_dim(split, s_at, 2, keepdims=False).reshape(rows_own, half),
            lax.dynamic_index_in_dim(split, 1 - s_at, 2, keepdims=False).reshape(rows_own, half),
        )

    split_all = [halves(weight) for weight in (w_key, w_value, w_query[0])]
    w_keep = jnp.concatenate([pair[0] for pair in split_all], axis=1)
    w_give = jnp.concatenate([pair[1] for pair in split_all], axis=1)
    w_took = swap_x(w_give)
    w_pair = jnp.where(
        s_at == 0,
        jnp.concatenate([w_keep, w_took], axis=0),
        jnp.concatenate([w_took, w_keep], axis=0),
    )
    w_three = dp_gather(w_pair)
    out_w = dp_gather(w_out[0])

    small = jnp.concatenate(
        [gain_attn[None], router_attn.T, gain_mlp[None], router_mlp.T], axis=0
    )
    small = lax.all_gather(small, ("dp", "seq"), axis=1, tiled=True)
    norm_one = small[0].astype(F32)
    route_one = small[1 : 1 + experts].T
    norm_two = small[1 + experts].astype(F32)
    route_two = small[2 + experts :].T

    column = lax.broadcasted_iota(jnp.int32, (seq_count, stretch), 1)
    is_valid = (block * stretch + column < lengths[:, None]).reshape(tok)
    order = slot_order.reshape(tok)
    attn_idx = attn_routes.reshape(tok, top_count)
    mlp_idx = mlp_routes.reshape(tok, top_count)
    attn_kept, attn_slot = route_pairs(attn_idx, order, is_valid, cap)
    mlp_kept, mlp_slot = route_pairs(mlp_idx, order, is_valid, cap)
    attn_keep = attn_kept.astype(F32)
    mlp_keep = mlp_kept.astype(F32)
    attn_hot = spots(attn_idx, attn_kept, attn_slot, experts, cap)
    mlp_hot = spots(mlp_idx, mlp_kept, mlp_slot, experts, cap)
    attn_pick = (attn_hot[0] | attn_hot[1]).astype(BF)
    mlp_pick = (mlp_hot[0] | mlp_hot[1]).astype(BF)

    g_low = d_out.reshape(tok, width)
    grad_out = g_low.astype(F32)
    g_send = t_dot(mlp_pick, g_low).astype(BF).reshape(experts, cap, width)
    g_took = z_rounds([g_send[r] for r in range(experts)], -1)
    g_parts = square_gather(jnp.concatenate(g_took, axis=0))
    g_rows = jnp.concatenate(g_parts, axis=0)
    gate_w, up_w, down_w = w_gate[0], w_up[0], w_down[0]
    act_back = dot_t(g_rows, down_w)

    flat = jnp.where(attn_kept, attn_idx * cap + attn_slot, -1)
    slot_ids = lax.broadcasted_iota(jnp.int32, (1, slots), 1)
    tok_ids = lax.broadcasted_iota(jnp.int32, (tok, 1), 0) + 1
    table = sum(
        jnp.sum(jnp.where(flat[:, k : k + 1] == slot_ids, tok_ids, 0), axis=0, dtype=jnp.int32)
        for k in range(top_count)
    )
    tables = lax.all_gather(table.reshape(experts, cap), ("expert", "seq"), axis=0, tiled=False)
    tables = lax.dynamic_index_in_dim(tables, e_at, 1, keepdims=False)[block_of] - 1
    pick = (tables[:, :, None] == lax.broadcasted_iota(jnp.int32, (1, 1, tok), 2)).astype(BF)
    row_seq = jnp.where(tables >= 0, tables // stretch, 0)
    row_place = jnp.where(tables >= 0, block_of[:, None] * stretch + tables % stretch, 0)
    info = jnp.stack([row_seq, row_place], axis=2)

    x_all = jnp.concatenate(x_blocks, axis=0)
    normed_all = rms_norm(x_all.astype(F32), norm_one).astype(BF)
    both = dot(normed_all, w_three[:, : 2 * half]).astype(BF).reshape(total, tok, 2 * half)
    rows_one = jnp.einsum(
        "bct,btd->bcd", pick, normed_all.reshape(total, tok, width), preferred_element_type=F32
    ).astype(BF)
    query = dot(rows_one.reshape(total * cap, width), w_three[:, 2 * half :]).astype(BF)
    query = query.reshape(total, cap, half)
    mixed, logs = attend(index, info, query, both)
    partial = dot(mixed.reshape(total * cap, half), out_w).astype(BF)
    partial = partial.reshape(seqs, experts, cap, width)
    attn_out = [
        add_low(partial[0, r], swap_x(partial[1, r])) for r in range(experts)
    ]
    attn_pairs = jnp.concatenate(z_rounds(attn_out, 1), axis=0)

    x_in = x_low.astype(F32)
    normed_one = normed_all[:tok]
    attn_gates = gate_values(normed_one, route_one, attn_idx)
    attn_weight = attn_gates * attn_keep
    attn_mix = weigh(attn_hot, attn_weight)
    mix_high, mix_low = in_two(attn_mix)
    hidden = x_in + dot(mix_high, attn_pairs) + dot(mix_low, attn_pairs)
    normed_two = rms_norm(hidden, norm_two).astype(BF)
    mlp_gates = gate_values(normed_two, route_two, mlp_idx)
    mlp_weight = mlp_gates * mlp_keep
    mlp_mix = weigh(mlp_hot, mlp_weight)

    rows_send = t_dot(mlp_pick, normed_two).astype(BF).reshape(experts, cap, width)
    rows_took = z_rounds([rows_send[r] for r in range(experts)], -1)
    gates_send = jnp.sum(mlp_mix, axis=0).reshape(experts, cap)
    gates_took = z_rounds([gates_send[r : r + 1] for r in range(experts)], -1)
    rows_parts = square_gather(jnp.concatenate(rows_took, axis=0))
    gates_parts = square_gather(jnp.concatenate(gates_took, axis=0))
    rows = jnp.concatenate(rows_parts, axis=0)
    pair_gate = jnp.concatenate(gates_parts, axis=0).reshape(-1, 1)
    everyone = dps * seqs
    gate_pre = dot(rows, gate_w)
    up_pre = dot(rows, up_w)
    sigma = jax.nn.sigmoid(gate_pre)
    activated = gate_pre * sigma
    act = activated * up_pre
    act_low = act.astype(BF)
    gate_partial = jnp.sum(act * act_back, axis=1)
    hidden_grad = act_back * pair_gate
    gate_grad = (hidden_grad * up_pre * sigma * (1.0 + gate_pre * (1.0 - sigma))).astype(BF)
    up_grad = (hidden_grad * activated).astype(BF)
    act_scaled = (act * pair_gate).astype(BF)
    in_partial = (dot_t(gate_grad, gate_w) + dot_t(up_grad, up_w)).astype(BF)
    in_partial = in_partial.reshape(everyone, slots, width)
    in_sum = square_scatter([in_partial[j] for j in range(everyone)])
    gate_partial = gate_partial.reshape(everyone, experts, cap)
    gate_sum = square_scatter([gate_partial[j] for j in range(everyone)])
    out_partial = dot(act_low, down_w).astype(BF).reshape(everyone, slots, width)
    out_sum = square_scatter([out_partial[j] for j in range(everyone)])
    in_pairs = jnp.concatenate(
        z_rounds([in_sum[r * cap : (r + 1) * cap] for r in range(experts)], 1), axis=0
    )
    slot_grad = jnp.concatenate(
        z_rounds([gate_sum[r : r + 1] for r in range(experts)], 1), axis=0
    ).reshape(1, slots)
    out_pairs = jnp.concatenate(
        z_rounds([out_sum[r * cap : (r + 1) * cap] for r in range(experts)], 1), axis=0
    )
    grad_gate = t_dot(rows, gate_grad)
    grad_up = t_dot(rows, up_grad)
    grad_down = t_dot(act_scaled, g_rows)

    mlp_high, mlp_low = in_two(mlp_mix)
    output = hidden + dot(mlp_high, out_pairs) + dot(mlp_low, out_pairs)
    result_out = output.astype(BF).reshape(seq_count, stretch, width)

    mlp_gate_grad = jnp.concatenate(
        [jnp.sum(jnp.where(hot, slot_grad, 0.0), axis=1, keepdims=True) for hot in mlp_hot], axis=1
    )
    router_two_grad, router_two_input = gate_grads(
        normed_two, route_two, mlp_idx, mlp_gates, mlp_gate_grad
    )
    normed_two_grad = dot(mlp_pick, in_pairs) + router_two_input
    residual_grad, norm_two_grad = norm_back(hidden, norm_two, normed_two_grad)
    hidden_total = grad_out + residual_grad

    total_high, total_low = in_two(hidden_total)
    mix_t = attn_mix.T
    row_weight = jnp.sum(attn_mix, axis=0)[:, None]
    dh_send = (
        (t_dot(attn_pick, total_high) + t_dot(attn_pick, total_low)) * row_weight
    ).astype(BF).reshape(experts, cap, width)
    dh_own = z_rounds([dh_send[r] for r in range(experts)], -1)
    dh_other = [swap_x(part) for part in dh_own]
    dh_rows = jnp.concatenate(dh_own + dh_other, axis=0)
    slot_dots = dot_t(total_high, attn_pairs)
    attn_gate_grad = jnp.concatenate(
        [jnp.sum(jnp.where(hot, slot_dots, 0.0), axis=1, keepdims=True) for hot in attn_hot], axis=1
    )
    mixed_grad = dot_t(dh_rows, out_w).astype(BF).reshape(total, cap, half)
    grad_out_w = dp_scatter(
        lambda d: t_dot(
            lax.dynamic_slice_in_dim(
                mixed.reshape(total * cap, half), d * rows_own, rows_own, axis=1
            ),
            dh_rows,
        ).astype(BF)
    )
    q_grad, k_grad, v_grad = attend_back(index, info, query, both, logs, mixed_grad)
    q_slots = jnp.einsum("bct,bch->bth", pick, q_grad, preferred_element_type=F32).astype(BF)
    three_grad = jnp.concatenate([k_grad, v_grad, q_slots], axis=2)
    flat_three = three_grad.reshape(total * tok, 3 * half)
    in_one = dot_t(flat_three, w_three).astype(BF).reshape(total, tok, width)
    one_sum = group_scatter([in_one[j] for j in range(total)])

    feature_rows = rows_own * seqs
    w_grads = dp_scatter(
        lambda d: t_dot(
            lax.dynamic_slice_in_dim(normed_all, d * feature_rows, feature_rows, axis=1),
            flat_three,
        ).astype(BF)
    ).reshape(seqs, rows_own, 3 * half)
    w_mine = lax.dynamic_index_in_dim(w_grads, s_at, 0, keepdims=False)
    w_other = swap_x(lax.dynamic_index_in_dim(w_grads, 1 - s_at, 0, keepdims=False))

    def joined(mine, other):
        pieces = [part.reshape(rows_own, dps, inner // (dps * seqs)) for part in (mine, other)]
        pair = jnp.where(
            s_at == 0, jnp.stack(pieces, axis=2), jnp.stack(pieces[::-1], axis=2)
        )
        return pair.reshape(rows_own, inner)

    grad_query = joined(w_mine[:, 2 * half :], w_other[:, 2 * half :]).astype(F32)
    shared_grads = jnp.stack(
        [joined(w_mine[:, j * half : (j + 1) * half], w_other[:, j * half : (j + 1) * half]) for j in range(2)]
    )
    shared_grads = lax.psum(shared_grads, "expert").astype(F32)

    router_one_grad, router_one_input = gate_grads(
        normed_one, route_one, attn_idx, attn_gates, attn_gate_grad
    )
    normed_one_grad = one_sum.astype(F32) + router_one_input
    input_grad, norm_one_grad = norm_back(x_in, norm_one, normed_one_grad)
    grad_x = (hidden_total + input_grad).astype(BF).reshape(seq_count, stretch, width)

    little = jnp.concatenate(
        [norm_one_grad[None], router_one_grad.T, norm_two_grad[None], router_two_grad.T], axis=0
    )
    little = lax.psum(little, ("dp", "expert", "seq"))
    little = lax.dynamic_slice_in_dim(little, (d_at * seqs + s_at) * rows_own, rows_own, axis=1)
    return (
        result_out,
        grad_x,
        little[0],
        little[1 : 1 + experts].T,
        shared_grads[0],
        shared_grads[1],
        grad_query[None],
        grad_out_w.astype(F32)[None],
        little[1 + experts],
        little[2 + experts :].T,
        grad_gate[None],
        grad_up[None],
        grad_down[None],
    )


def solution(mesh):
    in_specs = (
        P("dp", ("expert", "seq"), None),
        P("dp"),
        P("dp", ("expert", "seq"), None),
        P("dp", ("expert", "seq"), None),
        P("dp", ("expert", "seq"), None),
        P(("dp", "seq")),
        P(("dp", "seq"), None),
        P(("dp", "seq"), None),
        P(("dp", "seq"), None),
        P("expert", ("dp", "seq"), None),
        P("expert", ("dp", "seq"), None),
        P(("dp", "seq")),
        P(("dp", "seq"), None),
        P("expert", None, ("dp", "seq")),
        P("expert", None, ("dp", "seq")),
        P("expert", ("dp", "seq"), None),
        P("dp", ("expert", "seq"), None),
    )
    out_specs = (
        P("dp", ("expert", "seq"), None),
        P("dp", ("expert", "seq"), None),
        P(("dp", "seq")),
        P(("dp", "seq"), None),
        P(("dp", "seq"), None),
        P(("dp", "seq"), None),
        P("expert", ("dp", "seq"), None),
        P("expert", ("dp", "seq"), None),
        P(("dp", "seq")),
        P(("dp", "seq"), None),
        P("expert", None, ("dp", "seq")),
        P("expert", None, ("dp", "seq")),
        P("expert", ("dp", "seq"), None),
    )
    return jax.shard_map(body, mesh=mesh, in_specs=in_specs, out_specs=out_specs, check_vma=False)
```

time: 2450 us -> 1590 us (0.65)
  waiting for transfers between devices: 1210 us -> 697 us
  local copies, waits for them, and re-layouts: 327 us -> 106 us
  blocking collectives: 192 us -> 63.9 us
  matrix products: 481 us -> 355 us
  starting transfers between devices: 32.3 us -> 135 us
  Pallas kernels: 0 us -> 77.2 us
  other arithmetic: 177 us -> 132 us
    reduce_scatter x8 -> x0, waiting for transfers between devices: 648 us -> none  [the longest x1 143 us: body(): lax.psum_scatter(key_grad.reshape(seq_count, seq_len, -1).astype(jnp.bflo...]
    ppermute x0 -> x118, waiting for transfers between devices: none -> 517 us  [the longest x33 276 us: swap_x(): return lax.ppermute(value, 'seq', flip(2, 1))]
    all_gather x8 -> x0, waiting for transfers between devices: 346 us -> none  [the longest x1 97.3 us: body(): lax.all_gather(values_here.reshape(seq_count, stretch, -1), ('expert', 's...]
    all_to_all x7 -> x0, waiting for transfers between devices: 169 us -> none  [the longest x1 75.8 us: body(): lax.all_to_all(attn_send, 'expert', split_axis=0, concat_axis=0, tiled=True)]
    psum x1 -> x2, waiting for transfers between devices: 40.8 us -> 180 us  [the longest x1 101 us: body(): little = lax.psum(little, ('dp', 'expert', 'seq'))]
    ppermute x0 -> x118, starting transfers between devices: none -> 135 us  [the longest x24 46.2 us: z_rounds(): lax.ppermute(pieces[r], 'expert', ring(count, sign * r))]
    dot_general x55 -> x40, matrix products: 481 us -> 355 us  [the longest x6 118 us: dot_t(): lax.dot_general(left, right, (((1,), (1,)), ((), ())), preferred_element_...]
    all_to_all x2 -> x0, blocking collectives: 107 us -> none  [the longest x1 54.4 us: body(): lax.all_to_all(mlp_send, 'expert', split_axis=0, concat_axis=0, tiled=True)]
  transfers between devices with their start and end apart: 26 -> 120, of which waited for: 19 -> 48; matrix products, arithmetic and copies ran while one was open for 22% -> 28% of each run, Pallas kernels for 0% -> 2%
where the time goes in v1:
time: 1590 us; the launch traced here: 1580 us
  waiting for transfers between devices  697 us (44%)
  matrix products  355 us (22%)
  starting transfers between devices  135 us (8%)
  other arithmetic  132 us (8%)
  local copies, waits for them, and re-layouts  106 us (7%)
  Pallas kernels  77.2 us (5%)
  blocking collectives  63.9 us (4%)
  between operations  16.6 us (1%)
    ppermute x33, waiting for transfers between devices, swap_x(): return lax.ppermute(value, 'seq', flip(2, 1))  276 us
    ppermute x24, waiting for transfers between devices, z_rounds(): lax.ppermute(pieces[r], 'expert', ring(count, sign * r))  119 us
    dot_general x6, matrix products, dot_t(): lax.dot_general(left, right, (((1,), (1,)), ((), ())), preferred_element_...  118 us
    dot_general x15, matrix products, t_dot(): lax.dot_general(left, right, (((0,), (0,)), ((), ())), preferred_element_...  116 us
    dot_general x13, matrix products, dot(): return jnp.dot(left, right, preferred_element_type=F32)  104 us
    psum x1, waiting for transfers between devices, body(): little = lax.psum(little, ('dp', 'expert', 'seq'))  101 us
    psum x1, waiting for transfers between devices, body(): shared_grads = lax.psum(shared_grads, 'expert').astype(F32)  79.5 us
    ppermute x19, waiting for transfers between devices, swap_y(): return lax.ppermute(value, 'dp', flip(4, 2))  73.4 us
  transfers between devices with their start and end apart: 120, of which 48 were waited for; matrix products, arithmetic and copies ran while one was open for 28% of the time, Pallas kernels for 2%

profile of v1, /device:TPU:0, one launch (start us, length us, event | category | flops | bytes accessed | tf_op | source)
XLA Modules:
  0.0 1583.1 jit_solution(1669114109369370785)
XLA Ops:
  31.3 51.5 %all_gather.7 = s32[8,4,128]{2,1,0:T(4,128)S(1)} all-gather(s32[1,4,128]{2,1,0:T(4,128)S(1)} %add_bitcast_fusion), channel_id=1, replica_groups=mesh['dp'=4,'expert'=4,'seq'=2] {'expert','seq'}, dimensions={0}, use_global_device_ids=true | all-gather | bytes 18432 | tf_op jit(solution)/shard_map/all_gather | solution.py:520
  83.7 12.5 all_gather.6
  101.4 18.2 %maximum_select_fusion.4 = bf16[512,3072]{0,1:T(8,128)(2,1)} fusion(bf16[256,3072]{0,1:T(8,128)(2,1)} %collective-permute-done.8, bf16[256,1024]{0,1:T(8,128)(2,1)S(1)} %bitcast.280, bf16[256,1024]{0,1:T(8,128)(2,1)S(1)} %bitcast.281, bf16[256,1024]{0,1:T(8,128)(2,1)S(1)} %bitcast.282, pred[]{:T(512)S(6)} %eq.254), kind=kLoop, calls=%fused_computation.50 | loop fusion | flops 26738688 | bytes 6291457 | tf_op jit(solution)/shard_map/jit(_where)/select_n | solution.py:473
  138.8 10.2 collective-permute-done.3
  152.8 15.9 %collective-permute-done.5 = bf16[256,2048]{1,0:T(8,128)(2,1)S(1)} collective-permute-done((bf16[256,2048]{1,0:T(8,128)(2,1)}, bf16[256,2048]{1,0:T(8,128)(2,1)S(1)}, u32[]{:S(2)}, u32[]{:S(2)}) %collective-permute-start.5) | collective-permute-done | bytes 1048608 | tf_op jit(solution)/shard_map/ppermute | solution.py:40
  175.1 16.0 %collective-permute-done.6 = bf16[256,2048]{1,0:T(8,128)(2,1)S(1)} collective-permute-done((bf16[256,2048]{1,0:T(8,128)(2,1)S(1)}, bf16[256,2048]{1,0:T(8,128)(2,1)S(1)}, u32[]{:S(2)}, u32[]{:S(2)}) %collective-permute-start.6) | collective-permute-done | bytes 1048608 | tf_op jit(solution)/shard_map/ppermute | solution.py:40
  193.0 20.5 %collective-permute-done.7 = bf16[256,2048]{1,0:T(8,128)(2,1)S(1)} collective-permute-done((bf16[256,2048]{1,0:T(8,128)(2,1)}, bf16[256,2048]{1,0:T(8,128)(2,1)S(1)}, u32[]{:S(2)}, u32[]{:S(2)}) %collective-permute-start.7) | collective-permute-done | bytes 1048608 | tf_op jit(solution)/shard_map/ppermute | solution.py:40
  217.3 8.2 fusion.14
  225.5 8.6 multiply_convert_fusion.1
  234.1 7.8 maximum_select_fusion.1
  242.0 7.3 maximum_select_fusion.2
  254.1 5.7 fusion.62
  259.9 21.1 %fusion.6 = bf16[2048,2048]{1,0:T(8,128)(2,1)} fusion(bf16[2048,2048]{1,0:T(8,128)(2,1)} %multiply_convert_fusion.1, bf16[2048,3072]{0,1:T(8,128)(2,1)S(1)} %maximum_select_fusion), kind=kOutput, calls=%fused_computation.19 | convolution fusion | flops 17184063488 | bytes 25165824 | tf_op jit(solution)/shard_map/dot_general | solution.py:20
  281.0 27.8 %shard_map.264 = (bf16[8,128,1024]{2,1,0:T(8,128)(2,1)S(1)}, f32[8,128,128]{2,1,0:T(8,128)S(1)}) custom-call(s32[8]{0:T(128)S(1)} %get-tuple-element.237.index, s32[8,128,2]{2,1,0:T(8,128)S(1)} %copy.161.info, bf16[8,128,1024]{2,1,0:T(8,128)(2,1)} %bitcast.381, bf16[8,256,2048]{2,1,0:T(8,128)(2,1)} %bitcast.376, bf16[8,256,2048]{2,1,0:T(8,128)(2,1)} %bitcast.377), custom_call_target="tpu_custom_call" | custom-call | flops 8589934592 | bytes 16777216 | tf_op jit(solution)/shard_map/pallas_call | solution.py:356
  322.8 6.0 collective-permute-done.15
  329.4 10.7 collective-permute-done.20
  340.0 11.2 collective-permute-done.18
  351.3 10.5 collective-permute-done.16
  365.7 11.1 collective-permute-done.21
  377.7 31.5 %collective-permute-done.19 = bf16[128,2048]{1,0:T(8,128)(2,1)S(1)} collective-permute-done((bf16[128,2048]{1,0:T(8,128)(2,1)S(1)}, bf16[128,2048]{1,0:T(8,128)(2,1)S(1)}, u32[]{:S(2)}, u32[]{:S(2)}) %collective-permute-start.19) | collective-permute-done | bytes 524320 | tf_op jit(solution)/shard_map/ppermute | solution.py:54
  418.2 7.5 collective-permute-done.49
  440.5 12.1 collective-permute-done.23
  452.6 8.2 collective-permute-done.22
  480.7 30.1 %collective-permute-done.26 = bf16[512,2048]{1,0:T(8,128)(2,1)S(1)} collective-permute-done((bf16[512,2048]{1,0:T(8,128)(2,1)S(1)}, bf16[512,2048]{1,0:T(8,128)(2,1)S(1)}, u32[]{:S(2)}, u32[]{:S(2)}) %collective-permute-start.26) | collective-permute-done | bytes 2097184 | tf_op jit(solution)/shard_map/ppermute | solution.py:48
  519.2 16.6 %collective-permute-done.28 = bf16[256,2048]{1,0:T(8,128)(2,1)S(1)} collective-permute-done((bf16[256,2048]{1,0:T(8,128)(2,1)S(1)}, bf16[256,2048]{1,0:T(8,128)(2,1)S(1)}, u32[]{:S(2)}, u32[]{:S(2)}) %collective-permute-start.28) | collective-permute-done | bytes 1048608 | tf_op jit(solution)/shard_map/ppermute | solution.py:40
  541.3 17.5 %fusion.20 = f32[4096,704]{0,1:T(8,128)} fusion(bf16[4096,2048]{1,0:T(8,128)(2,1)S(1)} %constant_dynamic-update-slice_fusion.9, bf16[1,2048,704]{1,2,0:T(8,128)(2,1)} %param.31), kind=kOutput, calls=%fused_computation.59 | convolution fusion | flops 11811160064 | bytes 31195136 | tf_op jit(solution)/shard_map/dot_general | solution.py:20
  558.8 16.2 %fusion.24 = f32[4096,704]{0,1:T(8,128)} fusion(bf16[4096,2048]{1,0:T(8,128)(2,1)S(1)} %constant_dynamic-update-slice_fusion.9, bf16[1,2048,704]{1,2,0:T(8,128)(2,1)} %param.30), kind=kOutput, calls=%fused_computation.63 | convolution fusion | flops 11811160064 | bytes 31195136 | tf_op jit(solution)/shard_map/dot_general | solution.py:20
  575.0 33.3 %multiply_reduce_fusion.1 = (f32[4096]{0:T(1024)S(1)}, f32[4096,704]{0,1:T(8,128)}) fusion(f32[4096,704]{0,1:T(8,128)} %fusion.20, f32[4096,704]{0,1:T(8,128)} %fusion.24, bf16[4096,2048]{1,0:T(8,128)(2,1)} %constant_dynamic-update-slice_fusion.21, bf16[1,704,2048]{2,1,0:T(8,128)(2,1)S(1)} %copy-done), kind=kOutput, calls=%fused_computation.9 | convolution fusion | flops 11831341056 | bytes 54280192 | tf_op jit(solution)/shard_map/dot_general | solution.py:24
  617.9 25.6 %convolution_convert_fusion = bf16[4096,2048]{1,0:T(8,128)(2,1)} fusion(bf16[1,704,2048]{2,1,0:T(8,128)(2,1)S(1)} %copy-done, f32[4096,704]{0,1:T(8,128)} %fusion.20, f32[4096,704]{0,1:T(8,128)} %fusion.24), kind=kOutput, calls=%fused_computation.5 | convolution fusion | flops 11836850176 | bytes 42729472 | tf_op jit(solution)/shard_map/dot_general | solution.py:20
  650.1 6.0 fusion.200
  676.0 23.3 %fusion.15 = f32[1,704,2048]{2,1,0:T(8,128)} fusion(bf16[4096,2048]{1,0:T(8,128)(2,1)} %constant_dynamic-update-slice_fusion.21, f32[4096]{0:T(1024)S(1)} %bitcast.305, f32[4096,704]{0,1:T(8,128)} %fusion.20, f32[4096,704]{0,1:T(8,128)} %fusion.24), kind=kOutput, calls=%fused_computation.47 | convolution fusion | flops 11831345152 | bytes 45629440 | tf_op jit(solution)/shard_map/dot_general | solution.py:28
  699.3 16.5 %multiply_convert_fusion.3 = (bf16[4096,704]{0,1:T(8,128)(2,1)}, bf16[4096,704]{0,1:T(8,128)(2,1)S(1)}) fusion(f32[4096,704]{0,1:T(8,128)} %get-tuple-element.234, f32[4096]{0:T(1024)S(1)} %bitcast.306, f32[4096,704]{0,1:T(8,128)} %fusion.24, f32[4096,704]{0,1:T(8,128)} %fusion.20), kind=kLoop, calls=%fused_computation.10 | loop fusion | flops 40370176 | bytes 46153728 | tf_op jit(solution)/shard_map/convert_element_type | solution.py:573
  715.8 17.6 %fusion.22 = f32[4096,2048]{1,0:T(8,128)} fusion(bf16[4096,704]{0,1:T(8,128)(2,1)S(1)} %get-tuple-element.98, bf16[1,2048,704]{1,2,0:T(8,128)(2,1)S(1)} %copy-done.87), kind=kOutput, calls=%fused_computation.61 | convolution fusion | flops 11811160064 | bytes 42205184 | tf_op jit(solution)/shard_map/dot_general | solution.py:24
  733.4 26.3 %add_convert_fusion = bf16[4096,2048]{1,0:T(8,128)(2,1)} fusion(f32[4096,2048]{1,0:T(8,128)} %fusion.22, bf16[4096,704]{0,1:T(8,128)(2,1)} %get-tuple-element.97, bf16[1,2048,704]{1,2,0:T(8,128)(2,1)} %param.31), kind=kOutput, calls=%fused_computation.1 | convolution fusion | flops 11827937280 | bytes 58982400 | tf_op jit(solution)/shard_map/dot_general | solution.py:24
  759.7 6.6 fusion.199
  767.4 19.2 %convolution_bitcast_fusion = f32[1,2048,704]{1,2,0:T(8,128)} fusion(bf16[4096,704]{0,1:T(8,128)(2,1)} %get-tuple-element.97, bf16[4096,2048]{1,0:T(8,128)(2,1)} %copy-done.63), kind=kOutput, calls=%fused_computation.48 | convolution fusion | flops 11811160064 | bytes 28311552 | tf_op jit(solution)/shard_map/dot_general | solution.py:28
  796.1 8.2 add_convert_fusion.7
  805.6 34.6 %collective-permute-done.38 = bf16[256,2048]{1,0:T(8,128)(2,1)S(1)} collective-permute-done((bf16[256,2048]{1,0:T(8,128)(2,1)S(1)}, bf16[256,2048]{1,0:T(8,128)(2,1)S(1)}, u32[]{:S(2)}, u32[]{:S(2)}) %collective-permute-start.38) | collective-permute-done | bytes 1048608 | tf_op jit(solution)/shard_map/ppermute | solution.py:40
  843.1 19.6 %collective-permute-done.73 = bf16[256,2048]{1,0:T(8,128)(2,1)S(1)} collective-permute-done((bf16[256,2048]{1,0:T(8,128)(2,1)S(1)}, bf16[256,2048]{1,0:T(8,128)(2,1)S(1)}, u32[]{:S(2)}, u32[]{:S(2)}) %collective-permute-start.73) | collective-permute-done | bytes 1048608 | tf_op jit(solution)/shard_map/ppermute | solution.py:40
  869.5 19.2 %collective-permute-done.39 = bf16[256,2048]{1,0:T(8,128)(2,1)S(1)} collective-permute-done((bf16[256,2048]{1,0:T(8,128)(2,1)S(1)}, bf16[256,2048]{1,0:T(8,128)(2,1)S(1)}, u32[]{:S(2)}, u32[]{:S(2)}) %collective-permute-start.39) | collective-permute-done | bytes 1048608 | tf_op jit(solution)/shard_map/ppermute | solution.py:48
  892.0 19.1 %collective-permute-done.70 = bf16[256,2048]{1,0:T(8,128)(2,1)S(1)} collective-permute-done((bf16[256,2048]{1,0:T(8,128)(2,1)S(1)}, bf16[256,2048]{1,0:T(8,128)(2,1)S(1)}, u32[]{:S(2)}, u32[]{:S(2)}) %collective-permute-start.70) | collective-permute-done | bytes 1048608 | tf_op jit(solution)/shard_map/ppermute | solution.py:40
  913.6 19.2 %collective-permute-done.74 = bf16[256,2048]{1,0:T(8,128)(2,1)S(1)} collective-permute-done((bf16[256,2048]{1,0:T(8,128)(2,1)S(1)}, bf16[256,2048]{1,0:T(8,128)(2,1)S(1)}, u32[]{:S(2)}, u32[]{:S(2)}) %collective-permute-start.74) | collective-permute-done | bytes 1048608 | tf_op jit(solution)/shard_map/ppermute | solution.py:48
  938.3 17.5 %convolution_bitcast_fusion.1 = f32[1,2048,704]{1,2,0:T(8,128)} fusion(bf16[4096,704]{0,1:T(8,128)(2,1)S(1)} %bitcast.271, bf16[4096,2048]{1,0:T(8,128)(2,1)} %copy-done.63), kind=kOutput, calls=%fused_computation.49 | convolution fusion | flops 11811160064 | bytes 28311552 | tf_op jit(solution)/shard_map/dot_general | solution.py:28
  958.1 22.0 %collective-permute-done.79 = bf16[128,2048]{1,0:T(8,128)(2,1)S(1)} collective-permute-done((bf16[128,2048]{1,0:T(8,128)(2,1)S(1)}, bf16[128,2048]{1,0:T(8,128)(2,1)S(1)}, u32[]{:S(2)}, u32[]{:S(2)}) %collective-permute-start.79) | collective-permute-done | bytes 524320 | tf_op jit(solution)/shard_map/ppermute | solution.py:54
  987.4 11.7 collective-permute-start.96
  1003.4 10.2 collective-permute-done.96
  1015.4 19.8 %collective-permute-done.95 = bf16[128,2048]{1,0:T(8,128)(2,1)S(1)} collective-permute-done((bf16[128,2048]{1,0:T(8,128)(2,1)S(1)}, bf16[128,2048]{1,0:T(8,128)(2,1)S(1)}, u32[]{:S(2)}, u32[]{:S(2)}) %collective-permute-start.95) | collective-permute-done | bytes 524320 | tf_op jit(solution)/shard_map/ppermute | solution.py:54
  1037.4 22.8 %collective-permute-done.98 = bf16[128,2048]{1,0:T(8,128)(2,1)S(1)} collective-permute-done((bf16[128,2048]{1,0:T(8,128)(2,1)S(1)}, bf16[128,2048]{1,0:T(8,128)(2,1)S(1)}, u32[]{:S(2)}, u32[]{:S(2)}) %collective-permute-start.98) | collective-permute-done | bytes 524320 | tf_op jit(solution)/shard_map/ppermute | solution.py:40
  1060.4 7.6 convolution_convert_fusion.14
  1070.3 49.4 %shard_map.265 = (bf16[8,128,1024]{2,1,0:T(8,128)(2,1)S(1)}, bf16[8,256,1024]{2,1,0:T(8,128)(2,1)}, bf16[8,256,1024]{2,1,0:T(8,128)(2,1)}) custom-call(s32[8]{0:T(128)S(1)} %get-tuple-element.237.index, s32[8,128,2]{2,1,0:T(8,128)S(1)} %copy.161.info, bf16[8,128,1024]{2,1,0:T(8,128)(2,1)} %bitcast.382, bf16[8,256,2048]{2,1,0:T(8,128)(2,1)} %bitcast.378, ...), custom_call_target="tpu_custom_call" | custom-call | flops 21474836480 | bytes 33554432 | tf_op jit(solution)/shard_map/pallas_call | solution.py:387
  1126.5 32.1 %convolution_convert_fusion.1 = bf16[2048,2048]{1,0:T(8,128)(2,1)} fusion(bf16[2048,3072]{1,0:T(8,128)(2,1)S(1)} %bitcast.255, bf16[2048,3072]{0,1:T(8,128)(2,1)} %copy-done.12), kind=kOutput, calls=%fused_computation.20 | convolution fusion | flops 25773998080 | bytes 33554432 | tf_op jit(solution)/shard_map/dot_general | solution.py:24
  1158.6 9.8 convolution_convert_fusion.2
  1176.8 8.8 convolution_convert_fusion.3
  1185.6 9.8 convolution_convert_fusion.4
  1201.0 20.5 %collective-permute-done.106 = bf16[256,2048]{1,0:T(8,128)(2,1)} collective-permute-done((bf16[256,2048]{1,0:T(8,128)(2,1)}, bf16[256,2048]{1,0:T(8,128)(2,1)}, u32[]{:S(2)}, u32[]{:S(2)}) %collective-permute-start.106) | collective-permute-done | bytes 1048608 | tf_op jit(solution)/shard_map/ppermute | solution.py:40
  1223.1 20.8 %collective-permute-done.103 = bf16[256,2048]{1,0:T(8,128)(2,1)} collective-permute-done((bf16[256,2048]{1,0:T(8,128)(2,1)}, bf16[256,2048]{1,0:T(8,128)(2,1)}, u32[]{:S(2)}, u32[]{:S(2)}) %collective-permute-start.103) | collective-permute-done | bytes 1048608 | tf_op jit(solution)/shard_map/ppermute | solution.py:40
  1244.0 22.1 %collective-permute-done.102 = bf16[256,2048]{1,0:T(8,128)(2,1)} collective-permute-done((bf16[256,2048]{1,0:T(8,128)(2,1)}, bf16[256,2048]{1,0:T(8,128)(2,1)}, u32[]{:S(2)}, u32[]{:S(2)}) %collective-permute-start.102) | collective-permute-done | bytes 1048608 | tf_op jit(solution)/shard_map/ppermute | solution.py:40
  1271.2 8.4 collective-permute-start.104
  1282.5 8.8 convolution_convert_fusion.5
  1296.2 7.9 collective-permute-done.109
  1334.1 9.6 collective-permute-done.105
  1343.8 6.8 collective-permute-done.110
  1376.7 100.7 %all-reduce.3.cloned.1.call-done = f32[10,2048]{1,0:T(8,128)} async-done(((f32[10,2048]{1,0:T(8,128)}), f32[10,2048]{1,0:T(8,128)}) %all-reduce.3.cloned.1.call-update) | async-done | bytes 81936 | tf_op jit(solution)/shard_map/psum | solution.py:671
  1486.4 79.5 %all-reduce.5.cloned.1.call-done = bf16[2,256,2048]{1,2,0:T(8,128)(2,1)} async-done(((bf16[2,256,2048]{1,2,0:T(8,128)(2,1)}), bf16[2,256,2048]{1,2,0:T(8,128)(2,1)}) %all-reduce.5.cloned.1.call-update) | async-done | bytes 2097168 | tf_op jit(solution)/shard_map/psum | solution.py:659
  (649 shorter events, 345.2 us)
Async XLA Ops:
  7.2 1470.1 %all-reduce.3.cloned.1.call-start = ((), (), s32[]{:S(2)}) async-start(), calls=%async_computation | async-start | bytes 262144 | tf_op jit(solution)/shard_map/psum | solution.py:671
  7.2 125.0 %collective-permute-start.13 = (bf16[256,2048]{1,0:T(8,128)(2,1)}, bf16[256,2048]{1,0:T(8,128)(2,1)}, u32[]{:S(2)}, u32[]{:S(2)}) collective-permute-start(bf16[256,2048]{1,0:T(8,128)(2,1)} %bitcast.293), channel_id=1, source_target_pairs={{0,16},{8,24},{16,0},{24,8},{1,17},{9,25},{17,1},{25,9},{2,18},{10... | collective-permute-start | bytes 3145736 | tf_op jit(solution)/shard_map/ppermute | solution.py:48
  10.3 113.3 %collective-permute-start.12 = (bf16[256,2048]{1,0:T(8,128)(2,1)}, bf16[256,2048]{1,0:T(8,128)(2,1)}, u32[]{:S(2)}, u32[]{:S(2)}) collective-permute-start(bf16[256,2048]{1,0:T(8,128)(2,1)} %bitcast.294), channel_id=1, source_target_pairs={{0,8},{8,0},{16,24},{24,16},{1,9},{9,1},{17,25},{25,17},{2,10},{10... | collective-permute-start | bytes 3145736 | tf_op jit(solution)/shard_map/ppermute | solution.py:44
  10.3 109.9 %collective-permute-start.1 = (bf16[256,2048]{1,0:T(8,128)(2,1)}, bf16[256,2048]{1,0:T(8,128)(2,1)}, u32[]{:S(2)}, u32[]{:S(2)}) collective-permute-start(bf16[256,2048]{1,0:T(8,128)(2,1)} %bitcast.261), channel_id=1, source_target_pairs={{0,2},{2,4},{4,6},{6,0},{1,3},{3,5},{5,7},{7,1},{8,10},{10,12},{12... | collective-permute-start | bytes 3145736 | tf_op jit(solution)/shard_map/ppermute | solution.py:105
  11.9 110.4 %collective-permute-start = (bf16[256,2048]{1,0:T(8,128)(2,1)}, bf16[256,2048]{1,0:T(8,128)(2,1)}, u32[]{:S(2)}, u32[]{:S(2)}) collective-permute-start(bf16[256,2048]{1,0:T(8,128)(2,1)} %bitcast.262), channel_id=1, source_target_pairs={{0,6},{2,0},{4,2},{6,4},{1,7},{3,1},{5,3},{7,5},{8,14},{10,8},{12,... | collective-permute-start | bytes 3145736 | tf_op jit(solution)/shard_map/ppermute | solution.py:104
  27.0 74.5 %collective-permute-start.8 = (bf16[256,3072]{0,1:T(8,128)(2,1)}, bf16[256,3072]{0,1:T(8,128)(2,1)}, u32[]{:S(2)}, u32[]{:S(2)}) collective-permute-start(bf16[256,3072]{0,1:T(8,128)(2,1)} %pad_maximum_fusion.8), channel_id=1, source_target_pairs={{0,1},{1,0},{2,3},{3,2},{4,5},{5,4},{6,7},{7,6},{8,9},{9,8},{10,11... | collective-permute-start | bytes 4718600 | tf_op jit(solution)/shard_map/ppermute | solution.py:40
  119.6 94.4 %collective-permute-start.10 = (bf16[512,3072]{0,1:T(8,128)(2,1)}, bf16[512,3072]{0,1:T(8,128)(2,1)}, u32[]{:S(2)}, u32[]{:S(2)}) collective-permute-start(bf16[512,3072]{0,1:T(8,128)(2,1)} %maximum_select_fusion.4), channel_id=1, source_target_pairs={{0,16},{8,24},{16,0},{24,8},{1,17},{9,25},{17,1},{25,9},{2,18},{10... | collective-permute-start | bytes 9437192 | tf_op jit(solution)/shard_map/ppermute | solution.py:48
  120.2 30.5 %collective-permute-start.4 = (bf16[256,2048]{1,0:T(8,128)(2,1)S(1)}, bf16[256,2048]{1,0:T(8,128)(2,1)S(1)}, u32[]{:S(2)}, u32[]{:S(2)}) collective-permute-start(bf16[256,2048]{1,0:T(8,128)(2,1)S(1)} %bitcast.264), channel_id=1, source_target_pairs={{0,1},{1,0},{2,3},{3,2},{4,5},{5,4},{6,7},{7,6},{8,9},{9,8},{10,11... | collective-permute-start | bytes 3145736 | tf_op jit(solution)/shard_map/ppermute | solution.py:40
  132.3 36.4 %collective-permute-start.5 = (bf16[256,2048]{1,0:T(8,128)(2,1)}, bf16[256,2048]{1,0:T(8,128)(2,1)S(1)}, u32[]{:S(2)}, u32[]{:S(2)}) collective-permute-start(bf16[256,2048]{1,0:T(8,128)(2,1)} %collective-permute-done), channel_id=1, source_target_pairs={{0,1},{1,0},{2,3},{3,2},{4,5},{5,4},{6,7},{7,6},{8,9},{9,8},{10,11... | collective-permute-start | bytes 3145736 | tf_op jit(solution)/shard_map/ppermute | solution.py:40
  138.8 30.4 %collective-permute-start.14 = (bf16[256,2048]{1,0:T(8,128)(2,1)}, bf16[256,2048]{1,0:T(8,128)(2,1)S(1)}, u32[]{:S(2)}, u32[]{:S(2)}) collective-permute-start(bf16[256,2048]{1,0:T(8,128)(2,1)} %collective-permute-done.13), channel_id=1, source_target_pairs={{0,8},{8,0},{16,24},{24,16},{1,9},{9,1},{17,25},{25,17},{2,10},{10... | collective-permute-start | bytes 3145736 | tf_op jit(solution)/shard_map/ppermute | solution.py:44
  149.1 42.0 %collective-permute-start.6 = (bf16[256,2048]{1,0:T(8,128)(2,1)S(1)}, bf16[256,2048]{1,0:T(8,128)(2,1)S(1)}, u32[]{:S(2)}, u32[]{:S(2)}) collective-permute-start(bf16[256,2048]{1,0:T(8,128)(2,1)S(1)} %pad_maximum_fusion.9), channel_id=1, source_target_pairs={{0,1},{1,0},{2,3},{3,2},{4,5},{5,4},{6,7},{7,6},{8,9},{9,8},{10,11... | collective-permute-start | bytes 3145736 | tf_op jit(solution)/shard_map/ppermute | solution.py:40
  150.6 62.9 %collective-permute-start.7 = (bf16[256,2048]{1,0:T(8,128)(2,1)}, bf16[256,2048]{1,0:T(8,128)(2,1)S(1)}, u32[]{:S(2)}, u32[]{:S(2)}) collective-permute-start(bf16[256,2048]{1,0:T(8,128)(2,1)} %collective-permute-done.1), channel_id=1, source_target_pairs={{0,1},{1,0},{2,3},{3,2},{4,5},{5,4},{6,7},{7,6},{8,9},{9,8},{10,11... | collective-permute-start | bytes 3145736 | tf_op jit(solution)/shard_map/ppermute | solution.py:40
  168.7 147.4 %collective-permute-start.48 = (bf16[128,2048]{1,0:T(8,128)(2,1)}, bf16[128,2048]{1,0:T(8,128)(2,1)}, u32[]{:S(2)}, u32[]{:S(2)}) collective-permute-start(bf16[128,2048]{1,0:T(8,128)(2,1)} %get-tuple-element.146), channel_id=1, source_target_pairs={{0,2},{2,4},{4,6},{6,0},{1,3},{3,5},{5,7},{7,1},{8,10},{10,12},{12... | collective-permute-start | bytes 1572872 | tf_op jit(solution)/shard_map/ppermute | solution.py:54
  169.2 147.4 %collective-permute-start.47 = (bf16[128,2048]{1,0:T(8,128)(2,1)}, bf16[128,2048]{1,0:T(8,128)(2,1)}, u32[]{:S(2)}, u32[]{:S(2)}) collective-permute-start(bf16[128,2048]{1,0:T(8,128)(2,1)} %get-tuple-element.147), channel_id=1, source_target_pairs={{0,4},{2,6},{4,0},{6,2},{1,5},{3,7},{5,1},{7,3},{8,12},{10,14},{12... | collective-permute-start | bytes 1572872 | tf_op jit(solution)/shard_map/ppermute | solution.py:54
  191.1 127.0 %collective-permute-start.46 = (bf16[128,2048]{1,0:T(8,128)(2,1)}, bf16[128,2048]{1,0:T(8,128)(2,1)}, u32[]{:S(2)}, u32[]{:S(2)}) collective-permute-start(bf16[128,2048]{1,0:T(8,128)(2,1)} %get-tuple-element.148), channel_id=1, source_target_pairs={{0,6},{2,0},{4,2},{6,4},{1,7},{3,1},{5,3},{7,5},{8,14},{10,8},{12,... | collective-permute-start | bytes 1572872 | tf_op jit(solution)/shard_map/ppermute | solution.py:54
  316.1 35.2 %collective-permute-start.18 = (bf16[128,2048]{1,0:T(8,128)(2,1)S(1)}, bf16[128,2048]{1,0:T(8,128)(2,1)S(1)}, u32[]{:S(2)}, u32[]{:S(2)}) collective-permute-start(bf16[128,2048]{1,0:T(8,128)(2,1)S(1)} %get-tuple-element.131), channel_id=1, source_target_pairs={{0,1},{1,0},{2,3},{3,2},{4,5},{5,4},{6,7},{7,6},{8,9},{9,8},{10,11... | collective-permute-start | bytes 1572872 | tf_op jit(solution)/shard_map/ppermute | solution.py:40
  316.6 45.1 %collective-permute-start.16 = (bf16[128,2048]{1,0:T(8,128)(2,1)S(1)}, bf16[128,2048]{1,0:T(8,128)(2,1)S(1)}, u32[]{:S(2)}, u32[]{:S(2)}) collective-permute-start(bf16[128,2048]{1,0:T(8,128)(2,1)S(1)} %get-tuple-element.132), channel_id=1, source_target_pairs={{0,1},{1,0},{2,3},{3,2},{4,5},{5,4},{6,7},{7,6},{8,9},{9,8},{10,11... | collective-permute-start | bytes 1572872 | tf_op jit(solution)/shard_map/ppermute | solution.py:40
  321.1 144.8 %collective-permute-start.53 = (bf16[512,2048]{1,0:T(8,128)(2,1)}, bf16[512,2048]{1,0:T(8,128)(2,1)}, u32[]{:S(2)}, u32[]{:S(2)}) collective-permute-start(bf16[512,2048]{1,0:T(8,128)(2,1)} %pad_maximum_fusion.5), channel_id=1, source_target_pairs={{0,8},{8,0},{16,24},{24,16},{1,9},{9,1},{17,25},{25,17},{2,10},{10... | collective-permute-start | bytes 6291464 | tf_op jit(solution)/shard_map/ppermute | solution.py:44
  328.8 87.2 %collective-permute-start.50 = (bf16[512,2048]{1,0:T(8,128)(2,1)}, bf16[512,2048]{1,0:T(8,128)(2,1)S(1)}, u32[]{:S(2)}, u32[]{:S(2)}) collective-permute-start(bf16[512,2048]{1,0:T(8,128)(2,1)} %pad_maximum_fusion.5), channel_id=1, source_target_pairs={{0,16},{8,24},{16,0},{24,8},{1,17},{9,25},{17,1},{25,9},{2,18},{10... | collective-permute-start | bytes 6291464 | tf_op jit(solution)/shard_map/ppermute | solution.py:48
  364.4 44.8 %collective-permute-start.19 = (bf16[128,2048]{1,0:T(8,128)(2,1)S(1)}, bf16[128,2048]{1,0:T(8,128)(2,1)S(1)}, u32[]{:S(2)}, u32[]{:S(2)}) collective-permute-start(bf16[128,2048]{1,0:T(8,128)(2,1)S(1)} %get-tuple-element.127), channel_id=1, source_target_pairs={{0,4},{2,6},{4,0},{6,2},{1,5},{3,7},{5,1},{7,3},{8,12},{10,14},{12... | collective-permute-start | bytes 1572872 | tf_op jit(solution)/shard_map/ppermute | solution.py:54
  364.4 44.8 %collective-permute-start.17 = (bf16[128,2048]{1,0:T(8,128)(2,1)S(1)}, bf16[128,2048]{1,0:T(8,128)(2,1)S(1)}, u32[]{:S(2)}, u32[]{:S(2)}) collective-permute-start(bf16[128,2048]{1,0:T(8,128)(2,1)S(1)} %get-tuple-element.128), channel_id=1, source_target_pairs={{0,2},{2,4},{4,6},{6,0},{1,3},{3,5},{5,7},{7,1},{8,10},{10,12},{12... | collective-permute-start | bytes 1572872 | tf_op jit(solution)/shard_map/ppermute | solution.py:54
  376.8 48.8 %collective-permute-start.49 = (bf16[512,2048]{1,0:T(8,128)(2,1)}, bf16[512,2048]{1,0:T(8,128)(2,1)S(1)}, u32[]{:S(2)}, u32[]{:S(2)}) collective-permute-start(bf16[512,2048]{1,0:T(8,128)(2,1)} %pad_maximum_fusion.5), channel_id=1, source_target_pairs={{0,1},{1,0},{2,3},{3,2},{4,5},{5,4},{6,7},{7,6},{8,9},{9,8},{10,11... | collective-permute-start | bytes 6291464 | tf_op jit(solution)/shard_map/ppermute | solution.py:40
  417.1 45.6 %collective-permute-start.52 = (bf16[256,2048]{1,0:T(8,128)(2,1)}, bf16[256,2048]{1,0:T(8,128)(2,1)}, u32[]{:S(2)}, u32[]{:S(2)}) collective-permute-start(bf16[256,2048]{1,0:T(8,128)(2,1)} %slice.776), channel_id=1, source_target_pairs={{0,1},{1,0},{2,3},{3,2},{4,5},{5,4},{6,7},{7,6},{8,9},{9,8},{10,11... | collective-permute-start | bytes 3145736 | tf_op jit(solution)/shard_map/ppermute | solution.py:40
  426.8 37.1 %collective-permute-start.51 = (bf16[256,2048]{1,0:T(8,128)(2,1)}, bf16[256,2048]{1,0:T(8,128)(2,1)}, u32[]{:S(2)}, u32[]{:S(2)}) collective-permute-start(bf16[256,2048]{1,0:T(8,128)(2,1)} %slice.775), channel_id=1, source_target_pairs={{0,16},{8,24},{16,0},{24,8},{1,17},{9,25},{17,1},{25,9},{2,18},{10... | collective-permute-start | bytes 3145736 | tf_op jit(solution)/shard_map/ppermute | solution.py:48
  452.6 60.2 %collective-permute-start.55 = (bf16[512,2048]{1,0:T(8,128)(2,1)}, bf16[512,2048]{1,0:T(8,128)(2,1)S(1)}, u32[]{:S(2)}, u32[]{:S(2)}) collective-permute-start(bf16[512,2048]{1,0:T(8,128)(2,1)} %copy-done.21), channel_id=1, source_target_pairs={{0,8},{8,0},{16,24},{24,16},{1,9},{9,1},{17,25},{25,17},{2,10},{10... | collective-permute-start | bytes 6291464 | tf_op jit(solution)/shard_map/ppermute | solution.py:44
  462.7 48.1 %collective-permute-start.26 = (bf16[512,2048]{1,0:T(8,128)(2,1)S(1)}, bf16[512,2048]{1,0:T(8,128)(2,1)S(1)}, u32[]{:S(2)}, u32[]{:S(2)}) collective-permute-start(bf16[512,2048]{1,0:T(8,128)(2,1)S(1)} %pad_maximum_fusion.2), channel_id=1, source_target_pairs={{0,16},{8,24},{16,0},{24,8},{1,17},{9,25},{17,1},{25,9},{2,18},{10... | collective-permute-start | bytes 6291464 | tf_op jit(solution)/shard_map/ppermute | solution.py:48
  463.8 48.0 %collective-permute-start.25 = (bf16[512,2048]{1,0:T(8,128)(2,1)S(1)}, bf16[512,2048]{1,0:T(8,128)(2,1)S(1)}, u32[]{:S(2)}, u32[]{:S(2)}) collective-permute-start(bf16[512,2048]{1,0:T(8,128)(2,1)S(1)} %pad_maximum_fusion.2), channel_id=1, source_target_pairs={{0,1},{1,0},{2,3},{3,2},{4,5},{5,4},{6,7},{7,6},{8,9},{9,8},{10,11... | collective-permute-start | bytes 6291464 | tf_op jit(solution)/shard_map/ppermute | solution.py:40
  465.9 48.5 %collective-permute-start.56 = (bf16[512,2048]{1,0:T(8,128)(2,1)S(1)}, bf16[512,2048]{1,0:T(8,128)(2,1)S(1)}, u32[]{:S(2)}, u32[]{:S(2)}) collective-permute-start(bf16[512,2048]{1,0:T(8,128)(2,1)S(1)} %pad_maximum_fusion.6), channel_id=1, source_target_pairs={{0,8},{8,0},{16,24},{24,16},{1,9},{9,1},{17,25},{25,17},{2,10},{10... | collective-permute-start | bytes 6291464 | tf_op jit(solution)/shard_map/ppermute | solution.py:44
  656.1 110.6 %collective-permute-start.33 = (bf16[512,2048]{1,0:T(8,128)(2,1)}, bf16[512,2048]{1,0:T(8,128)(2,1)}, u32[]{:S(2)}, u32[]{:S(2)}) collective-permute-start(bf16[512,2048]{1,0:T(8,128)(2,1)} %get-tuple-element.111), channel_id=1, source_target_pairs={{0,8},{8,0},{16,24},{24,16},{1,9},{9,1},{17,25},{25,17},{2,10},{10... | collective-permute-start | bytes 6291464 | tf_op jit(solution)/shard_map/ppermute | solution.py:44
  675.3 91.5 %collective-permute-start.37 = (bf16[512,2048]{1,0:T(8,128)(2,1)}, bf16[512,2048]{1,0:T(8,128)(2,1)S(1)}, u32[]{:S(2)}, u32[]{:S(2)}) collective-permute-start(bf16[512,2048]{1,0:T(8,128)(2,1)} %get-tuple-element.112), channel_id=1, source_target_pairs={{0,8},{8,0},{16,24},{24,16},{1,9},{9,1},{17,25},{25,17},{2,10},{10... | collective-permute-start | bytes 6291464 | tf_op jit(solution)/shard_map/ppermute | solution.py:44
  675.3 91.9 %collective-permute-start.36 = (bf16[512,2048]{1,0:T(8,128)(2,1)}, bf16[512,2048]{1,0:T(8,128)(2,1)}, u32[]{:S(2)}, u32[]{:S(2)}) collective-permute-start(bf16[512,2048]{1,0:T(8,128)(2,1)} %get-tuple-element.113), channel_id=1, source_target_pairs={{0,8},{8,0},{16,24},{24,16},{1,9},{9,1},{17,25},{25,17},{2,10},{10... | collective-permute-start | bytes 6291464 | tf_op jit(solution)/shard_map/ppermute | solution.py:44
  675.8 110.8 %collective-permute-start.34 = (bf16[512,2048]{1,0:T(8,128)(2,1)}, bf16[512,2048]{1,0:T(8,128)(2,1)}, u32[]{:S(2)}, u32[]{:S(2)}) collective-permute-start(bf16[512,2048]{1,0:T(8,128)(2,1)} %get-tuple-element.114), channel_id=1, source_target_pairs={{0,8},{8,0},{16,24},{24,16},{1,9},{9,1},{17,25},{25,17},{2,10},{10... | collective-permute-start | bytes 6291464 | tf_op jit(solution)/shard_map/ppermute | solution.py:44
  791.6 75.8 %collective-permute-start.35 = (bf16[256,2048]{1,0:T(8,128)(2,1)S(1)}, bf16[256,2048]{1,0:T(8,128)(2,1)S(1)}, u32[]{:S(2)}, u32[]{:S(2)}) collective-permute-start(bf16[256,2048]{1,0:T(8,128)(2,1)S(1)} %slice.756), channel_id=1, source_target_pairs={{0,1},{1,0},{2,3},{3,2},{4,5},{5,4},{6,7},{7,6},{8,9},{9,8},{10,11... | collective-permute-start | bytes 3145736 | tf_op jit(solution)/shard_map/ppermute | solution.py:40
  792.7 76.0 %collective-permute-start.43 = (bf16[256,2048]{1,0:T(8,128)(2,1)S(1)}, bf16[256,2048]{1,0:T(8,128)(2,1)}, u32[]{:S(2)}, u32[]{:S(2)}) collective-permute-start(bf16[256,2048]{1,0:T(8,128)(2,1)S(1)} %slice.768), channel_id=1, source_target_pairs={{0,16},{8,24},{16,0},{24,8},{1,17},{9,25},{17,1},{25,9},{2,18},{10... | collective-permute-start | bytes 3145736 | tf_op jit(solution)/shard_map/ppermute | solution.py:48
  794.0 46.2 %collective-permute-start.38 = (bf16[256,2048]{1,0:T(8,128)(2,1)S(1)}, bf16[256,2048]{1,0:T(8,128)(2,1)S(1)}, u32[]{:S(2)}, u32[]{:S(2)}) collective-permute-start(bf16[256,2048]{1,0:T(8,128)(2,1)S(1)} %get-tuple-element.151), channel_id=1, source_target_pairs={{0,1},{1,0},{2,3},{3,2},{4,5},{5,4},{6,7},{7,6},{8,9},{9,8},{10,11... | collective-permute-start | bytes 3145736 | tf_op jit(solution)/shard_map/ppermute | solution.py:40
  794.8 46.5 %collective-permute-start.41 = (bf16[256,2048]{1,0:T(8,128)(2,1)S(1)}, bf16[256,2048]{1,0:T(8,128)(2,1)S(1)}, u32[]{:S(2)}, u32[]{:S(2)}) collective-permute-start(bf16[256,2048]{1,0:T(8,128)(2,1)S(1)} %get-tuple-element.152), channel_id=1, source_target_pairs={{0,16},{8,24},{16,0},{24,8},{1,17},{9,25},{17,1},{25,9},{2,18},{10... | collective-permute-start | bytes 3145736 | tf_op jit(solution)/shard_map/ppermute | solution.py:48
  804.7 57.9 %collective-permute-start.73 = (bf16[256,2048]{1,0:T(8,128)(2,1)S(1)}, bf16[256,2048]{1,0:T(8,128)(2,1)S(1)}, u32[]{:S(2)}, u32[]{:S(2)}) collective-permute-start(bf16[256,2048]{1,0:T(8,128)(2,1)S(1)} %get-tuple-element.142), channel_id=1, source_target_pairs={{0,1},{1,0},{2,3},{3,2},{4,5},{5,4},{6,7},{7,6},{8,9},{9,8},{10,11... | collective-permute-start | bytes 3145736 | tf_op jit(solution)/shard_map/ppermute | solution.py:40
  841.3 47.3 %collective-permute-start.39 = (bf16[256,2048]{1,0:T(8,128)(2,1)S(1)}, bf16[256,2048]{1,0:T(8,128)(2,1)S(1)}, u32[]{:S(2)}, u32[]{:S(2)}) collective-permute-start(bf16[256,2048]{1,0:T(8,128)(2,1)S(1)} %add_convert_fusion.23), channel_id=1, source_target_pairs={{0,16},{8,24},{16,0},{24,8},{1,17},{9,25},{17,1},{25,9},{2,18},{10... | collective-permute-start | bytes 3145736 | tf_op jit(solution)/shard_map/ppermute | solution.py:48
  866.2 44.9 %collective-permute-start.70 = (bf16[256,2048]{1,0:T(8,128)(2,1)S(1)}, bf16[256,2048]{1,0:T(8,128)(2,1)S(1)}, u32[]{:S(2)}, u32[]{:S(2)}) collective-permute-start(bf16[256,2048]{1,0:T(8,128)(2,1)S(1)} %slice.782), channel_id=1, source_target_pairs={{0,1},{1,0},{2,3},{3,2},{4,5},{5,4},{6,7},{7,6},{8,9},{9,8},{10,11... | collective-permute-start | bytes 3145736 | tf_op jit(solution)/shard_map/ppermute | solution.py:40
  867.4 44.5 %collective-permute-start.78 = (bf16[256,2048]{1,0:T(8,128)(2,1)S(1)}, bf16[256,2048]{1,0:T(8,128)(2,1)S(1)}, u32[]{:S(2)}, u32[]{:S(2)}) collective-permute-start(bf16[256,2048]{1,0:T(8,128)(2,1)S(1)} %slice.794), channel_id=1, source_target_pairs={{0,16},{8,24},{16,0},{24,8},{1,17},{9,25},{17,1},{25,9},{2,18},{10... | collective-permute-start | bytes 3145736 | tf_op jit(solution)/shard_map/ppermute | solution.py:48
  868.7 64.1 %collective-permute-start.74 = (bf16[256,2048]{1,0:T(8,128)(2,1)S(1)}, bf16[256,2048]{1,0:T(8,128)(2,1)S(1)}, u32[]{:S(2)}, u32[]{:S(2)}) collective-permute-start(bf16[256,2048]{1,0:T(8,128)(2,1)S(1)} %add_convert_fusion.19), channel_id=1, source_target_pairs={{0,16},{8,24},{16,0},{24,8},{1,17},{9,25},{17,1},{25,9},{2,18},{10... | collective-permute-start | bytes 3145736 | tf_op jit(solution)/shard_map/ppermute | solution.py:48
  888.7 44.1 %collective-permute-start.77 = (bf16[256,2048]{1,0:T(8,128)(2,1)S(1)}, bf16[256,2048]{1,0:T(8,128)(2,1)S(1)}, u32[]{:S(2)}, u32[]{:S(2)}) collective-permute-start(bf16[256,2048]{1,0:T(8,128)(2,1)S(1)} %add_convert_fusion.17), channel_id=1, source_target_pairs={{0,1},{1,0},{2,3},{3,2},{4,5},{5,4},{6,7},{7,6},{8,9},{9,8},{10,11... | collective-permute-start | bytes 3145736 | tf_op jit(solution)/shard_map/ppermute | solution.py:40
  891.9 44.8 %collective-permute-start.40 = (bf16[128,2048]{1,0:T(8,128)(2,1)S(1)}, bf16[128,2048]{1,0:T(8,128)(2,1)S(1)}, u32[]{:S(2)}, u32[]{:S(2)}) collective-permute-start(bf16[128,2048]{1,0:T(8,128)(2,1)S(1)} %get-tuple-element.173), channel_id=1, source_target_pairs={{0,2},{2,4},{4,6},{6,0},{1,3},{3,5},{5,7},{7,1},{8,10},{10,12},{12... | collective-permute-start | bytes 1572872 | tf_op jit(solution)/shard_map/ppermute | solution.py:54
  911.1 44.6 %collective-permute-start.44 = (bf16[128,2048]{1,0:T(8,128)(2,1)S(1)}, bf16[128,2048]{1,0:T(8,128)(2,1)S(1)}, u32[]{:S(2)}, u32[]{:S(2)}) collective-permute-start(bf16[128,2048]{1,0:T(8,128)(2,1)S(1)} %get-tuple-element.174), channel_id=1, source_target_pairs={{0,4},{2,6},{4,0},{6,2},{1,5},{3,7},{5,1},{7,3},{8,12},{10,14},{12... | collective-permute-start | bytes 1572872 | tf_op jit(solution)/shard_map/ppermute | solution.py:54
  911.9 43.9 %collective-permute-start.45 = (bf16[128,2048]{1,0:T(8,128)(2,1)S(1)}, bf16[128,2048]{1,0:T(8,128)(2,1)S(1)}, u32[]{:S(2)}, u32[]{:S(2)}) collective-permute-start(bf16[128,2048]{1,0:T(8,128)(2,1)S(1)} %get-tuple-element.175), channel_id=1, source_target_pairs={{0,6},{2,0},{4,2},{6,4},{1,7},{3,1},{5,3},{7,5},{8,14},{10,8},{12,... | collective-permute-start | bytes 1572872 | tf_op jit(solution)/shard_map/ppermute | solution.py:54
  934.3 45.7 %collective-permute-start.79 = (bf16[128,2048]{1,0:T(8,128)(2,1)S(1)}, bf16[128,2048]{1,0:T(8,128)(2,1)S(1)}, u32[]{:S(2)}, u32[]{:S(2)}) collective-permute-start(bf16[128,2048]{1,0:T(8,128)(2,1)S(1)} %get-tuple-element.170), channel_id=1, source_target_pairs={{0,4},{2,6},{4,0},{6,2},{1,5},{3,7},{5,1},{7,3},{8,12},{10,14},{12... | collective-permute-start | bytes 1572872 | tf_op jit(solution)/shard_map/ppermute | solution.py:54
  936.7 43.3 %collective-permute-start.80 = (bf16[128,2048]{1,0:T(8,128)(2,1)S(1)}, bf16[128,2048]{1,0:T(8,128)(2,1)S(1)}, u32[]{:S(2)}, u32[]{:S(2)}) collective-permute-start(bf16[128,2048]{1,0:T(8,128)(2,1)S(1)} %get-tuple-element.171), channel_id=1, source_target_pairs={{0,6},{2,0},{4,2},{6,4},{1,7},{3,1},{5,3},{7,5},{8,14},{10,8},{12,... | collective-permute-start | bytes 1572872 | tf_op jit(solution)/shard_map/ppermute | solution.py:54
  987.0 50.3 %collective-permute-start.97 = (bf16[128,2048]{1,0:T(8,128)(2,1)S(1)}, bf16[128,2048]{1,0:T(8,128)(2,1)S(1)}, u32[]{:S(2)}, u32[]{:S(2)}) collective-permute-start(bf16[128,2048]{1,0:T(8,128)(2,1)S(1)} %get-tuple-element.135), channel_id=1, source_target_pairs={{0,1},{1,0},{2,3},{3,2},{4,5},{5,4},{6,7},{7,6},{8,9},{9,8},{10,11... | collective-permute-start | bytes 1572872 | tf_op jit(solution)/shard_map/ppermute | solution.py:40
  999.1 36.1 %collective-permute-start.95 = (bf16[128,2048]{1,0:T(8,128)(2,1)S(1)}, bf16[128,2048]{1,0:T(8,128)(2,1)S(1)}, u32[]{:S(2)}, u32[]{:S(2)}) collective-permute-start(bf16[128,2048]{1,0:T(8,128)(2,1)S(1)} %get-tuple-element.138), channel_id=1, source_target_pairs={{0,4},{2,6},{4,0},{6,2},{1,5},{3,7},{5,1},{7,3},{8,12},{10,14},{12... | collective-permute-start | bytes 1572872 | tf_op jit(solution)/shard_map/ppermute | solution.py:54
  1001.3 35.6 %collective-permute-start.94 = (bf16[128,2048]{1,0:T(8,128)(2,1)S(1)}, bf16[128,2048]{1,0:T(8,128)(2,1)S(1)}, u32[]{:S(2)}, u32[]{:S(2)}) collective-permute-start(bf16[128,2048]{1,0:T(8,128)(2,1)S(1)} %get-tuple-element.139), channel_id=1, source_target_pairs={{0,6},{2,0},{4,2},{6,4},{1,7},{3,1},{5,3},{7,5},{8,14},{10,8},{12,... | collective-permute-start | bytes 1572872 | tf_op jit(solution)/shard_map/ppermute | solution.py:54
  1013.6 46.7 %collective-permute-start.100 = (bf16[128,2048]{1,0:T(8,128)(2,1)S(1)}, bf16[128,2048]{1,0:T(8,128)(2,1)S(1)}, u32[]{:S(2)}, u32[]{:S(2)}) collective-permute-start(bf16[128,2048]{1,0:T(8,128)(2,1)S(1)} %collective-permute-done.96), channel_id=1, source_target_pairs={{0,1},{1,0},{2,3},{3,2},{4,5},{5,4},{6,7},{7,6},{8,9},{9,8},{10,11... | collective-permute-start | bytes 1572872 | tf_op jit(solution)/shard_map/ppermute | solution.py:40
  1174.4 47.1 %collective-permute-start.106 = (bf16[256,2048]{1,0:T(8,128)(2,1)}, bf16[256,2048]{1,0:T(8,128)(2,1)}, u32[]{:S(2)}, u32[]{:S(2)}) collective-permute-start(bf16[256,2048]{1,0:T(8,128)(2,1)} %get-tuple-element.120), channel_id=1, source_target_pairs={{0,1},{1,0},{2,3},{3,2},{4,5},{5,4},{6,7},{7,6},{8,9},{9,8},{10,11... | collective-permute-start | bytes 3145736 | tf_op jit(solution)/shard_map/ppermute | solution.py:40
  1174.8 69.2 %collective-permute-start.103 = (bf16[256,2048]{1,0:T(8,128)(2,1)}, bf16[256,2048]{1,0:T(8,128)(2,1)}, u32[]{:S(2)}, u32[]{:S(2)}) collective-permute-start(bf16[256,2048]{1,0:T(8,128)(2,1)} %get-tuple-element.121), channel_id=1, source_target_pairs={{0,1},{1,0},{2,3},{3,2},{4,5},{5,4},{6,7},{7,6},{8,9},{9,8},{10,11... | collective-permute-start | bytes 3145736 | tf_op jit(solution)/shard_map/ppermute | solution.py:40
  1176.4 89.6 %collective-permute-start.102 = (bf16[256,2048]{1,0:T(8,128)(2,1)}, bf16[256,2048]{1,0:T(8,128)(2,1)}, u32[]{:S(2)}, u32[]{:S(2)}) collective-permute-start(bf16[256,2048]{1,0:T(8,128)(2,1)} %get-tuple-element.122), channel_id=1, source_target_pairs={{0,1},{1,0},{2,3},{3,2},{4,5},{5,4},{6,7},{7,6},{8,9},{9,8},{10,11... | collective-permute-start | bytes 3145736 | tf_op jit(solution)/shard_map/ppermute | solution.py:40
  1197.7 125.2 %collective-permute-start.116 = (bf16[256,2048]{1,0:T(8,128)(2,1)}, bf16[256,2048]{1,0:T(8,128)(2,1)}, u32[]{:S(2)}, u32[]{:S(2)}) collective-permute-start(bf16[256,2048]{1,0:T(8,128)(2,1)} %convolution_convert_fusion.10), channel_id=1, source_target_pairs={{0,8},{8,0},{16,24},{24,16},{1,9},{9,1},{17,25},{25,17},{2,10},{10... | collective-permute-start | bytes 3145736 | tf_op jit(solution)/shard_map/ppermute | solution.py:44
  1200.5 109.5 %collective-permute-start.111 = (bf16[512,3072]{1,0:T(8,128)(2,1)}, bf16[512,3072]{1,0:T(8,128)(2,1)}, u32[]{:S(2)}, u32[]{:S(2)}) collective-permute-start(bf16[512,3072]{1,0:T(8,128)(2,1)} %convolution_convert_fusion.4), channel_id=1, source_target_pairs={{0,8},{8,0},{16,24},{24,16},{1,9},{9,1},{17,25},{25,17},{2,10},{10... | collective-permute-start | bytes 9437192 | tf_op jit(solution)/shard_map/ppermute | solution.py:44
  1221.5 88.5 %collective-permute-start.113 = (bf16[512,3072]{1,0:T(8,128)(2,1)}, bf16[512,3072]{1,0:T(8,128)(2,1)}, u32[]{:S(2)}, u32[]{:S(2)}) collective-permute-start(bf16[512,3072]{1,0:T(8,128)(2,1)} %add_convert_fusion.2), channel_id=1, source_target_pairs={{0,16},{8,24},{16,0},{24,8},{1,17},{9,25},{17,1},{25,9},{2,18},{10... | collective-permute-start | bytes 9437192 | tf_op jit(solution)/shard_map/ppermute | solution.py:48
  1295.3 34.1 %collective-permute-start.108 = (bf16[128,2048]{1,0:T(8,128)(2,1)}, bf16[128,2048]{1,0:T(8,128)(2,1)}, u32[]{:S(2)}, u32[]{:S(2)}) collective-permute-start(bf16[128,2048]{1,0:T(8,128)(2,1)} %slice.822), channel_id=1, source_target_pairs={{0,2},{2,4},{4,6},{6,0},{1,3},{3,5},{5,7},{7,1},{8,10},{10,12},{12... | collective-permute-start | bytes 1572872 | tf_op jit(solution)/shard_map/ppermute | solution.py:146
  1309.9 33.8 %collective-permute-start.105 = (bf16[128,2048]{1,0:T(8,128)(2,1)}, bf16[128,2048]{1,0:T(8,128)(2,1)}, u32[]{:S(2)}, u32[]{:S(2)}) collective-permute-start(bf16[128,2048]{1,0:T(8,128)(2,1)} %add_convert_fusion.27), channel_id=1, source_target_pairs={{0,2},{2,4},{4,6},{6,0},{1,3},{3,5},{5,7},{7,1},{8,10},{10,12},{12... | collective-permute-start | bytes 1572872 | tf_op jit(solution)/shard_map/ppermute | solution.py:145
  1310.0 40.6 %collective-permute-start.110 = (bf16[128,2048]{1,0:T(8,128)(2,1)}, bf16[128,2048]{1,0:T(8,128)(2,1)}, u32[]{:S(2)}, u32[]{:S(2)}) collective-permute-start(bf16[128,2048]{1,0:T(8,128)(2,1)} %add_convert_fusion.25), channel_id=1, source_target_pairs={{0,6},{2,0},{4,2},{6,4},{1,7},{3,1},{5,3},{7,5},{8,14},{10,8},{12,... | collective-permute-start | bytes 1572872 | tf_op jit(solution)/shard_map/ppermute | solution.py:147
  1322.9 38.5 %collective-permute-start.114 = (bf16[256,3072]{0,1:T(8,128)(2,1)}, bf16[256,3072]{0,1:T(8,128)(2,1)}, u32[]{:S(2)}, u32[]{:S(2)}) collective-permute-start(bf16[256,3072]{0,1:T(8,128)(2,1)} %bitcast.292), channel_id=1, source_target_pairs={{0,1},{1,0},{2,3},{3,2},{4,5},{5,4},{6,7},{7,6},{8,9},{9,8},{10,11... | collective-permute-start | bytes 4718600 | tf_op jit(solution)/shard_map/ppermute | solution.py:40
  1329.3 41.3 %collective-permute-start.115 = (bf16[256,2048]{1,0:T(8,128)(2,1)}, bf16[256,2048]{1,0:T(8,128)(2,1)}, u32[]{:S(2)}, u32[]{:S(2)}) collective-permute-start(bf16[256,2048]{1,0:T(8,128)(2,1)} %convolution_convert_fusion.12), channel_id=1, source_target_pairs={{0,8},{8,0},{16,24},{24,16},{1,9},{9,1},{17,25},{25,17},{2,10},{10... | collective-permute-start | bytes 3145736 | tf_op jit(solution)/shard_map/ppermute | solution.py:44
  1332.5 38.1 %collective-permute-start.117 = (bf16[256,2048]{1,0:T(8,128)(2,1)}, bf16[256,2048]{1,0:T(8,128)(2,1)}, u32[]{:S(2)}, u32[]{:S(2)}) collective-permute-start(bf16[256,2048]{1,0:T(8,128)(2,1)} %fusion.34), channel_id=1, source_target_pairs={{0,16},{8,24},{16,0},{24,8},{1,17},{9,25},{17,1},{25,9},{2,18},{10... | collective-permute-start | bytes 3145736 | tf_op jit(solution)/shard_map/ppermute | solution.py:48
  1356.2 209.6 %all-reduce.5.cloned.1.call-start = ((), (), s32[]{:S(2)}) async-start(), calls=%async_computation.1 | async-start | bytes 4194304 | tf_op jit(solution)/shard_map/psum | solution.py:659
  (169 other events, 6027.4 us)
Sparse Core Ops, SparseCore 0:
  1356.3 120.9 all-reduce.2
  1480.3 85.5 all-reduce.4

commit v2 on v1

v2 whole, which is shorter than its diff:
```python
import functools

import jax
import jax.numpy as jnp
from jax import lax
from jax.experimental import pallas as pl
from jax.experimental.pallas import tpu as pltpu
from jax.sharding import PartitionSpec as P

HEAD = 128
EPS = 1e-06
NEG = -1e30
HIGH = lax.Precision.HIGHEST
BF = jnp.bfloat16
F32 = jnp.float32
LOG2E = 1.4426950408889634


def dot(left, right):
    return jnp.dot(left, right, preferred_element_type=F32)


def dot_t(left, right):
    return lax.dot_general(left, right, (((1,), (1,)), ((), ())), preferred_element_type=F32)


def t_dot(left, right):
    return lax.dot_general(left, right, (((0,), (0,)), ((), ())), preferred_element_type=F32)


def after(value, *others):
    return lax.optimization_barrier((value, others))[0]


def ring(count, shift):
    return [(j, (j + shift) % count) for j in range(count)]


def flip(count, bit):
    return [(j, j ^ bit) for j in range(count)]


def swap_x(value):
    return lax.ppermute(value, "seq", flip(2, 1))


def swap_core(value):
    return lax.ppermute(value, "dp", flip(lax.axis_size("dp"), 1))


def swap_y(value):
    return lax.ppermute(value, "dp", flip(4, 2))


def z_rounds(pieces, sign):
    count = lax.axis_size("expert")
    return [pieces[0]] + [
        lax.ppermute(pieces[r], "expert", ring(count, sign * r)) for r in range(1, count)
    ]


def is_small():
    return lax.axis_size("dp") == 4 and lax.axis_size("expert") == 4


def add_low(*terms):
    total = terms[0].astype(F32)
    for term in terms[1:]:
        total = total + term.astype(F32)
    return total.astype(terms[0].dtype)


def square_gather(piece):
    return lax.all_gather(piece, ("dp", "seq"), axis=0, tiled=True)


def square_scatter(parts):
    return lax.psum_scatter(parts, ("dp", "seq"), scatter_dimension=0, tiled=True)


def group_gather(block):
    count = lax.axis_size("expert")
    if is_small():
        half = block.shape[0] // 2
        up = lax.ppermute(block, "expert", ring(count, -1))
        down = lax.ppermute(block, "expert", ring(count, 1))
        far = jnp.concatenate(
            [
                lax.ppermute(down[:half], "expert", ring(count, 1)),
                lax.ppermute(up[half:], "expert", ring(count, -1)),
            ],
            axis=0,
        )
        own = [block, up, far, down]
        return own + [swap_x(piece) for piece in own]
    e_at, s_at = lax.axis_index("expert"), lax.axis_index("seq")
    every = lax.all_gather(block, ("expert", "seq"), axis=0, tiled=False)
    wanted = [
        (lax.rem(e_at + r, count)) * 2 + lax.rem(s_at + sp, 2)
        for sp in range(2)
        for r in range(count)
    ]
    return [lax.dynamic_index_in_dim(every, at, 0, keepdims=False) for at in wanted]


def group_scatter(own, other):
    count = lax.axis_size("expert")
    if not is_small():
        e_at, s_at = lax.axis_index("expert"), lax.axis_index("seq")
        stacked = jnp.stack(list(own) + list(other))
        spots_of = [
            (lax.rem(s_at + b % 2, 2)) * count + lax.rem(b // 2 - e_at + count, count)
            for b in range(2 * count)
        ]
        ordered = jnp.stack(
            [lax.dynamic_index_in_dim(stacked, at, 0, keepdims=False) for at in spots_of]
        )
        total = lax.psum_scatter(ordered, ("expert", "seq"), scatter_dimension=0, tiled=False)
        return total.astype(F32), []
    half = own[0].shape[0] // 2
    halves = (slice(0, half), slice(half, 2 * half))
    far_took = swap_x(other[2])
    near_took = [swap_x(after(other[1], far_took)), swap_x(after(other[3], far_took))]
    own_took = swap_x(after(other[0], *near_took))
    far = [add_low(own[2][rows], far_took[rows]) for rows in halves]
    far_up = lax.ppermute(far[0], "expert", ring(count, 1))
    far_down = lax.ppermute(far[1], "expert", ring(count, -1))
    up = jnp.concatenate(
        [
            add_low(own[1][halves[0]], near_took[0][halves[0]], far_up),
            add_low(own[1][halves[1]], near_took[0][halves[1]]),
        ],
        axis=0,
    )
    down = jnp.concatenate(
        [
            add_low(own[3][halves[0]], near_took[1][halves[0]]),
            add_low(own[3][halves[1]], near_took[1][halves[1]], far_down),
        ],
        axis=0,
    )
    from_below = lax.ppermute(up, "expert", ring(count, 1))
    from_above = lax.ppermute(down, "expert", ring(count, -1))
    return add_low(own[0].astype(F32), own_took, from_below, from_above), [up, down]


def dp_first(parts):
    at = lax.axis_index("dp")
    core, row = at % 2, at // 2
    split = parts.reshape((2, 2) + parts.shape[1:])
    took = swap_core(lax.dynamic_index_in_dim(split, 1 - core, 1, keepdims=False))

    def of(y):
        mine = lax.dynamic_index_in_dim(split, y, 0, keepdims=False)
        mine = lax.dynamic_index_in_dim(mine, core, 0, keepdims=False)
        return add_low(mine, lax.dynamic_index_in_dim(took, y, 0, keepdims=False))

    return of(row), of(1 - row)


def tiny_scatter(value):
    if lax.axis_size("dp") != 4:
        shape = value.shape[2:]
        flat = lax.psum(value.reshape((-1,) + shape), ("dp", "seq"))
        at = lax.axis_index("dp") * 2 + lax.axis_index("seq")
        return lax.dynamic_index_in_dim(flat, at, 0, keepdims=False)
    at, s_at = lax.axis_index("dp"), lax.axis_index("seq")

    def fold(array, bit, axis, swap):
        mine = lax.dynamic_index_in_dim(array, bit, axis, keepdims=False)
        return mine + swap(lax.dynamic_index_in_dim(array, 1 - bit, axis, keepdims=False))

    value = fold(value, s_at, 1, swap_x)
    value = fold(value.reshape((2, 2) + value.shape[1:]), at % 2, 1, swap_core)
    return fold(value, at // 2, 0, swap_y)


def little_sum(value):
    rows, features = value.shape
    d_count, e_count = lax.axis_size("dp"), lax.axis_size("expert")
    own = features // (2 * d_count)
    held = tiny_scatter(value.reshape(rows, d_count, 2, own).transpose(1, 2, 0, 3))
    if e_count != 4:
        return lax.psum(held, "expert")
    held = held + lax.ppermute(held, "expert", flip(e_count, 1))
    return held + lax.ppermute(held, "expert", flip(e_count, 2))


def route_pairs(routes, order, is_valid, capacity):
    tokens_here, top_count = routes.shape
    pairs = tokens_here * top_count
    target = routes.reshape(pairs)
    second = lax.broadcasted_iota(jnp.int32, routes.shape, 1)
    priority = (order[:, None] * top_count + second).reshape(pairs)
    living = jnp.broadcast_to(is_valid[:, None], routes.shape).reshape(pairs)
    earlier = (
        (target[:, None] == target[None, :])
        & (priority[None, :] < priority[:, None])
        & living[None, :]
    )
    slot_index = jnp.sum(earlier.astype(jnp.int32), axis=1, dtype=jnp.int32)
    kept_pair = living & (slot_index < capacity)
    return (kept_pair.reshape(routes.shape), slot_index.reshape(routes.shape))


def spots(routes, kept, slot_index, experts, capacity):
    away = lax.rem(lax.axis_index("expert") - routes + experts, experts)
    part = capacity // 2
    place = (slot_index // part) * (experts * part) + away * part + slot_index % part
    flat = jnp.where(kept, place, -1)
    return flat


def hots(flat, experts, capacity):
    slots = lax.broadcasted_iota(jnp.int32, (1, experts * capacity), 1)
    return [flat[:, k : k + 1] == slots for k in range(flat.shape[1])]


def weigh(hot, weight):
    return sum(jnp.where(hot[k], weight[:, k : k + 1], 0.0) for k in range(len(hot)))


def in_two(value):
    high = lax.reduce_precision(value, 8, 7)
    return high.astype(BF), (value - high).astype(BF)


def in_columns(value):
    first = lax.reduce_precision(value, 8, 7)
    second = lax.reduce_precision(value - first, 8, 7)
    third = value - first - second
    columns = jnp.concatenate([first, second, third], axis=1).astype(BF)
    return jnp.pad(columns, ((0, 0), (0, 125)))


def rms_norm(values, gain):
    return values * lax.rsqrt(jnp.mean(values * values, axis=-1, keepdims=True) + EPS) * gain


def norm_back(values, gain, grad):
    factor = lax.rsqrt(jnp.mean(values * values, axis=1, keepdims=True) + EPS)
    unit = values * factor
    gain_grad = jnp.sum(grad * unit, axis=0)
    scaled = grad * gain
    return (factor * (scaled - unit * jnp.mean(scaled * unit, axis=1, keepdims=True)), gain_grad)


def gate_values(normed, router, routes):
    logits = dot(normed, router)
    experts = lax.broadcasted_iota(jnp.int32, logits.shape, 1)
    chosen = jnp.concatenate(
        [
            jnp.sum(jnp.where(routes[:, k : k + 1] == experts, logits, 0.0), axis=1, keepdims=True)
            for k in range(routes.shape[1])
        ],
        axis=1,
    )
    top = jnp.max(chosen, axis=1, keepdims=True)
    expo = jnp.exp(chosen - top)
    return expo / jnp.sum(expo, axis=1, keepdims=True)


def gate_grads(normed, router, routes, gates, gate_grad):
    chosen = gates * (gate_grad - jnp.sum(gates * gate_grad, axis=1, keepdims=True))
    experts = lax.broadcasted_iota(jnp.int32, (1, 1, router.shape[1]), 2)
    logit_grad = jnp.sum(jnp.where(routes[:, :, None] == experts, chosen[:, :, None], 0.0), axis=1)
    router_grad = jnp.dot(normed.astype(F32).T, logit_grad, precision=HIGH)
    input_grad = jnp.dot(logit_grad, router.astype(F32).T, precision=HIGH)
    return (router_grad, input_grad)


def tile_bias(info, tile, blocks, tokens):
    stretch = tokens // 2
    row_seq, row_place = info[:, 0:1], info[:, 1:2]
    rows = info.shape[0]
    col = lax.broadcasted_iota(jnp.int32, (rows, tokens), 1)
    same = (col // stretch) == row_seq
    near = jnp.where(same, 0.0, NEG)
    place = lax.rem(col, stretch)
    diagonal = [
        jnp.where(same & (place + (tile * blocks + j) * stretch <= row_place), 0.0, NEG)
        for j in range(blocks)
    ]
    return jnp.concatenate([near] * (tile * blocks) + diagonal, axis=1)


def picked(ref, index, at, count):
    return jnp.concatenate([ref[index[at + j]] for j in range(count)], axis=0)


def attend_kernel(index, info, query, keys, values, mixed, logs, *, blocks):
    head = pl.program_id(0)
    total, capacity, _ = query.shape
    tokens = keys.shape[1]
    rate = HEAD ** (-0.5) * LOG2E
    lane = lax.broadcasted_iota(jnp.int32, (capacity, logs.shape[2]), 1)
    for tile in range(total // blocks):
        first = tile * blocks
        q = picked(query, index, first, blocks)
        k = picked(keys, index, 0, first + blocks)
        v = picked(values, index, 0, first + blocks)
        bias = tile_bias(picked(info, index, first, blocks), tile, blocks, tokens)
        scores = dot_t(q, k) + bias
        top = jnp.max(scores, axis=1, keepdims=True)
        expo = jnp.exp2((scores - top) * rate)
        norm = jnp.sum(expo, axis=1, keepdims=True)
        out = (dot(expo.astype(BF), v) / norm).astype(BF)
        log = top * rate + jnp.log2(norm)
        for j in range(blocks):
            rows = slice(j * capacity, (j + 1) * capacity)
            mixed[index[first + j]] = out[rows]
            held = logs[index[first + j]]
            logs[index[first + j]] = jnp.where(lane == head, log[rows], held)


def attend_back_kernel(
    index, info, query, keys, values, logs, mixed_grad, q_grad, k_grad, v_grad, k_sum, v_sum, *, blocks
):
    head = pl.program_id(0)
    total, capacity, _ = query.shape
    tokens = keys.shape[1]
    scale = HEAD ** (-0.5)
    rate = scale * LOG2E
    k_sum[...] = jnp.zeros_like(k_sum)
    v_sum[...] = jnp.zeros_like(v_sum)
    for tile in range(total // blocks):
        first = tile * blocks
        q = picked(query, index, first, blocks)
        k = picked(keys, index, 0, first + blocks)
        v = picked(values, index, 0, first + blocks)
        g = picked(mixed_grad, index, first, blocks)
        log = picked(logs, index, first, blocks)
        lane = lax.broadcasted_iota(jnp.int32, log.shape, 1)
        log = jnp.sum(jnp.where(lane == head, log, 0.0), axis=1, keepdims=True)
        bias = tile_bias(picked(info, index, first, blocks), tile, blocks, tokens)
        probs = jnp.exp2((dot_t(q, k) + bias) * rate - log)
        prob_grad = dot_t(g, v)
        center = jnp.sum(probs * prob_grad, axis=1, keepdims=True)
        score_grad = (probs * (prob_grad - center)).astype(BF)
        out = (dot(score_grad, k) * scale).astype(BF)
        for j in range(blocks):
            q_grad[index[first + j]] = out[j * capacity : (j + 1) * capacity]
        k_part = t_dot(score_grad, q)
        v_part = t_dot(probs.astype(BF), g)
        for j in range(first + blocks):
            rows = slice(j * tokens, (j + 1) * tokens)
            k_sum[index[j]] += k_part[rows]
            v_sum[index[j]] += v_part[rows]
    k_grad[...] = (k_sum[...] * scale).astype(BF)
    v_grad[...] = v_sum[...].astype(BF)


def head_spec(shape, skip=0):
    return pl.BlockSpec((shape[0], shape[1], HEAD), lambda h, index: (0, 0, h + skip))


def flat_spec(shape):
    return pl.BlockSpec(shape, lambda h, index: (0, 0, 0))


def attend(index, info, query, both):
    total, capacity, width = query.shape
    tokens = both.shape[1]
    heads = width // HEAD
    blocks = max(1, 256 // capacity)
    log_shape = (total, capacity, 128)
    flops = 4 * total * capacity * total * tokens * width
    return pl.pallas_call(
        functools.partial(attend_kernel, blocks=blocks),
        grid_spec=pltpu.PrefetchScalarGridSpec(
            num_scalar_prefetch=1,
            grid=(heads,),
            in_specs=[
                flat_spec(info.shape),
                head_spec(query.shape),
                head_spec(both.shape),
                head_spec(both.shape, heads),
            ],
            out_specs=[head_spec(query.shape), flat_spec(log_shape)],
        ),
        out_shape=[
            jax.ShapeDtypeStruct(query.shape, BF),
            jax.ShapeDtypeStruct(log_shape, F32),
        ],
        compiler_params=pltpu.CompilerParams(vmem_limit_bytes=50 << 20),
        cost_estimate=pl.CostEstimate(
            flops=flops, bytes_accessed=16 << 20, transcendentals=flops // 512
        ),
    )(index, info, query, both, both)


def attend_back(index, info, query, both, logs, mixed_grad):
    total, capacity, width = query.shape
    tokens = both.shape[1]
    heads = width // HEAD
    blocks = max(1, 256 // capacity)
    flops = 10 * total * capacity * total * tokens * width
    return pl.pallas_call(
        functools.partial(attend_back_kernel, blocks=blocks),
        grid_spec=pltpu.PrefetchScalarGridSpec(
            num_scalar_prefetch=1,
            grid=(heads,),
            in_specs=[
                flat_spec(info.shape),
                head_spec(query.shape),
                head_spec(both.shape),
                head_spec(both.shape, heads),
                flat_spec(logs.shape),
                head_spec(mixed_grad.shape),
            ],
            out_specs=[head_spec(query.shape)] + [head_spec((total, tokens, width))] * 2,
            scratch_shapes=[
                pltpu.VMEM((total, tokens, HEAD), F32),
                pltpu.VMEM((total, tokens, HEAD), F32),
            ],
        ),
        out_shape=[
            jax.ShapeDtypeStruct(query.shape, BF),
        ]
        + [jax.ShapeDtypeStruct((total, tokens, width), BF)] * 2,
        compiler_params=pltpu.CompilerParams(vmem_limit_bytes=50 << 20),
        cost_estimate=pl.CostEstimate(
            flops=flops, bytes_accessed=32 << 20, transcendentals=flops // 1280
        ),
    )(index, info, query, both, both, logs, mixed_grad)


def held_spec(shape):
    return pl.BlockSpec(
        shape, lambda *at: (0,) * len(shape), pipeline_mode=pl.Buffered(buffer_count=1)
    )


def held_out(shape):
    return pl.BlockSpec(shape, lambda *at: (0,) * len(shape))


def step_spec(shape, skip=0):
    zeros = (0,) * (len(shape) - 1)
    return pl.BlockSpec(shape, lambda step, *rest: (step + skip,) + zeros)


def fetch(step, refs, target):
    for piece, ref in enumerate(refs):

        @pl.when(step == piece)
        def _(ref=ref):
            target[...] = ref[...]


def halves_kernel(place, *refs, count):
    small, keep, give = refs[2 * count :]
    step = pl.program_id(0)
    size = refs[0].shape[1]
    blocks = (keep.shape[1] - 128) // (count * size)
    for j in range(count):
        at = pl.ds(pl.multiple_of((j * blocks + step) * size, 128), size)
        keep[:, at] = refs[2 * j][...]
        give[:, at] = refs[2 * j + 1][...]
    keep[:, keep.shape[1] - 128 :] = small[...]
    give[:, keep.shape[1] - 128 :] = small[...]


def weight_halves(s_at, weights, small, blocks):
    rows, columns = weights[0].shape
    size = columns // (2 * blocks)
    count = len(weights)
    shape = (rows, count * blocks * size + 128)
    specs = []
    for _ in weights:
        specs.append(pl.BlockSpec((rows, size), lambda step, place: (0, 2 * step + place[0])))
        specs.append(pl.BlockSpec((rows, size), lambda step, place: (0, 2 * step + 1 - place[0])))
    return pl.pallas_call(
        functools.partial(halves_kernel, count=count),
        grid_spec=pltpu.PrefetchScalarGridSpec(
            num_scalar_prefetch=1,
            grid=(blocks,),
            in_specs=specs + [pl.BlockSpec((rows, 128), lambda step, place: (0, 0))],
            out_specs=[pl.BlockSpec(shape, lambda step, place: (0, 0))] * 2,
        ),
        out_shape=[jax.ShapeDtypeStruct(shape, BF)] * 2,
        compiler_params=pltpu.CompilerParams(vmem_limit_bytes=24 << 20),
        cost_estimate=pl.CostEstimate(flops=0, bytes_accessed=8 << 20, transcendentals=0),
    )(s_at[None], *[w for weight in weights for w in (weight, weight)], small)


def join_kernel(place, *refs, count, blocks):
    mine, other, outs = refs[:count], refs[count : 2 * count], refs[2 * count :]
    size = mine[0].shape[1] // blocks
    for j in range(count):
        for block in range(blocks):
            for seq, ref in enumerate((mine[j], other[j])):
                found = ref[:, block * size : (block + 1) * size].astype(outs[j].dtype)
                outs[j][:, block_at(place, block, seq, size)] = found


def join_columns(s_at, mine, other, blocks, dtype):
    rows, half = mine[0].shape
    count = len(mine)
    return pl.pallas_call(
        functools.partial(join_kernel, count=count, blocks=blocks),
        grid_spec=pltpu.PrefetchScalarGridSpec(
            num_scalar_prefetch=1,
            grid=(1,),
            in_specs=[held_spec((rows, half))] * 2 * count,
            out_specs=[held_out((rows, 2 * half))] * count,
        ),
        out_shape=[jax.ShapeDtypeStruct((rows, 2 * half), dtype)] * count,
        compiler_params=pltpu.CompilerParams(vmem_limit_bytes=40 << 20),
        cost_estimate=pl.CostEstimate(flops=0, bytes_accessed=4 << 20, transcendentals=0),
    )(s_at[None], *mine, *other)


def block_at(place, block, other, size):
    seq = 1 - place[0] if other else place[0]
    return pl.ds(pl.multiple_of((2 * block + seq) * size, 128), size)


def project_kernel(place, gain, pick, keep, took, *refs, x_count, dps):
    normed_out, both_out, query_out, held, low, rows = refs[x_count:]
    double, half = both_out.shape[2], query_out.shape[2]
    blocks, tok, width = normed_out.shape
    cap = query_out.shape[1]
    size = width // (2 * dps)
    step = pl.program_id(0)
    for j in range(blocks):
        fetch(step * blocks + j, refs[:x_count], held.at[pl.ds(j * tok, tok)])
    x = held[:, :width].astype(F32)
    factor = lax.rsqrt(jnp.mean(x * x, axis=1, keepdims=True) + EPS)
    normed = (x * factor * gain[...]).astype(BF)
    low[...] = normed
    for j in range(blocks):
        mine = normed[j * tok : (j + 1) * tok]
        normed_out[j] = mine
        rows[j * cap : (j + 1) * cap] = dot(pick[j], mine).astype(BF)
    both = query = None
    for other, weights in enumerate((keep, took)):
        left = jnp.concatenate([low[:, block_at(place, d, other, size)] for d in range(dps)], axis=1)
        right = jnp.concatenate([rows[:, block_at(place, d, other, size)] for d in range(dps)], axis=1)
        kv_part = dot(left, weights[:, :double])
        q_part = dot(right, weights[:, double : double + half])
        both = kv_part if both is None else both + kv_part
        query = q_part if query is None else query + q_part
    both, query = both.astype(BF), query.astype(BF)
    for j in range(blocks):
        both_out[j] = both[j * tok : (j + 1) * tok]
        query_out[j] = query[j * cap : (j + 1) * cap]


def project(s_at, gain, pick, x_parts, keep, took, half, dps):
    total, cap, tok = pick.shape
    width = gain.shape[1]
    blocks = 2
    flops = 2 * total * (tok * width * 2 * half + cap * width * half)
    return pl.pallas_call(
        functools.partial(project_kernel, x_count=len(x_parts), dps=dps),
        grid_spec=pltpu.PrefetchScalarGridSpec(
            num_scalar_prefetch=1,
            grid=(total // blocks,),
            in_specs=[
                held_spec((1, width)),
                step_spec((blocks, cap, tok)),
                held_spec(keep.shape),
                held_spec(took.shape),
            ]
            + [held_spec(part.shape) for part in x_parts],
            out_specs=[
                step_spec((blocks, tok, width)),
                step_spec((blocks, tok, 2 * half)),
                step_spec((blocks, cap, half)),
            ],
            scratch_shapes=[
                pltpu.VMEM((blocks * tok, x_parts[0].shape[1]), BF),
                pltpu.VMEM((blocks * tok, width), BF),
                pltpu.VMEM((blocks * cap, width), BF),
            ],
        ),
        out_shape=[
            jax.ShapeDtypeStruct((total, tok, width), BF),
            jax.ShapeDtypeStruct((total, tok, 2 * half), BF),
            jax.ShapeDtypeStruct((total, cap, half), BF),
        ],
        compiler_params=pltpu.CompilerParams(vmem_limit_bytes=58 << 20),
        cost_estimate=pl.CostEstimate(flops=flops, bytes_accessed=40 << 20, transcendentals=0),
    )(s_at[None], gain, pick, keep, took, *x_parts)


def back_kernel(place, k_grad, v_grad, slots, keep, took, *refs, dps):
    outs, held = refs[:-1], refs[-1]
    blocks, tok, half = slots.shape
    size = held.shape[1] // (2 * dps)
    q_rows = jnp.concatenate([slots[j] for j in range(blocks)], axis=0)
    k_rows = jnp.concatenate([k_grad[j] for j in range(blocks)], axis=0)
    v_rows = jnp.concatenate([v_grad[j] for j in range(blocks)], axis=0)
    for other, weights in enumerate((keep, took)):
        part = (
            dot_t(k_rows, weights[:, :half])
            + dot_t(v_rows, weights[:, half : 2 * half])
            + dot_t(q_rows, weights[:, 2 * half : 3 * half])
        ).astype(BF)
        for d in range(dps):
            held[:, block_at(place, d, other, size)] = part[:, d * size : (d + 1) * size]
    for j, out in enumerate(outs):

        @pl.when(pl.program_id(0) == j // blocks)
        def _(out=out, at=j % blocks * tok):
            out[...] = held[at : at + tok]


def project_back(s_at, both_grad, slots, keep, took, first, count, dps):
    total, tok, half = slots.shape
    width = 2 * keep.shape[0]
    blocks = 2
    skip = first // blocks
    whole = pl.BlockSpec((tok, width), lambda *at: (0, 0))
    return pl.pallas_call(
        functools.partial(back_kernel, dps=dps),
        grid_spec=pltpu.PrefetchScalarGridSpec(
            num_scalar_prefetch=1,
            grid=(count // blocks,),
            in_specs=[
                step_spec((blocks, tok, half), skip),
                step_spec((blocks, tok, half), skip),
                step_spec((blocks, tok, half), skip),
                held_spec(keep.shape),
                held_spec(took.shape),
            ],
            out_specs=[whole] * count,
            scratch_shapes=[pltpu.VMEM((blocks * tok, width), BF)],
        ),
        out_shape=[jax.ShapeDtypeStruct((tok, width), BF)] * count,
        compiler_params=pltpu.CompilerParams(vmem_limit_bytes=58 << 20),
        cost_estimate=pl.CostEstimate(
            flops=6 * count * tok * width * half, bytes_accessed=24 << 20, transcendentals=0
        ),
    )(s_at[None], *both_grad, slots, keep, took)


def expert_kernel(
    rows, act_back, gate_wt, up_wt, in_out, gate_out, up_out, scaled_out, act_out, dots_out
):
    width = gate_wt.shape[1]
    x = rows[:, :width]
    tail = rows[:, width : width + 128].astype(F32)
    weight = tail[:, 0:1] + tail[:, 1:2] + tail[:, 2:3]
    gate_pre = dot_t(x, gate_wt[...])
    up_pre = dot_t(x, up_wt[...])
    sigma = jax.nn.sigmoid(gate_pre)
    activated = gate_pre * sigma
    act = activated * up_pre
    back = act_back[...]
    dots_out[...] = jnp.sum(act * back, axis=1, keepdims=True)
    back = back * weight
    gate_grad = (back * up_pre * sigma * (1.0 + gate_pre * (1.0 - sigma))).astype(BF)
    up_grad = (back * activated).astype(BF)
    gate_out[...] = gate_grad
    up_out[...] = up_grad
    scaled_out[...] = (act * weight).astype(BF)
    act_out[...] = act.astype(BF)
    in_out[...] = (dot(gate_grad, gate_wt[...]) + dot(up_grad, up_wt[...])).astype(BF)


def expert_mlp(rows, act_back, gate_wt, up_wt):
    inner, width = gate_wt.shape
    every = rows.shape[0]
    size = min(512, every)
    return pl.pallas_call(
        expert_kernel,
        grid=(every // size,),
        in_specs=[step_spec((size, rows.shape[1])), step_spec((size, inner))]
        + [held_spec(w.shape) for w in (gate_wt, up_wt)],
        out_specs=[step_spec((size, width))]
        + [step_spec((size, inner))] * 4
        + [step_spec((size, 1))],
        out_shape=[jax.ShapeDtypeStruct((every, width), BF)]
        + [jax.ShapeDtypeStruct((every, inner), BF)] * 4
        + [jax.ShapeDtypeStruct((every, 1), F32)],
        compiler_params=pltpu.CompilerParams(vmem_limit_bytes=58 << 20),
        cost_estimate=pl.CostEstimate(
            flops=8 * every * width * inner,
            bytes_accessed=60 << 20,
            transcendentals=2 * every * inner,
        ),
    )(rows, act_back, gate_wt, up_wt)


def lanes_of(value):
    return lax.broadcasted_iota(jnp.int32, (value.shape[0], 128), 1)


def three_low(value):
    first = value.astype(BF)
    rest = value - first.astype(F32)
    second = rest.astype(BF)
    return first, second, (rest - second.astype(F32)).astype(BF)


def hot_of(flat, slots):
    ids = lax.broadcasted_iota(jnp.int32, (flat.shape[0], slots), 1)
    return [flat[:, k : k + 1] == ids for k in range(flat.shape[1])]


def combine_kernel(x, mix_high, mix_low, gain, router, routes, flat, *refs, count):
    pairs = jnp.concatenate([ref[...] for ref in refs[:count]], axis=0)
    hidden_out, normed_out, gates_out, mix_out = refs[count : count + 4]
    sends = refs[count + 4 :]
    part, width = refs[0].shape
    hidden = x[...].astype(F32) + dot(mix_high[...], pairs) + dot(mix_low[...], pairs)
    hidden_out[...] = hidden
    factor = lax.rsqrt(jnp.mean(hidden * hidden, axis=1, keepdims=True) + EPS)
    normed = (hidden * factor * gain[...]).astype(BF)
    normed_out[...] = normed
    logits = dot(normed, router[...])
    lanes = lanes_of(logits)
    ids, places = routes[...], flat[...]
    one, two = [
        jnp.sum(jnp.where(lanes == ids[:, k : k + 1], logits, 0.0), axis=1, keepdims=True)
        for k in range(2)
    ]
    top = jnp.maximum(one, two)
    one, two = jnp.exp(one - top), jnp.exp(two - top)
    gates = [one / (one + two), two / (one + two)]
    gates_out[...] = jnp.where(lanes == 0, gates[0], jnp.where(lanes == 1, gates[1], 0.0))
    hot = hot_of(places, part * count)
    mix = jnp.where(hot[0], gates[0], 0.0) + jnp.where(hot[1], gates[1], 0.0)
    mix_out[...] = mix
    pick = jnp.where(hot[0] | hot[1], 1.0, 0.0).astype(BF)
    rows = t_dot(pick, normed).astype(BF)
    ones = jnp.ones((hidden.shape[0], 128), BF)
    columns = [t_dot(term, ones) for term in three_low(mix)]
    lanes = lanes_of(columns[0])
    tail = jnp.where(lanes == 0, columns[0], 0.0)
    for j in (1, 2):
        tail = tail + jnp.where(lanes == j, columns[j], 0.0)
    tail = tail.astype(BF)
    for j, send in enumerate(sends):
        at = slice(j * part, (j + 1) * part)
        send[:, :width] = rows[at]
        send[:, width:] = tail[at]


def combine(x, mix_high, mix_low, gain, router, routes, flat, pairs):
    tok, width = x.shape
    part = pairs[0].shape[0]
    count = len(pairs)
    operands = (x, mix_high, mix_low, gain, router, routes, flat, *pairs)
    return pl.pallas_call(
        functools.partial(combine_kernel, count=count),
        grid=(1,),
        in_specs=[held_spec(operand.shape) for operand in operands],
        out_specs=[held_out((tok, width))] * 2
        + [held_out((tok, 128)), held_out((tok, part * count))]
        + [held_out((part, width + 128))] * count,
        out_shape=[
            jax.ShapeDtypeStruct((tok, width), F32),
            jax.ShapeDtypeStruct((tok, width), BF),
            jax.ShapeDtypeStruct((tok, 128), F32),
            jax.ShapeDtypeStruct((tok, part * count), F32),
        ]
        + [jax.ShapeDtypeStruct((part, width + 128), BF)] * count,
        compiler_params=pltpu.CompilerParams(vmem_limit_bytes=40 << 20),
        cost_estimate=pl.CostEstimate(
            flops=6 * tok * part * count * width, bytes_accessed=10 << 20, transcendentals=0
        ),
    )(*operands)


def between_kernel(
    hidden, normed, grad_out, gain, router, routes, flat, gates, attn_pick, weight, *refs, count
):
    parts = refs[:count]
    total_out, high_out, gain_out, logit_out = refs[count : count + 4]
    sends = refs[count + 4 :]
    part, width = sends[0].shape
    rows = jnp.concatenate([ref[:, :width] for ref in parts], axis=0)
    tail = jnp.concatenate([ref[:, width:] for ref in parts], axis=0)
    hot = hot_of(flat[...], part * count)
    ids, held = routes[...], gates[...]
    lanes = lanes_of(held)
    slot_grad = []
    for k in range(2):
        found = dot(jnp.where(hot[k], 1.0, 0.0).astype(BF), tail)
        slot_grad.append(jnp.sum(jnp.where(lanes < 3, found, 0.0), axis=1, keepdims=True))
    gate = [held[:, 0:1], held[:, 1:2]]
    center = gate[0] * slot_grad[0] + gate[1] * slot_grad[1]
    logit_grad = jnp.zeros(held.shape, F32)
    for k in range(2):
        chosen = gate[k] * (slot_grad[k] - center)
        logit_grad = logit_grad + jnp.where(lanes == ids[:, k : k + 1], chosen, 0.0)
    logit_out[...] = logit_grad
    pick = jnp.where(hot[0] | hot[1], 1.0, 0.0).astype(BF)
    grad = dot(pick, rows)
    for term in three_low(logit_grad):
        grad = grad + dot_t(term, router[...])
    values = hidden[...]
    factor = lax.rsqrt(jnp.mean(values * values, axis=1, keepdims=True) + EPS)
    unit = values * factor
    gain_out[...] = jnp.sum(grad * unit, axis=0, keepdims=True)
    scaled = grad * gain[...]
    back = factor * (scaled - unit * jnp.mean(scaled * unit, axis=1, keepdims=True))
    total = grad_out[...].astype(F32) + back
    total_out[...] = total
    high = total.astype(BF)
    low = (total - high.astype(F32)).astype(BF)
    high_out[...] = high
    picked_rows = t_dot(attn_pick[...], high) + t_dot(attn_pick[...], low)
    picked_rows = (picked_rows * weight[...]).astype(BF)
    for j, send in enumerate(sends):
        send[...] = picked_rows[j * part : (j + 1) * part]


def between(hidden, normed, grad_out, gain, router, routes, flat, gates, attn_pick, weight, parts):
    tok, width = hidden.shape
    part = parts[0].shape[0]
    count = len(parts)
    operands = (
        hidden, normed, grad_out, gain, router, routes, flat, gates, attn_pick, weight, *parts
    )
    return pl.pallas_call(
        functools.partial(between_kernel, count=count),
        grid=(1,),
        in_specs=[held_spec(operand.shape) for operand in operands],
        out_specs=[held_out((tok, width))] * 2
        + [held_out((1, width)), held_out((tok, 128))]
        + [held_out((part, width))] * count,
        out_shape=[
            jax.ShapeDtypeStruct((tok, width), F32),
            jax.ShapeDtypeStruct((tok, width), BF),
            jax.ShapeDtypeStruct((1, width), F32),
            jax.ShapeDtypeStruct((tok, 128), F32),
        ]
        + [jax.ShapeDtypeStruct((part, width), BF)] * count,
        compiler_params=pltpu.CompilerParams(vmem_limit_bytes=40 << 20),
        cost_estimate=pl.CostEstimate(
            flops=6 * tok * part * count * width, bytes_accessed=12 << 20, transcendentals=0
        ),
    )(*operands)


def act_back_kernel(grads, down_w, out):
    out[...] = dot_t(grads[...], down_w[...])


def expert_act_back(grads, down_w):
    every, width = grads.shape
    inner = down_w.shape[0]
    size = min(512, every)
    return pl.pallas_call(
        act_back_kernel,
        grid=(every // size,),
        in_specs=[step_spec((size, width)), held_spec(down_w.shape)],
        out_specs=step_spec((size, inner)),
        out_shape=jax.ShapeDtypeStruct((every, inner), F32),
        compiler_params=pltpu.CompilerParams(vmem_limit_bytes=40 << 20),
        cost_estimate=pl.CostEstimate(
            flops=2 * every * width * inner, bytes_accessed=18 << 20, transcendentals=0
        ),
    )(grads, down_w)


def body(
    inputs,
    lengths,
    attn_routes,
    mlp_routes,
    slot_order,
    gain_attn,
    router_attn,
    w_key,
    w_value,
    w_query,
    w_out,
    gain_mlp,
    router_mlp,
    w_gate,
    w_up,
    w_down,
    d_out,
):
    seq_count, stretch, width = inputs.shape
    tok = seq_count * stretch
    top_count = attn_routes.shape[2]
    experts = router_attn.shape[1]
    cap = top_count * tok // experts
    slots = experts * cap
    dps, seqs = lax.axis_size("dp"), lax.axis_size("seq")
    total = experts * seqs
    e_at, s_at = lax.axis_index("expert"), lax.axis_index("seq")
    block = e_at * seqs + s_at
    rows_own = w_key.shape[0]
    inner = w_key.shape[1]
    half = inner // seqs

    absolute = lax.broadcasted_iota(jnp.int32, (total,), 0)
    index = lax.rem(absolute % seqs - s_at + seqs, seqs) * experts + lax.rem(
        absolute // seqs - e_at + experts, experts
    )
    block_of = lax.rem(absolute % experts + e_at, experts) * seqs + lax.rem(
        absolute // experts + s_at, seqs
    )

    x_low = inputs.reshape(tok, width)
    attn_idx = attn_routes.reshape(tok, top_count)
    mlp_idx = mlp_routes.reshape(tok, top_count)
    order = slot_order.reshape(tok)
    marks = jnp.concatenate([attn_idx, order[:, None]], axis=1).astype(BF)
    marks = jnp.pad(marks, ((0, 0), (0, 128 - marks.shape[1])))
    x_marked = jnp.concatenate([x_low, marks], axis=1)

    small = [gain_attn[:, None], router_attn, gain_mlp[:, None], router_mlp]
    small.append(jnp.zeros((rows_own, 128 - 2 - 2 * experts), BF))
    w_keep, w_give = weight_halves(
        s_at, (w_key, w_value, w_query[0]), jnp.concatenate(small, axis=1), dps
    )
    x_parts = group_gather(x_marked)
    w_keep = lax.all_gather(w_keep, "dp", axis=0, tiled=True)
    w_took = lax.all_gather(swap_x(w_give), "dp", axis=0, tiled=True)
    out_w = lax.all_gather(w_out[0], "dp", axis=0, tiled=True)

    def feature_rows(first, last):
        pair = [w[:, 3 * half + first : 3 * half + last] for w in (w_keep, w_took)]
        pair = [w.reshape(dps, rows_own, last - first) for w in pair]
        pair = jnp.where(s_at == 0, jnp.stack(pair, axis=1), jnp.stack(pair[::-1], axis=1))
        return pair.reshape(width, last - first)

    small = feature_rows(0, 2 + 2 * experts)
    norm_one = small[:, 0].astype(F32)[None]
    route_one = small[:, 1 : 1 + experts]
    norm_two = small[:, 1 + experts].astype(F32)[None]
    route_two = jnp.pad(small[:, 2 + experts :], ((0, 0), (0, 128 - experts)))

    column = lax.broadcasted_iota(jnp.int32, (seq_count, stretch), 1)
    is_valid = (block * stretch + column < lengths[:, None]).reshape(tok)
    attn_kept, attn_slot = route_pairs(attn_idx, order, is_valid, cap)
    mlp_kept, mlp_slot = route_pairs(mlp_idx, order, is_valid, cap)
    attn_keep = attn_kept.astype(F32)
    attn_flat = spots(attn_idx, attn_kept, attn_slot, experts, cap)
    mlp_flat = spots(mlp_idx, mlp_kept, mlp_slot, experts, cap)
    attn_hot = hots(attn_flat, experts, cap)
    mlp_hot = hots(mlp_flat, experts, cap)
    attn_pick = (attn_hot[0] | attn_hot[1]).astype(BF)
    mlp_pick = (mlp_hot[0] | mlp_hot[1]).astype(BF)

    part = cap // 2
    chunk = experts * part
    chunks = [slice(c * chunk, (c + 1) * chunk) for c in range(2)]

    def pieces_of(array):
        return [array[r * part : (r + 1) * part] for r in range(experts)]

    g_low = d_out.reshape(tok, width)
    gate_wt, up_wt, down_w = w_gate[0].T, w_up[0].T, w_down[0]
    found = jnp.stack(
        [rows[:, width : width + 3] for rows in x_parts]
    ).astype(jnp.int32)
    tok_ids = lax.broadcasted_iota(jnp.int32, (1, tok), 1)
    places = block_of[:, None] * stretch + tok_ids % stretch
    limits = jnp.where(tok_ids // stretch == 0, lengths[0], lengths[1])
    mine = ((found[:, :, 0] == e_at) | (found[:, :, 1] == e_at)) & (places < limits)
    ranks = found[:, :, 2]
    ahead = mine[:, None, :] & (ranks[:, None, :] < ranks[:, :, None])
    ahead = jnp.sum(ahead.astype(jnp.int32), axis=2, dtype=jnp.int32)
    ahead = jnp.where(mine, ahead, cap)
    chosen = ahead[:, None, :] == lax.broadcasted_iota(jnp.int32, (1, cap, 1), 1)
    pick = chosen.astype(BF)
    row_seq = jnp.sum(jnp.where(chosen, (tok_ids // stretch)[:, None], 0), axis=2, dtype=jnp.int32)
    row_place = jnp.sum(jnp.where(chosen, places[:, None], 0), axis=2, dtype=jnp.int32)
    info = jnp.stack([row_seq, row_place], axis=2)

    normed_all, both, query = project(s_at, norm_one, pick, x_parts, w_keep, w_took, half, dps)
    g_send = t_dot(mlp_pick, g_low).astype(BF).reshape(2, experts, part, width)
    g_send = after(g_send, x_parts)
    g_took = z_rounds([g_send[:, r] for r in range(experts)], -1)
    g_took = jnp.stack(after(g_took, query), axis=1)
    g_rows = [square_gather(g_took[c].reshape(chunk, width)) for c in range(2)]
    act_back = [expert_act_back(rows, down_w) for rows in g_rows]
    mixed, logs = attend(index, info, query, both)
    mixed_parts = mixed.reshape(seqs, experts, 2, part, half)
    attn_pairs, took_before = [], []
    for c in range(2):
        partial = dot(mixed_parts[:, :, c].reshape(seqs * chunk, half), out_w).astype(BF)
        took = swap_x(after(partial[chunk:], *took_before))
        took_before = [took]
        attn_out = [
            add_low(mine, other) for mine, other in zip(pieces_of(partial[:chunk]), pieces_of(took))
        ]
        attn_pairs += z_rounds(attn_out, 1)
    attn_pairs, act_back = lax.optimization_barrier((attn_pairs, act_back))

    x_in = x_low.astype(F32)
    normed_one = normed_all[0]
    attn_gates = gate_values(normed_one, route_one, attn_idx)
    attn_weight = attn_gates * attn_keep
    attn_mix = weigh(attn_hot, attn_weight)
    mix_high, mix_low = in_two(attn_mix)
    hidden, normed_two, mlp_gates, mlp_mix, *rows_sends = combine(
        x_low, mix_high, mix_low, norm_two, route_two, mlp_idx, mlp_flat, attn_pairs
    )

    expert_out, rows_before = [], []
    for c in range(2):
        rows_send = after(rows_sends[c * experts : (c + 1) * experts], *rows_before)
        rows_took = jnp.concatenate(z_rounds(rows_send, -1), axis=0)
        rows_before = [rows_took]
        rows = square_gather(rows_took)
        expert_out.append(
            (rows,) + tuple(expert_mlp(rows, act_back[c], gate_wt, up_wt))
        )
    in_pairs, out_parts = [], []
    grads = []
    for c in range(2):
        found = expert_out[c]
        grads.append(
            [
                t_dot(found[0][:, :width], found[2]),
                t_dot(found[0][:, :width], found[3]),
                t_dot(found[4], g_rows[c]),
            ]
        )
        if c == 1:
            grads = [low + high for low, high in zip(*grads)]
        in_sum = square_scatter(found[1])
        out_parts.append(dot(after(found[5], expert_out[1][1]), down_w).astype(BF))
        if c == 1:
            in_sum, grads, out_parts = lax.optimization_barrier((in_sum, grads, out_parts))
        dots = tiny_scatter(found[6].reshape(dps, seqs, chunk))
        in_sum = jnp.concatenate([in_sum, in_columns(dots[:, None])], axis=1)
        in_pairs += z_rounds(pieces_of(in_sum), 1)
    grad_gate, grad_up, grad_down = grads

    attn_columns = jnp.sum(attn_mix, axis=0)[:, None]
    hidden_total, total_high, norm_two_grad, logit_grad, *dh_sends = between(
        hidden, normed_two, g_low, norm_two, route_two, mlp_idx, mlp_flat, mlp_gates, attn_pick,
        attn_columns, in_pairs,
    )
    router_two_grad = jnp.dot(
        normed_two.astype(F32).T, logit_grad[:, :experts], precision=HIGH
    )

    dh_own, dh_other = [], []
    for c in range(2):
        dh_send = after(dh_sends[c * experts : (c + 1) * experts], *dh_own)
        dh_own.append(jnp.concatenate(z_rounds(dh_send, -1), axis=0))
        dh_other.append(swap_x(after(dh_own[-1], *dh_other)))
    dh_rows = jnp.stack([jnp.stack(dh_own), jnp.stack(dh_other)])
    dh_rows = dh_rows.reshape(seqs, 2, experts, part, width).transpose(0, 2, 1, 3, 4)
    dh_rows = dh_rows.reshape(total * cap, width)

    out_sums = [
        square_scatter(out_parts[0]),
        square_scatter(after(out_parts[1], dh_rows)),
    ]

    slot_dots = dot_t(total_high, jnp.concatenate(attn_pairs, axis=0))
    attn_gate_grad = jnp.concatenate(
        [jnp.sum(jnp.where(hot, slot_dots, 0.0), axis=1, keepdims=True) for hot in attn_hot], axis=1
    )
    mixed_grad = dot_t(dh_rows, out_w).astype(BF).reshape(total, cap, half)
    grad_out_w = t_dot(mixed.reshape(total * cap, half), dh_rows).astype(BF)
    mixed_grad, grad_out_w = lax.optimization_barrier((mixed_grad, grad_out_w))
    mixed_grad = after(mixed_grad, out_sums[0])
    grad_out_w = lax.psum_scatter(grad_out_w, "dp", scatter_dimension=0, tiled=True)
    q_grad, *both_grad = attend_back(index, info, query, both, logs, mixed_grad)

    flat_normed = normed_all.reshape(total * tok, width)
    both_dots = [
        t_dot(flat_normed, array.reshape(total * tok, half))
        .astype(BF)
        .reshape(dps, seqs * rows_own, half)
        for array in both_grad
    ]
    q_grad, both_grad = after((q_grad, both_grad), out_sums[1])
    if is_small():
        firsts = [dp_first(dots) for dots in both_dots]
        q_grad, both_grad = after((q_grad, both_grad), [far for _, far in firsts])
    q_slots = jnp.einsum("bct,bch->bth", pick, q_grad, preferred_element_type=F32).astype(BF)
    query_grads = t_dot(flat_normed, q_slots.reshape(total * tok, half)).astype(BF)
    q_slots = after(q_slots, query_grads)
    query_grads = lax.psum_scatter(query_grads, "dp", scatter_dimension=0, tiled=True)

    in_other = project_back(s_at, both_grad, q_slots, w_keep, w_took, experts, experts, dps)
    if is_small():
        both_grads = [after(add_low(mine, swap_y(far)), in_other) for mine, far in firsts]
    else:
        both_grads = [
            lax.psum_scatter(dots, "dp", scatter_dimension=0, tiled=False) for dots in both_dots
        ]
    q_slots = after(q_slots, both_grads)
    in_own = project_back(s_at, both_grad, q_slots, w_keep, w_took, 0, experts, dps)
    one_sum, _ = group_scatter(in_own, in_other)
    shared = lax.psum(jnp.stack(both_grads), "expert")

    out_sums = after(out_sums, both_grads)
    out_pairs = []
    for out_sum in out_sums:
        out_pairs += z_rounds(pieces_of(out_sum), 1)
    out_pairs = jnp.concatenate(out_pairs, axis=0)
    mlp_high, mlp_low = in_two(mlp_mix)
    output = hidden + dot(mlp_high, out_pairs) + dot(mlp_low, out_pairs)
    result_out = output.astype(BF).reshape(seq_count, stretch, width)

    def joined(arrays):
        arrays = [array.reshape(seqs, rows_own, half) for array in arrays]
        mine = [lax.dynamic_index_in_dim(array, s_at, 0, keepdims=False) for array in arrays]
        give = [lax.dynamic_index_in_dim(array, 1 - s_at, 0, keepdims=False) for array in arrays]
        return join_columns(s_at, mine, [swap_x(array) for array in give], dps, F32)

    (grad_query,) = joined([query_grads])
    shared_grads = joined([shared[0], shared[1]])

    router_one_grad, router_one_input = gate_grads(
        normed_one, route_one, attn_idx, attn_gates, attn_gate_grad
    )
    normed_one_grad = one_sum + router_one_input
    input_grad, norm_one_grad = norm_back(x_in, norm_one, normed_one_grad)
    grad_x = (hidden_total + input_grad).astype(BF).reshape(seq_count, stretch, width)

    little = little_sum(
        jnp.concatenate(
            [norm_one_grad[None], router_one_grad.T, norm_two_grad, router_two_grad.T], axis=0
        )
    )
    return (
        result_out,
        grad_x,
        little[0],
        little[1 : 1 + experts].T,
        shared_grads[0],
        shared_grads[1],
        grad_query[None],
        grad_out_w.astype(F32)[None],
        little[1 + experts],
        little[2 + experts :].T,
        grad_gate[None],
        grad_up[None],
        grad_down[None],
    )


def solution(mesh):
    in_specs = (
        P("dp", ("expert", "seq"), None),
        P("dp"),
        P("dp", ("expert", "seq"), None),
        P("dp", ("expert", "seq"), None),
        P("dp", ("expert", "seq"), None),
        P(("dp", "seq")),
        P(("dp", "seq"), None),
        P(("dp", "seq"), None),
        P(("dp", "seq"), None),
        P("expert", ("dp", "seq"), None),
        P("expert", ("dp", "seq"), None),
        P(("dp", "seq")),
        P(("dp", "seq"), None),
        P("expert", None, ("dp", "seq")),
        P("expert", None, ("dp", "seq")),
        P("expert", ("dp", "seq"), None),
        P("dp", ("expert", "seq"), None),
    )
    out_specs = (
        P("dp", ("expert", "seq"), None),
        P("dp", ("expert", "seq"), None),
        P(("dp", "seq")),
        P(("dp", "seq"), None),
        P(("dp", "seq"), None),
        P(("dp", "seq"), None),
        P("expert", ("dp", "seq"), None),
        P("expert", ("dp", "seq"), None),
        P(("dp", "seq")),
        P(("dp", "seq"), None),
        P("expert", None, ("dp", "seq")),
        P("expert", None, ("dp", "seq")),
        P("expert", ("dp", "seq"), None),
    )
    return jax.shard_map(body, mesh=mesh, in_specs=in_specs, out_specs=out_specs, check_vma=False)
```

time: 1590 us -> 1320 us (0.83)
  matrix products: 355 us -> 174 us
  Pallas kernels: 77.2 us -> 256 us
  waiting for transfers between devices: 697 us -> 550 us
  other arithmetic: 132 us -> 58.2 us
  blocking collectives: 63.9 us -> 0 us
  local copies, waits for them, and re-layouts: 106 us -> 122 us
    pallas_call x0 -> x12, Pallas kernels: none -> 181 us  [the longest x2 67.7 us: expert_mlp(): pl.pallas_call(expert_kernel, grid=(every // size,), in_specs=[step_spec(...]
    psum x2 -> x1, waiting for transfers between devices: 180 us -> 0.01 us  [body(): shared = lax.psum(jnp.stack(both_grads), 'expert')]
    dot_general x6 -> x2, matrix products: 118 us -> 13.5 us  [dot_t(): lax.dot_general(left, right, (((1,), (1,)), ((), ())), preferred_element_...]
    ppermute x33 -> x19, waiting for transfers between devices: 276 us -> 190 us  [swap_x(): return lax.ppermute(value, 'seq', flip(2, 1))]
    all_gather x0 -> x7, waiting for transfers between devices: none -> 83.8 us  [the longest x4 83.7 us: square_gather(): return lax.all_gather(piece, ('dp', 'seq'), axis=0, tiled=True)]
    ppermute x19 -> x5, waiting for transfers between devices: 73.4 us -> 8.51 us  [swap_y(): return lax.ppermute(value, 'dp', flip(4, 2))]
    dot_general x13 -> x7, matrix products: 104 us -> 38.9 us  [dot(): return jnp.dot(left, right, preferred_element_type=F32)]
    all_gather x2 -> x0, blocking collectives: 63.9 us -> none  [the longest x1 51.5 us: body(): lax.all_gather(table.reshape(experts, cap), ('expert', 'seq'), axis=0, ti...]
  transfers between devices with their start and end apart: 120 -> 86, of which waited for: 48 -> 45; matrix products, arithmetic and copies ran while one was open for 28% -> 23% of each run, Pallas kernels for 2% -> 19%
where the time goes in v2:
time: 1320 us; the launch traced here: 1310 us
  waiting for transfers between devices  550 us (42%)
  Pallas kernels  256 us (19%)
  matrix products  174 us (13%)
  starting transfers between devices  133 us (10%)
  local copies, waits for them, and re-layouts  122 us (9%)
  other arithmetic  58.2 us (4%)
  between operations  16 us (1%)
    ppermute x19, waiting for transfers between devices, swap_x(): return lax.ppermute(value, 'seq', flip(2, 1))  190 us
    ppermute x33, waiting for transfers between devices, z_rounds(): lax.ppermute(pieces[r], 'expert', ring(count, sign * r))  135 us
    dot_general x11, matrix products, t_dot(): lax.dot_general(left, right, (((0,), (0,)), ((), ())), preferred_element_...  112 us
    all_gather x4, waiting for transfers between devices, square_gather(): return lax.all_gather(piece, ('dp', 'seq'), axis=0, tiled=True)  83.7 us
    pallas_call x2, Pallas kernels, expert_mlp(): pl.pallas_call(expert_kernel, grid=(every // size,), in_specs=[step_spec(...  67.7 us
    unnamed x272, local copies, waits for them, and re-layouts  66.8 us
    ppermute x33, starting transfers between devices, z_rounds(): lax.ppermute(pieces[r], 'expert', ring(count, sign * r))  61.5 us
    pallas_call x1, Pallas kernels, attend_back(): pl.pallas_call(functools.partial(attend_back_kernel, blocks=blocks), grid...  48.5 us
  transfers between devices with their start and end apart: 86, of which 45 were waited for; matrix products, arithmetic and copies ran while one was open for 23% of the time, Pallas kernels for 19%

profile of v2, /device:TPU:0, one launch (start us, length us, event | category | flops | bytes accessed | tf_op | source)
XLA Modules:
  0.0 1309.0 jit_solution(4812257165080943025)
XLA Ops:
  19.4 35.9 %collective-permute-done = bf16[256,3200]{1,0:T(8,128)(2,1)} collective-permute-done((bf16[256,3200]{1,0:T(8,128)(2,1)S(1)}, bf16[256,3200]{1,0:T(8,128)(2,1)}, u32[]{:S(2)}, u32[]{:S(2)}) %collective-permute-start) | collective-permute-done | bytes 1638432 | tf_op jit(solution)/shard_map/ppermute | solution.py:44
  67.9 20.4 %collective-permute-done.2.refs_3_ = bf16[256,2176]{1,0:T(8,128)(2,1)} collective-permute-done((bf16[256,2176]{1,0:T(8,128)(2,1)}, bf16[256,2176]{1,0:T(8,128)(2,1)}, u32[]{:S(2)}, u32[]{:S(2)}) %collective-permute-start.2) | collective-permute-done | bytes 1114144 | tf_op jit(solution)/shard_map/ppermute | solution.py:86
  92.5 18.5 %collective-permute-done.1.refs_1_ = bf16[256,2176]{1,0:T(8,128)(2,1)} collective-permute-done((bf16[256,2176]{1,0:T(8,128)(2,1)}, bf16[256,2176]{1,0:T(8,128)(2,1)}, u32[]{:S(2)}, u32[]{:S(2)}) %collective-permute-start.1) | collective-permute-done | bytes 1114144 | tf_op jit(solution)/shard_map/ppermute | solution.py:85
  118.7 6.5 collective-permute-done.3
  127.2 6.6 collective-permute-done.4
  139.2 5.4 collective-permute-done.8.refs_7_
  145.5 22.9 %collective-permute-done.6.refs_5_ = bf16[256,2176]{1,0:T(8,128)(2,1)} collective-permute-done((bf16[256,2176]{1,0:T(8,128)(2,1)}, bf16[256,2176]{1,0:T(8,128)(2,1)}, u32[]{:S(2)}, u32[]{:S(2)}) %collective-permute-start.6) | collective-permute-done | bytes 1114144 | tf_op jit(solution)/shard_map/ppermute | solution.py:44
  169.3 17.7 %collective-permute-done.7.refs_6_ = bf16[256,2176]{1,0:T(8,128)(2,1)} collective-permute-done((bf16[256,2176]{1,0:T(8,128)(2,1)}, bf16[256,2176]{1,0:T(8,128)(2,1)}, u32[]{:S(2)}, u32[]{:S(2)}) %collective-permute-start.7) | collective-permute-done | bytes 1114144 | tf_op jit(solution)/shard_map/ppermute | solution.py:44
  202.3 36.4 %shard_map.265 = (bf16[8,256,2048]{2,1,0:T(8,128)(2,1)}, bf16[8,256,2048]{2,1,0:T(8,128)(2,1)}, bf16[8,128,1024]{2,1,0:T(8,128)(2,1)}) custom-call(s32[1]{0:T(128)} %bitcast.4.place, f32[1,2048]{1,0:T(1,128)} %bitcast.330, bf16[8,128,256]{2,1,0:T(8,128)(2,1)} %fusion.41.pick, bf16[1024,3200]{1,0:T(8,128)(2,1)} %all-gather.9.cloned.1.call-done.keep, ...), custom_call_target="tpu_custom_call" | custom-call | flops 21474836480 | bytes 41943040 | tf_op jit(solution)/shard_map/pallas_call | solution.py:555
  243.6 26.8 %shard_map.266 = (bf16[8,128,1024]{2,1,0:T(8,128)(2,1)S(1)}, f32[8,128,128]{2,1,0:T(8,128)S(1)}) custom-call(s32[8]{0:T(128)S(1)} %fusion.106.index, s32[8,128,2]{2,1,0:T(8,128)S(1)} %copy.214.info, bf16[8,128,1024]{2,1,0:T(8,128)(2,1)} %get-tuple-element.132.query, bf16[8,256,2048]{2,1,0:T(8,128)(2,1)} %get-tuple-element.133.keys.values, ...), custom_call_target="tpu_custom_call" | custom-call | flops 8589934592 | bytes 16777216 | tf_op jit(solution)/shard_map/pallas_call | solution.py:368
  273.3 4.9 fusion.20
  283.0 5.0 fusion.23
  288.1 27.2 %collective-permute-done.9 = bf16[256,2048]{1,0:T(8,128)(2,1)S(1)} collective-permute-done((bf16[256,2048]{1,0:T(8,128)(2,1)}, bf16[256,2048]{1,0:T(8,128)(2,1)S(1)}, u32[]{:S(2)}, u32[]{:S(2)}) %collective-permute-start.9) | collective-permute-done | bytes 1048608 | tf_op jit(solution)/shard_map/ppermute | solution.py:44
  323.4 27.0 %collective-permute-done.13 = bf16[256,2048]{1,0:T(8,128)(2,1)S(1)} collective-permute-done((bf16[256,2048]{1,0:T(8,128)(2,1)S(1)}, bf16[256,2048]{1,0:T(8,128)(2,1)S(1)}, u32[]{:S(2)}, u32[]{:S(2)}) %collective-permute-start.13) | collective-permute-done | bytes 1048608 | tf_op jit(solution)/shard_map/ppermute | solution.py:44
  357.0 9.1 shard_map.268.act_back
  370.5 5.1 all-gather.13.cloned.1.call-done.grads
  377.4 8.9 shard_map.267.act_back
  413.7 5.3 collective-permute-done.20
  419.7 16.5 %collective-permute-done.21 = bf16[64,2176]{1,0:T(8,128)(2,1)S(1)} collective-permute-done((bf16[64,2176]{1,0:T(8,128)(2,1)S(1)}, bf16[64,2176]{1,0:T(8,128)(2,1)S(1)}, u32[]{:S(2)}, u32[]{:S(2)}) %collective-permute-start.21) | collective-permute-done | bytes 278560 | tf_op jit(solution)/shard_map/ppermute | solution.py:58
  441.6 4.9 collective-permute-done.23
  446.5 17.4 %collective-permute-done.24 = bf16[64,2176]{1,0:T(8,128)(2,1)S(1)} collective-permute-done((bf16[64,2176]{1,0:T(8,128)(2,1)}, bf16[64,2176]{1,0:T(8,128)(2,1)S(1)}, u32[]{:S(2)}, u32[]{:S(2)}) %collective-permute-start.24) | collective-permute-done | bytes 278560 | tf_op jit(solution)/shard_map/ppermute | solution.py:58
  466.8 53.7 %all-gather.17.cloned.1.call-done.rows = bf16[2048,2176]{1,0:T(8,128)(2,1)} async-done(((bf16[256,2176]{1,0:T(8,128)(2,1)}), bf16[2048,2176]{1,0:T(8,128)(2,1)}) %all-gather.17.cloned.1.call-update) | async-done | bytes 8912912 | tf_op jit(solution)/shard_map/all_gather | solution.py:74
  520.5 33.9 %shard_map.270 = (bf16[2048,2048]{1,0:T(8,128)(2,1)}, bf16[2048,704]{1,0:T(8,128)(2,1)}, bf16[2048,704]{1,0:T(8,128)(2,1)}, bf16[2048,704]{1,0:T(8,128)(2,1)}, b...) custom-call(bf16[2048,2176]{1,0:T(8,128)(2,1)} %all-gather.17.cloned.1.call-done.rows, f32[2048,704]{1,0:T(8,128)} %copy-done.59, ...), custom_call_target="tpu_custom_call" | custom-call | flops 23622320128 | bytes 62914560 | tf_op jit(solution)/shard_map/pallas_call | solution.py:667
  554.6 24.9 %all-gather.19.cloned.1.call-done.rows = bf16[2048,2176]{1,0:T(8,128)(2,1)} async-done(((bf16[256,2176]{1,0:T(8,128)(2,1)}), bf16[2048,2176]{1,0:T(8,128)(2,1)}) %all-gather.19.cloned.1.call-update) | async-done | bytes 8912912 | tf_op jit(solution)/shard_map/all_gather | solution.py:74
  579.6 33.9 %shard_map.271 = (bf16[2048,2048]{1,0:T(8,128)(2,1)}, bf16[2048,704]{1,0:T(8,128)(2,1)}, bf16[2048,704]{1,0:T(8,128)(2,1)}, bf16[2048,704]{1,0:T(8,128)(2,1)}, b...) custom-call(bf16[2048,2176]{1,0:T(8,128)(2,1)} %all-gather.19.cloned.1.call-done.rows, f32[2048,704]{1,0:T(8,128)} %copy-done.58, ...), custom_call_target="tpu_custom_call" | custom-call | flops 23622320128 | bytes 62914560 | tf_op jit(solution)/shard_map/pallas_call | solution.py:667
  613.5 10.2 fusion.122
  623.7 10.7 convolution_add_fusion
  634.5 8.8 convolution_convert_fusion
  643.3 11.2 convolution_convert_fusion.1
  654.4 11.8 fusion.2
  666.2 9.7 fusion
  676.0 11.0 fusion.14
  687.0 8.5 fusion.17
  723.0 6.5 reduce-scatter.11.cloned.1.call-done
  743.0 11.6 collective-permute-start.35
  756.3 16.0 %collective-permute-done.30.refs_2_ = bf16[64,2176]{1,0:T(8,128)(2,1)} collective-permute-done((bf16[64,2176]{1,0:T(8,128)(2,1)}, bf16[64,2176]{1,0:T(8,128)(2,1)}, u32[]{:S(2)}, u32[]{:S(2)}) %collective-permute-start.30) | collective-permute-done | bytes 278560 | tf_op jit(solution)/shard_map/ppermute | solution.py:58
  772.3 10.8 collective-permute-done.36.refs_6_
  791.5 5.4 shard_map.272
  804.1 18.6 %collective-permute-done.39 = bf16[64,2048]{1,0:T(8,128)(2,1)S(1)} collective-permute-done((bf16[64,2048]{1,0:T(8,128)(2,1)S(1)}, bf16[64,2048]{1,0:T(8,128)(2,1)S(1)}, u32[]{:S(2)}, u32[]{:S(2)}) %collective-permute-start.39) | collective-permute-done | bytes 262176 | tf_op jit(solution)/shard_map/ppermute | solution.py:58
  826.3 6.0 collective-permute-done.41
  832.3 14.4 %collective-permute-done.42 = bf16[64,2048]{1,0:T(8,128)(2,1)S(1)} collective-permute-done((bf16[64,2048]{1,0:T(8,128)(2,1)S(1)}, bf16[64,2048]{1,0:T(8,128)(2,1)S(1)}, u32[]{:S(2)}, u32[]{:S(2)}) %collective-permute-start.42) | collective-permute-done | bytes 262176 | tf_op jit(solution)/shard_map/ppermute | solution.py:58
  848.3 22.6 %collective-permute-done.45 = bf16[256,2048]{1,0:T(8,128)(2,1)S(1)} collective-permute-done((bf16[256,2048]{1,0:T(8,128)(2,1)S(1)}, bf16[256,2048]{1,0:T(8,128)(2,1)S(1)}, u32[]{:S(2)}, u32[]{:S(2)}) %collective-permute-start.45) | collective-permute-done | bytes 1048608 | tf_op jit(solution)/shard_map/ppermute | solution.py:44
  875.5 9.6 convolution_convert_fusion.2
  885.1 10.6 fusion.34
  898.5 48.5 %shard_map.273 = (bf16[8,128,1024]{2,1,0:T(8,128)(2,1)S(1)}, bf16[8,256,1024]{2,1,0:T(8,128)(2,1)}, bf16[8,256,1024]{2,1,0:T(8,128)(2,1)}) custom-call(s32[8]{0:T(128)S(1)} %copy-done.57, s32[8,128,2]{2,1,0:T(8,128)S(1)} %copy-done.26, bf16[8,128,1024]{2,1,0:T(8,128)(2,1)} %get-tuple-element.132.query, bf16[8,256,2048]{2,1,0:T(8,128)(2,1)} %get-tuple-element.133.keys.values, ...), custom_call_target="tpu_custom_call" | custom-call | flops 21474836480 | bytes 33554432 | tf_op jit(solution)/shard_map/pallas_call | solution.py:398
  946.9 13.4 %bitcast_convert_fusion.2 = bf16[2048,1024]{1,0:T(8,128)(2,1)S(1)} fusion(bf16[8,256,2048]{2,1,0:T(8,128)(2,1)} %get-tuple-element.131, bf16[8,256,1024]{2,1,0:T(8,128)(2,1)} %get-tuple-element.215.k_grad), kind=kOutput, calls=%fused_computation.2 | convolution fusion | flops 8592031744 | bytes 16777216 | tf_op jit(solution)/shard_map/dot_general | solution.py:28
  964.8 12.2 bitcast_convert_fusion.1
  1001.5 12.9 bitcast_convert_fusion
  1014.3 22.3 %shard_map.274 = (bf16[256,2048]{1,0:T(8,128)(2,1)}, bf16[256,2048]{1,0:T(8,128)(2,1)}, bf16[256,2048]{1,0:T(8,128)(2,1)}, bf16[256,2048]{1,0:T(8,128)(2,1)}) custom-call(s32[1]{0:T(128)} %bitcast.4.place, bf16[8,256,1024]{2,1,0:T(8,128)(2,1)} %get-tuple-element.215.k_grad, bf16[8,256,1024]{2,1,0:T(8,128)(2,1)} %get-tuple-element.216.v_grad, ...), custom_call_target="tpu_custom_call" | custom-call | flops 12884901888 | bytes 25165824 | tf_op jit(solution)/shard_map/pallas_call | solution.py:616
  1070.1 22.4 %shard_map.275 = (bf16[256,2048]{1,0:T(8,128)(2,1)}, bf16[256,2048]{1,0:T(8,128)(2,1)}, bf16[256,2048]{1,0:T(8,128)(2,1)}, bf16[256,2048]{1,0:T(8,128)(2,1)}) custom-call(s32[1]{0:T(128)} %bitcast.4.place, bf16[8,256,1024]{2,1,0:T(8,128)(2,1)} %get-tuple-element.215.k_grad, bf16[8,256,1024]{2,1,0:T(8,128)(2,1)} %get-tuple-element.216.v_grad, ...), custom_call_target="tpu_custom_call" | custom-call | flops 12884901888 | bytes 25165824 | tf_op jit(solution)/shard_map/pallas_call | solution.py:616
  1092.5 11.9 collective-permute-done.50
  1105.1 6.4 collective-permute-done.51
  1125.5 3.7 collective-permute-done.53
  1132.5 19.1 %collective-permute-done.60 = bf16[128,2048]{1,0:T(8,128)(2,1)} collective-permute-done((bf16[128,2048]{1,0:T(8,128)(2,1)}, bf16[128,2048]{1,0:T(8,128)(2,1)}, u32[]{:S(2)}, u32[]{:S(2)}) %collective-permute-start.60) | collective-permute-done | bytes 524320 | tf_op jit(solution)/shard_map/ppermute | solution.py:126
  1151.6 14.1 %collective-permute-start.62 = (bf16[128,2048]{1,0:T(8,128)(2,1)S(1)}, bf16[128,2048]{1,0:T(8,128)(2,1)S(1)}, u32[]{:S(2)}, u32[]{:S(2)}) collective-permute-start(bf16[128,2048]{1,0:T(8,128)(2,1)S(1)} %copy-done.87), channel_id=1, source_target_pairs={{0,6},{2,0},{4,2},{6,4},{1,7},{3,1},{5,3},{7,5},{8,14},{10,8},{12,... | collective-permute-start | bytes 1572872 | tf_op jit(solution)/shard_map/ppermute | solution.py:127
  1168.7 14.3 %collective-permute-start.61 = (bf16[256,2048]{1,0:T(8,128)(2,1)}, bf16[256,2048]{1,0:T(8,128)(2,1)}, u32[]{:S(2)}, u32[]{:S(2)}) collective-permute-start(bf16[256,2048]{1,0:T(8,128)(2,1)} %pad_maximum_fusion.4), channel_id=1, source_target_pairs={{0,2},{2,4},{4,6},{6,0},{1,3},{3,5},{5,7},{7,1},{8,10},{10,12},{12... | collective-permute-start | bytes 3145736 | tf_op jit(solution)/shard_map/ppermute | solution.py:142
  1184.7 15.3 %collective-permute-done.62 = bf16[128,2048]{1,0:T(8,128)(2,1)S(1)} collective-permute-done((bf16[128,2048]{1,0:T(8,128)(2,1)S(1)}, bf16[128,2048]{1,0:T(8,128)(2,1)S(1)}, u32[]{:S(2)}, u32[]{:S(2)}) %collective-permute-start.62) | collective-permute-done | bytes 524320 | tf_op jit(solution)/shard_map/ppermute | solution.py:127
  1204.5 4.0 fusion.56
  1210.4 3.9 collective-permute-done.61
  1214.2 31.1 %collective-permute-done.63 = bf16[256,2048]{1,0:T(8,128)(2,1)} collective-permute-done((bf16[256,2048]{1,0:T(8,128)(2,1)}, bf16[256,2048]{1,0:T(8,128)(2,1)}, u32[]{:S(2)}, u32[]{:S(2)}) %collective-permute-start.63) | collective-permute-done | bytes 1048608 | tf_op jit(solution)/shard_map/ppermute | solution.py:143
  1245.4 4.2 multiply_reduce_fusion
  1261.3 7.6 collective-permute-done.69.refs_2_
  1269.0 10.9 collective-permute-done.70.refs_3_
  1292.8 7.7 collective-permute-done.71.refs_1_
  (602 shorter events, 318.6 us)
Async XLA Ops:
  7.2 191.4 %all-gather.9.cloned.1.call-start = ((), (), s32[]{:S(2)}) async-start(), calls=%async_computation.6 | async-start | bytes 8192000 | tf_op jit(solution)/shard_map/all_gather | solution.py:916
  16.4 183.3 %all-gather.11.cloned.1.call-start = ((), (), s32[]{:S(2)}) async-start(), calls=%async_computation.7 | async-start | bytes 8192000 | tf_op jit(solution)/shard_map/all_gather | solution.py:917
  16.4 38.9 %collective-permute-start = (bf16[256,3200]{1,0:T(8,128)(2,1)S(1)}, bf16[256,3200]{1,0:T(8,128)(2,1)}, u32[]{:S(2)}, u32[]{:S(2)}) collective-permute-start(bf16[256,3200]{1,0:T(8,128)(2,1)S(1)} %get-tuple-element.130), channel_id=1, source_target_pairs={{0,1},{1,0},{2,3},{3,2},{4,5},{5,4},{6,7},{7,6},{8,9},{9,8},{10,11... | collective-permute-start | bytes 4915208 | tf_op jit(solution)/shard_map/ppermute | solution.py:44
  55.4 217.9 %all-gather.21.cloned.1.call-start = ((), (), s32[]{:S(2)}) async-start(), calls=%async_computation.19 | async-start | bytes 5242880 | tf_op jit(solution)/shard_map/all_gather | solution.py:918
  57.0 58.8 %collective-permute-start.5 = (bf16[256,2176]{1,0:T(8,128)(2,1)}, bf16[256,2176]{1,0:T(8,128)(2,1)}, u32[]{:S(2)}, u32[]{:S(2)}) collective-permute-start(bf16[256,2176]{1,0:T(8,128)(2,1)} %pad_maximum_fusion.2.refs_0_), channel_id=1, source_target_pairs={{0,1},{1,0},{2,3},{3,2},{4,5},{5,4},{6,7},{7,6},{8,9},{9,8},{10,11... | collective-permute-start | bytes 3342344 | tf_op jit(solution)/shard_map/ppermute | solution.py:44
  58.7 29.6 %collective-permute-start.2 = (bf16[256,2176]{1,0:T(8,128)(2,1)}, bf16[256,2176]{1,0:T(8,128)(2,1)}, u32[]{:S(2)}, u32[]{:S(2)}) collective-permute-start(bf16[256,2176]{1,0:T(8,128)(2,1)} %pad_maximum_fusion.2.refs_0_), channel_id=1, source_target_pairs={{0,2},{2,4},{4,6},{6,0},{1,3},{3,5},{5,7},{7,1},{8,10},{10,12},{12... | collective-permute-start | bytes 3342344 | tf_op jit(solution)/shard_map/ppermute | solution.py:86
  60.3 50.7 %collective-permute-start.1 = (bf16[256,2176]{1,0:T(8,128)(2,1)}, bf16[256,2176]{1,0:T(8,128)(2,1)}, u32[]{:S(2)}, u32[]{:S(2)}) collective-permute-start(bf16[256,2176]{1,0:T(8,128)(2,1)} %pad_maximum_fusion.2.refs_0_), channel_id=1, source_target_pairs={{0,6},{2,0},{4,2},{6,4},{1,7},{3,1},{5,3},{7,5},{8,14},{10,8},{12,... | collective-permute-start | bytes 3342344 | tf_op jit(solution)/shard_map/ppermute | solution.py:85
  62.6 292.7 %all-gather.15.cloned.1.call-start = ((), (), s32[]{:S(2)}) async-start(), calls=%async_computation.9 | async-start | bytes 9437184 | tf_op jit(solution)/shard_map/all_gather | solution.py:74
  90.2 35.0 %collective-permute-start.3 = (bf16[128,2176]{1,0:T(8,128)(2,1)}, bf16[128,2176]{1,0:T(8,128)(2,1)}, u32[]{:S(2)}, u32[]{:S(2)}) collective-permute-start(bf16[128,2176]{1,0:T(8,128)(2,1)} %slice.387), channel_id=1, source_target_pairs={{0,2},{2,4},{4,6},{6,0},{1,3},{3,5},{5,7},{7,1},{8,10},{10,12},{12... | collective-permute-start | bytes 1671176 | tf_op jit(solution)/shard_map/ppermute | solution.py:89
  116.7 27.9 %collective-permute-start.8 = (bf16[256,2176]{1,0:T(8,128)(2,1)}, bf16[256,2176]{1,0:T(8,128)(2,1)}, u32[]{:S(2)}, u32[]{:S(2)}) collective-permute-start(bf16[256,2176]{1,0:T(8,128)(2,1)} %collective-permute-done.2.refs_3_), channel_id=1, source_target_pairs={{0,1},{1,0},{2,3},{3,2},{4,5},{5,4},{6,7},{7,6},{8,9},{9,8},{10,11... | collective-permute-start | bytes 3342344 | tf_op jit(solution)/shard_map/ppermute | solution.py:44
  117.2 51.2 %collective-permute-start.6 = (bf16[256,2176]{1,0:T(8,128)(2,1)}, bf16[256,2176]{1,0:T(8,128)(2,1)}, u32[]{:S(2)}, u32[]{:S(2)}) collective-permute-start(bf16[256,2176]{1,0:T(8,128)(2,1)} %collective-permute-done.1.refs_1_), channel_id=1, source_target_pairs={{0,1},{1,0},{2,3},{3,2},{4,5},{5,4},{6,7},{7,6},{8,9},{9,8},{10,11... | collective-permute-start | bytes 3342344 | tf_op jit(solution)/shard_map/ppermute | solution.py:44
  135.8 51.2 %collective-permute-start.7 = (bf16[256,2176]{1,0:T(8,128)(2,1)}, bf16[256,2176]{1,0:T(8,128)(2,1)}, u32[]{:S(2)}, u32[]{:S(2)}) collective-permute-start(bf16[256,2176]{1,0:T(8,128)(2,1)} %constant_dynamic-update-slice_fusion.refs_2_), channel_id=1, source_target_pairs={{0,1},{1,0},{2,3},{3,2},{4,5},{5,4},{6,7},{7,6},{8,9},{9,8},{10,11... | collective-permute-start | bytes 3342344 | tf_op jit(solution)/shard_map/ppermute | solution.py:44
  189.4 49.4 %collective-permute-start.19 = (bf16[2,64,2048]{2,1,0:T(8,128)(2,1)}, bf16[2,64,2048]{2,1,0:T(8,128)(2,1)S(1)}, u32[]{:S(2)}, u32[]{:S(2)}) collective-permute-start(bf16[2,64,2048]{2,1,0:T(8,128)(2,1)} %get-tuple-element.286), channel_id=1, source_target_pairs={{0,2},{2,4},{4,6},{6,0},{1,3},{3,5},{5,7},{7,1},{8,10},{10,12},{12... | collective-permute-start | bytes 1572872 | tf_op jit(solution)/shard_map/ppermute | solution.py:58
  192.6 46.2 %collective-permute-start.18 = (bf16[2,64,2048]{2,1,0:T(8,128)(2,1)}, bf16[2,64,2048]{2,1,0:T(8,128)(2,1)}, u32[]{:S(2)}, u32[]{:S(2)}) collective-permute-start(bf16[2,64,2048]{2,1,0:T(8,128)(2,1)} %get-tuple-element.287), channel_id=1, source_target_pairs={{0,4},{2,6},{4,0},{6,2},{1,5},{3,7},{5,1},{7,3},{8,12},{10,14},{12... | collective-permute-start | bytes 1572872 | tf_op jit(solution)/shard_map/ppermute | solution.py:58
  193.6 45.2 %collective-permute-start.17 = (bf16[2,64,2048]{2,1,0:T(8,128)(2,1)}, bf16[2,64,2048]{2,1,0:T(8,128)(2,1)}, u32[]{:S(2)}, u32[]{:S(2)}) collective-permute-start(bf16[2,64,2048]{2,1,0:T(8,128)(2,1)} %get-tuple-element.288), channel_id=1, source_target_pairs={{0,6},{2,0},{4,2},{6,4},{1,7},{3,1},{5,3},{7,5},{8,14},{10,8},{12,... | collective-permute-start | bytes 1572872 | tf_op jit(solution)/shard_map/ppermute | solution.py:58
  241.8 133.8 %all-gather.13.cloned.1.call-start = ((), (), s32[]{:S(2)}) async-start(), calls=%async_computation.8 | async-start | bytes 9437184 | tf_op jit(solution)/shard_map/all_gather | solution.py:74
  242.4 278.1 %all-gather.17.cloned.1.call-start = ((), (), s32[]{:S(2)}) async-start(), calls=%async_computation.10 | async-start | bytes 10027008 | tf_op jit(solution)/shard_map/all_gather | solution.py:74
  279.2 36.0 %collective-permute-start.9 = (bf16[256,2048]{1,0:T(8,128)(2,1)}, bf16[256,2048]{1,0:T(8,128)(2,1)S(1)}, u32[]{:S(2)}, u32[]{:S(2)}) collective-permute-start(bf16[256,2048]{1,0:T(8,128)(2,1)} %slice.407), channel_id=1, source_target_pairs={{0,1},{1,0},{2,3},{3,2},{4,5},{5,4},{6,7},{7,6},{8,9},{9,8},{10,11... | collective-permute-start | bytes 3145736 | tf_op jit(solution)/shard_map/ppermute | solution.py:44
  315.2 35.2 %collective-permute-start.13 = (bf16[256,2048]{1,0:T(8,128)(2,1)S(1)}, bf16[256,2048]{1,0:T(8,128)(2,1)S(1)}, u32[]{:S(2)}, u32[]{:S(2)}) collective-permute-start(bf16[256,2048]{1,0:T(8,128)(2,1)S(1)} %slice.417), channel_id=1, source_target_pairs={{0,1},{1,0},{2,3},{3,2},{4,5},{5,4},{6,7},{7,6},{8,9},{9,8},{10,11... | collective-permute-start | bytes 3145736 | tf_op jit(solution)/shard_map/ppermute | solution.py:44
  318.8 50.0 %collective-permute-start.12 = (bf16[64,2048]{1,0:T(8,128)(2,1)}, bf16[64,2048]{1,0:T(8,128)(2,1)S(1)}, u32[]{:S(2)}, u32[]{:S(2)}) collective-permute-start(bf16[64,2048]{1,0:T(8,128)(2,1)} %get-tuple-element.272), channel_id=1, source_target_pairs={{0,6},{2,0},{4,2},{6,4},{1,7},{3,1},{5,3},{7,5},{8,14},{10,8},{12,... | collective-permute-start | bytes 786440 | tf_op jit(solution)/shard_map/ppermute | solution.py:58
  322.3 66.7 %collective-permute-start.11 = (bf16[64,2048]{1,0:T(8,128)(2,1)}, bf16[64,2048]{1,0:T(8,128)(2,1)S(1)}, u32[]{:S(2)}, u32[]{:S(2)}) collective-permute-start(bf16[64,2048]{1,0:T(8,128)(2,1)} %get-tuple-element.273), channel_id=1, source_target_pairs={{0,4},{2,6},{4,0},{6,2},{1,5},{3,7},{5,1},{7,3},{8,12},{10,14},{12... | collective-permute-start | bytes 786440 | tf_op jit(solution)/shard_map/ppermute | solution.py:58
  322.3 67.4 %collective-permute-start.10 = (bf16[64,2048]{1,0:T(8,128)(2,1)}, bf16[64,2048]{1,0:T(8,128)(2,1)S(1)}, u32[]{:S(2)}, u32[]{:S(2)}) collective-permute-start(bf16[64,2048]{1,0:T(8,128)(2,1)} %get-tuple-element.274), channel_id=1, source_target_pairs={{0,2},{2,4},{4,6},{6,0},{1,3},{3,5},{5,7},{7,1},{8,10},{10,12},{12... | collective-permute-start | bytes 786440 | tf_op jit(solution)/shard_map/ppermute | solution.py:58
  351.7 38.8 %collective-permute-start.16 = (bf16[64,2048]{1,0:T(8,128)(2,1)}, bf16[64,2048]{1,0:T(8,128)(2,1)S(1)}, u32[]{:S(2)}, u32[]{:S(2)}) collective-permute-start(bf16[64,2048]{1,0:T(8,128)(2,1)} %get-tuple-element.268), channel_id=1, source_target_pairs={{0,6},{2,0},{4,2},{6,4},{1,7},{3,1},{5,3},{7,5},{8,14},{10,8},{12,... | collective-permute-start | bytes 786440 | tf_op jit(solution)/shard_map/ppermute | solution.py:58
  355.2 36.0 %collective-permute-start.15 = (bf16[64,2048]{1,0:T(8,128)(2,1)}, bf16[64,2048]{1,0:T(8,128)(2,1)S(1)}, u32[]{:S(2)}, u32[]{:S(2)}) collective-permute-start(bf16[64,2048]{1,0:T(8,128)(2,1)} %get-tuple-element.269), channel_id=1, source_target_pairs={{0,4},{2,6},{4,0},{6,2},{1,5},{3,7},{5,1},{7,3},{8,12},{10,14},{12... | collective-permute-start | bytes 786440 | tf_op jit(solution)/shard_map/ppermute | solution.py:58
  368.8 23.1 %collective-permute-start.14 = (bf16[64,2048]{1,0:T(8,128)(2,1)S(1)}, bf16[64,2048]{1,0:T(8,128)(2,1)S(1)}, u32[]{:S(2)}, u32[]{:S(2)}) collective-permute-start(bf16[64,2048]{1,0:T(8,128)(2,1)S(1)} %copy-done.88), channel_id=1, source_target_pairs={{0,2},{2,4},{4,6},{6,0},{1,3},{3,5},{5,7},{7,1},{8,10},{10,12},{12... | collective-permute-start | bytes 786440 | tf_op jit(solution)/shard_map/ppermute | solution.py:58
  411.8 24.3 %collective-permute-start.21 = (bf16[64,2176]{1,0:T(8,128)(2,1)S(1)}, bf16[64,2176]{1,0:T(8,128)(2,1)S(1)}, u32[]{:S(2)}, u32[]{:S(2)}) collective-permute-start(bf16[64,2176]{1,0:T(8,128)(2,1)S(1)} %get-tuple-element.161), channel_id=1, source_target_pairs={{0,4},{2,6},{4,0},{6,2},{1,5},{3,7},{5,1},{7,3},{8,12},{10,14},{12... | collective-permute-start | bytes 835592 | tf_op jit(solution)/shard_map/ppermute | solution.py:58
  411.8 25.0 %collective-permute-start.22 = (bf16[64,2176]{1,0:T(8,128)(2,1)S(1)}, bf16[64,2176]{1,0:T(8,128)(2,1)S(1)}, u32[]{:S(2)}, u32[]{:S(2)}) collective-permute-start(bf16[64,2176]{1,0:T(8,128)(2,1)S(1)} %get-tuple-element.162), channel_id=1, source_target_pairs={{0,2},{2,4},{4,6},{6,0},{1,3},{3,5},{5,7},{7,1},{8,10},{10,12},{12... | collective-permute-start | bytes 835592 | tf_op jit(solution)/shard_map/ppermute | solution.py:58
  437.6 26.3 %collective-permute-start.24 = (bf16[64,2176]{1,0:T(8,128)(2,1)}, bf16[64,2176]{1,0:T(8,128)(2,1)S(1)}, u32[]{:S(2)}, u32[]{:S(2)}) collective-permute-start(bf16[64,2176]{1,0:T(8,128)(2,1)} %copy-done.54), channel_id=1, source_target_pairs={{0,4},{2,6},{4,0},{6,2},{1,5},{3,7},{5,1},{7,3},{8,12},{10,14},{12... | collective-permute-start | bytes 835592 | tf_op jit(solution)/shard_map/ppermute | solution.py:58
  439.6 24.3 %collective-permute-start.25 = (bf16[64,2176]{1,0:T(8,128)(2,1)}, bf16[64,2176]{1,0:T(8,128)(2,1)S(1)}, u32[]{:S(2)}, u32[]{:S(2)}) collective-permute-start(bf16[64,2176]{1,0:T(8,128)(2,1)} %copy-done.53), channel_id=1, source_target_pairs={{0,2},{2,4},{4,6},{6,0},{1,3},{3,5},{5,7},{7,1},{8,10},{10,12},{12... | collective-permute-start | bytes 835592 | tf_op jit(solution)/shard_map/ppermute | solution.py:58
  466.0 113.6 %all-gather.19.cloned.1.call-start = ((), (), s32[]{:S(2)}) async-start(), calls=%async_computation.12 | async-start | bytes 10027008 | tf_op jit(solution)/shard_map/all_gather | solution.py:74
  466.7 228.7 %reduce-scatter.7.cloned.1.call-start = ((), (), s32[]{:S(2)}) async-start(), calls=%async_computation.11 | async-start | bytes 9437184 | tf_op jit(solution)/shard_map/reduce_scatter | solution.py:78
  554.3 175.2 %reduce-scatter.11.cloned.1.call-start = ((), (), s32[]{:S(2)}) async-start(), calls=%async_computation.14 | async-start | bytes 9437184 | tf_op jit(solution)/shard_map/reduce_scatter | solution.py:78
  613.5 282.8 %reduce-scatter.9.cloned.1.call-start = ((), (), s32[]{:S(2)}) async-start(), calls=%async_computation.13 | async-start | bytes 9437184 | tf_op jit(solution)/shard_map/reduce_scatter | solution.py:78
  695.5 301.1 %reduce-scatter.13.cloned.1.call-start = ((), (), s32[]{:S(2)}) async-start(), calls=%async_computation.15 | async-start | bytes 9437184 | tf_op jit(solution)/shard_map/reduce_scatter | solution.py:78
  735.2 37.1 %collective-permute-start.30 = (bf16[64,2176]{1,0:T(8,128)(2,1)}, bf16[64,2176]{1,0:T(8,128)(2,1)}, u32[]{:S(2)}, u32[]{:S(2)}) collective-permute-start(bf16[64,2176]{1,0:T(8,128)(2,1)} %get-tuple-element.297), channel_id=1, source_target_pairs={{0,4},{2,6},{4,0},{6,2},{1,5},{3,7},{5,1},{7,3},{8,12},{10,14},{12... | collective-permute-start | bytes 835592 | tf_op jit(solution)/shard_map/ppermute | solution.py:58
  735.2 37.1 %collective-permute-start.29 = (bf16[64,2176]{1,0:T(8,128)(2,1)}, bf16[64,2176]{1,0:T(8,128)(2,1)}, u32[]{:S(2)}, u32[]{:S(2)}) collective-permute-start(bf16[64,2176]{1,0:T(8,128)(2,1)} %get-tuple-element.298), channel_id=1, source_target_pairs={{0,2},{2,4},{4,6},{6,0},{1,3},{3,5},{5,7},{7,1},{8,10},{10,12},{12... | collective-permute-start | bytes 835592 | tf_op jit(solution)/shard_map/ppermute | solution.py:58
  737.4 34.9 %collective-permute-start.37 = (bf16[64,2176]{1,0:T(8,128)(2,1)}, bf16[64,2176]{1,0:T(8,128)(2,1)}, u32[]{:S(2)}, u32[]{:S(2)}) collective-permute-start(bf16[64,2176]{1,0:T(8,128)(2,1)} %get-tuple-element.292), channel_id=1, source_target_pairs={{0,6},{2,0},{4,2},{6,4},{1,7},{3,1},{5,3},{7,5},{8,14},{10,8},{12,... | collective-permute-start | bytes 835592 | tf_op jit(solution)/shard_map/ppermute | solution.py:58
  740.2 42.9 %collective-permute-start.36 = (bf16[64,2176]{1,0:T(8,128)(2,1)}, bf16[64,2176]{1,0:T(8,128)(2,1)}, u32[]{:S(2)}, u32[]{:S(2)}) collective-permute-start(bf16[64,2176]{1,0:T(8,128)(2,1)} %get-tuple-element.293), channel_id=1, source_target_pairs={{0,4},{2,6},{4,0},{6,2},{1,5},{3,7},{5,1},{7,3},{8,12},{10,14},{12... | collective-permute-start | bytes 835592 | tf_op jit(solution)/shard_map/ppermute | solution.py:58
  743.0 40.0 %collective-permute-start.35 = (bf16[64,2176]{1,0:T(8,128)(2,1)}, bf16[64,2176]{1,0:T(8,128)(2,1)}, u32[]{:S(2)}, u32[]{:S(2)}) collective-permute-start(bf16[64,2176]{1,0:T(8,128)(2,1)} %get-tuple-element.294), channel_id=1, source_target_pairs={{0,2},{2,4},{4,6},{6,0},{1,3},{3,5},{5,7},{7,1},{8,10},{10,12},{12... | collective-permute-start | bytes 835592 | tf_op jit(solution)/shard_map/ppermute | solution.py:58
  797.0 25.8 %collective-permute-start.39 = (bf16[64,2048]{1,0:T(8,128)(2,1)S(1)}, bf16[64,2048]{1,0:T(8,128)(2,1)S(1)}, u32[]{:S(2)}, u32[]{:S(2)}) collective-permute-start(bf16[64,2048]{1,0:T(8,128)(2,1)S(1)} %get-tuple-element.194), channel_id=1, source_target_pairs={{0,4},{2,6},{4,0},{6,2},{1,5},{3,7},{5,1},{7,3},{8,12},{10,14},{12... | collective-permute-start | bytes 786440 | tf_op jit(solution)/shard_map/ppermute | solution.py:58
  800.0 22.8 %collective-permute-start.40 = (bf16[64,2048]{1,0:T(8,128)(2,1)S(1)}, bf16[64,2048]{1,0:T(8,128)(2,1)S(1)}, u32[]{:S(2)}, u32[]{:S(2)}) collective-permute-start(bf16[64,2048]{1,0:T(8,128)(2,1)S(1)} %get-tuple-element.195), channel_id=1, source_target_pairs={{0,2},{2,4},{4,6},{6,0},{1,3},{3,5},{5,7},{7,1},{8,10},{10,12},{12... | collective-permute-start | bytes 786440 | tf_op jit(solution)/shard_map/ppermute | solution.py:58
  822.8 24.0 %collective-permute-start.44 = (bf16[256,2048]{1,0:T(8,128)(2,1)S(1)}, bf16[256,2048]{1,0:T(8,128)(2,1)S(1)}, u32[]{:S(2)}, u32[]{:S(2)}) collective-permute-start(bf16[256,2048]{1,0:T(8,128)(2,1)S(1)} %constant_dynamic-update-slice_fusion.6), channel_id=1, source_target_pairs={{0,1},{1,0},{2,3},{3,2},{4,5},{5,4},{6,7},{7,6},{8,9},{9,8},{10,11... | collective-permute-start | bytes 3145736 | tf_op jit(solution)/shard_map/ppermute | solution.py:44
  846.9 24.1 %collective-permute-start.45 = (bf16[256,2048]{1,0:T(8,128)(2,1)S(1)}, bf16[256,2048]{1,0:T(8,128)(2,1)S(1)}, u32[]{:S(2)}, u32[]{:S(2)}) collective-permute-start(bf16[256,2048]{1,0:T(8,128)(2,1)S(1)} %constant_dynamic-update-slice_fusion.10), channel_id=1, source_target_pairs={{0,1},{1,0},{2,3},{3,2},{4,5},{5,4},{6,7},{7,6},{8,9},{9,8},{10,11... | collective-permute-start | bytes 3145736 | tf_op jit(solution)/shard_map/ppermute | solution.py:44
  873.1 247.3 %reduce-scatter.17.cloned.1.call-start = ((), (), s32[]{:S(2)}) async-start(), calls=%async_computation.18 | async-start | bytes 5242880 | tf_op jit(solution)/shard_map/reduce_scatter | solution.py:1062
  895.8 312.7 %all-reduce.6.cloned.1.call-start = ((), (), s32[]{:S(2)}) async-start(), calls=%async_computation.16 | async-start | bytes 4194304 | tf_op jit(solution)/shard_map/psum | solution.py:1091
  963.5 25.2 %collective-permute-start.46 = (bf16[2,512,1024]{2,1,0:T(8,128)(2,1)}, bf16[2,512,1024]{2,1,0:T(8,128)(2,1)}, u32[]{:S(2)}, u32[]{:S(2)}) collective-permute-start(bf16[2,512,1024]{2,1,0:T(8,128)(2,1)} %dynamic-slice_bitcast_fusion.1), channel_id=1, source_target_pairs={{0,8},{8,0},{16,24},{24,16},{1,9},{9,1},{17,25},{25,17},{2,10},{10... | collective-permute-start | bytes 6291464 | tf_op jit(solution)/shard_map/ppermute | solution.py:48
  991.7 50.8 %collective-permute-start.47 = (bf16[512,1024]{1,0:T(8,128)(2,1)}, bf16[512,1024]{1,0:T(8,128)(2,1)}, u32[]{:S(2)}, u32[]{:S(2)}) collective-permute-start(bf16[512,1024]{1,0:T(8,128)(2,1)} %fusion.32), channel_id=1, source_target_pairs={{0,16},{8,24},{16,0},{24,8},{1,17},{9,25},{17,1},{25,9},{2,18},{10... | collective-permute-start | bytes 3145736 | tf_op jit(solution)/shard_map/ppermute | solution.py:52
  996.0 44.0 %collective-permute-start.49 = (bf16[512,1024]{1,0:T(8,128)(2,1)}, bf16[512,1024]{1,0:T(8,128)(2,1)}, u32[]{:S(2)}, u32[]{:S(2)}) collective-permute-start(bf16[512,1024]{1,0:T(8,128)(2,1)} %fusion.31), channel_id=1, source_target_pairs={{0,16},{8,24},{16,0},{24,8},{1,17},{9,25},{17,1},{25,9},{2,18},{10... | collective-permute-start | bytes 3145736 | tf_op jit(solution)/shard_map/ppermute | solution.py:52
  1046.5 240.4 %reduce-scatter.15.cloned.1.call-start = ((), (), s32[]{:S(2)}) async-start(), calls=%async_computation.17 | async-start | bytes 5242880 | tf_op jit(solution)/shard_map/reduce_scatter | solution.py:1079
  1061.8 52.2 %collective-permute-start.56 = (bf16[256,2048]{1,0:T(8,128)(2,1)}, bf16[256,2048]{1,0:T(8,128)(2,1)}, u32[]{:S(2)}, u32[]{:S(2)}) collective-permute-start(bf16[256,2048]{1,0:T(8,128)(2,1)} %get-tuple-element.221), channel_id=1, source_target_pairs={{0,1},{1,0},{2,3},{3,2},{4,5},{5,4},{6,7},{7,6},{8,9},{9,8},{10,11... | collective-permute-start | bytes 3145736 | tf_op jit(solution)/shard_map/ppermute | solution.py:44
  1065.1 47.1 %collective-permute-start.52 = (bf16[64,2048]{1,0:T(8,128)(2,1)S(1)}, bf16[64,2048]{1,0:T(8,128)(2,1)S(1)}, u32[]{:S(2)}, u32[]{:S(2)}) collective-permute-start(bf16[64,2048]{1,0:T(8,128)(2,1)S(1)} %get-tuple-element.310), channel_id=1, source_target_pairs={{0,6},{2,0},{4,2},{6,4},{1,7},{3,1},{5,3},{7,5},{8,14},{10,8},{12,... | collective-permute-start | bytes 786440 | tf_op jit(solution)/shard_map/ppermute | solution.py:58
  1065.1 46.4 %collective-permute-start.51 = (bf16[64,2048]{1,0:T(8,128)(2,1)S(1)}, bf16[64,2048]{1,0:T(8,128)(2,1)S(1)}, u32[]{:S(2)}, u32[]{:S(2)}) collective-permute-start(bf16[64,2048]{1,0:T(8,128)(2,1)S(1)} %get-tuple-element.311), channel_id=1, source_target_pairs={{0,4},{2,6},{4,0},{6,2},{1,5},{3,7},{5,1},{7,3},{8,12},{10,14},{12... | collective-permute-start | bytes 786440 | tf_op jit(solution)/shard_map/ppermute | solution.py:58
  1068.1 36.3 %collective-permute-start.50 = (bf16[64,2048]{1,0:T(8,128)(2,1)S(1)}, bf16[64,2048]{1,0:T(8,128)(2,1)S(1)}, u32[]{:S(2)}, u32[]{:S(2)}) collective-permute-start(bf16[64,2048]{1,0:T(8,128)(2,1)S(1)} %get-tuple-element.312), channel_id=1, source_target_pairs={{0,2},{2,4},{4,6},{6,0},{1,3},{3,5},{5,7},{7,1},{8,10},{10,12},{12... | collective-permute-start | bytes 786440 | tf_op jit(solution)/shard_map/ppermute | solution.py:58
  1114.0 51.8 %collective-permute-start.57 = (bf16[256,2048]{1,0:T(8,128)(2,1)}, bf16[256,2048]{1,0:T(8,128)(2,1)}, u32[]{:S(2)}, u32[]{:S(2)}) collective-permute-start(bf16[256,2048]{1,0:T(8,128)(2,1)} %get-tuple-element.230), channel_id=1, source_target_pairs={{0,1},{1,0},{2,3},{3,2},{4,5},{5,4},{6,7},{7,6},{8,9},{9,8},{10,11... | collective-permute-start | bytes 3145736 | tf_op jit(solution)/shard_map/ppermute | solution.py:44
  1118.2 33.4 %collective-permute-start.60 = (bf16[128,2048]{1,0:T(8,128)(2,1)}, bf16[128,2048]{1,0:T(8,128)(2,1)}, u32[]{:S(2)}, u32[]{:S(2)}) collective-permute-start(bf16[128,2048]{1,0:T(8,128)(2,1)} %get-tuple-element.280), channel_id=1, source_target_pairs={{0,2},{2,4},{4,6},{6,0},{1,3},{3,5},{5,7},{7,1},{8,10},{10,12},{12... | collective-permute-start | bytes 1572872 | tf_op jit(solution)/shard_map/ppermute | solution.py:126
  1120.0 63.0 %collective-permute-start.58 = (bf16[256,2048]{1,0:T(8,128)(2,1)}, bf16[256,2048]{1,0:T(8,128)(2,1)}, u32[]{:S(2)}, u32[]{:S(2)}) collective-permute-start(bf16[256,2048]{1,0:T(8,128)(2,1)} %get-tuple-element.231), channel_id=1, source_target_pairs={{0,1},{1,0},{2,3},{3,2},{4,5},{5,4},{6,7},{7,6},{8,9},{9,8},{10,11... | collective-permute-start | bytes 3145736 | tf_op jit(solution)/shard_map/ppermute | solution.py:44
  1123.3 80.5 %collective-permute-start.55 = (bf16[64,2048]{1,0:T(8,128)(2,1)}, bf16[64,2048]{1,0:T(8,128)(2,1)S(1)}, u32[]{:S(2)}, u32[]{:S(2)}) collective-permute-start(bf16[64,2048]{1,0:T(8,128)(2,1)} %get-tuple-element.306), channel_id=1, source_target_pairs={{0,6},{2,0},{4,2},{6,4},{1,7},{3,1},{5,3},{7,5},{8,14},{10,8},{12,... | collective-permute-start | bytes 786440 | tf_op jit(solution)/shard_map/ppermute | solution.py:58
  1129.1 73.9 %collective-permute-start.54 = (bf16[64,2048]{1,0:T(8,128)(2,1)}, bf16[64,2048]{1,0:T(8,128)(2,1)S(1)}, u32[]{:S(2)}, u32[]{:S(2)}) collective-permute-start(bf16[64,2048]{1,0:T(8,128)(2,1)} %get-tuple-element.307), channel_id=1, source_target_pairs={{0,4},{2,6},{4,0},{6,2},{1,5},{3,7},{5,1},{7,3},{8,12},{10,14},{12... | collective-permute-start | bytes 786440 | tf_op jit(solution)/shard_map/ppermute | solution.py:58
  1151.6 48.4 %collective-permute-start.62 = (bf16[128,2048]{1,0:T(8,128)(2,1)S(1)}, bf16[128,2048]{1,0:T(8,128)(2,1)S(1)}, u32[]{:S(2)}, u32[]{:S(2)}) collective-permute-start(bf16[128,2048]{1,0:T(8,128)(2,1)S(1)} %copy-done.87), channel_id=1, source_target_pairs={{0,6},{2,0},{4,2},{6,4},{1,7},{3,1},{5,3},{7,5},{8,14},{10,8},{12,... | collective-permute-start | bytes 1572872 | tf_op jit(solution)/shard_map/ppermute | solution.py:127
  1168.7 45.5 %collective-permute-start.61 = (bf16[256,2048]{1,0:T(8,128)(2,1)}, bf16[256,2048]{1,0:T(8,128)(2,1)}, u32[]{:S(2)}, u32[]{:S(2)}) collective-permute-start(bf16[256,2048]{1,0:T(8,128)(2,1)} %pad_maximum_fusion.4), channel_id=1, source_target_pairs={{0,2},{2,4},{4,6},{6,0},{1,3},{3,5},{5,7},{7,1},{8,10},{10,12},{12... | collective-permute-start | bytes 3145736 | tf_op jit(solution)/shard_map/ppermute | solution.py:142
  1183.0 31.3 %collective-permute-start.59 = (bf16[256,2048]{1,0:T(8,128)(2,1)}, bf16[256,2048]{1,0:T(8,128)(2,1)}, u32[]{:S(2)}, u32[]{:S(2)}) collective-permute-start(bf16[256,2048]{1,0:T(8,128)(2,1)} %get-tuple-element.232), channel_id=1, source_target_pairs={{0,1},{1,0},{2,3},{3,2},{4,5},{5,4},{6,7},{7,6},{8,9},{9,8},{10,11... | collective-permute-start | bytes 3145736 | tf_op jit(solution)/shard_map/ppermute | solution.py:44
  1202.8 42.6 %collective-permute-start.63 = (bf16[256,2048]{1,0:T(8,128)(2,1)}, bf16[256,2048]{1,0:T(8,128)(2,1)}, u32[]{:S(2)}, u32[]{:S(2)}) collective-permute-start(bf16[256,2048]{1,0:T(8,128)(2,1)} %pad_maximum_fusion.5), channel_id=1, source_target_pairs={{0,6},{2,0},{4,2},{6,4},{1,7},{3,1},{5,3},{7,5},{8,14},{10,8},{12,... | collective-permute-start | bytes 3145736 | tf_op jit(solution)/shard_map/ppermute | solution.py:143
  1256.1 23.8 %collective-permute-start.70 = (bf16[256,1024]{1,0:T(8,128)(2,1)S(1)}, bf16[256,1024]{1,0:T(8,128)(2,1)S(1)}, u32[]{:S(2)}, u32[]{:S(2)}) collective-permute-start(bf16[256,1024]{1,0:T(8,128)(2,1)S(1)} %get-tuple-element.302), channel_id=1, source_target_pairs={{0,1},{1,0},{2,3},{3,2},{4,5},{5,4},{6,7},{7,6},{8,9},{9,8},{10,11... | collective-permute-start | bytes 1572872 | tf_op jit(solution)/shard_map/ppermute | solution.py:44
  1256.3 25.9 %collective-permute-start.66 = (f32[10,256]{1,0:T(8,128)S(1)}, f32[10,256]{1,0:T(8,128)S(1)}, u32[]{:S(2)}, u32[]{:S(2)}) collective-permute-start(f32[10,256]{1,0:T(8,128)S(1)} %dynamic-slice_bitcast_fusion.10), channel_id=1, source_target_pairs={{0,16},{8,24},{16,0},{24,8},{1,17},{9,25},{17,1},{25,9},{2,18},{10... | collective-permute-start | bytes 30728 | tf_op jit(solution)/shard_map/ppermute | solution.py:52
  (143 other events, 2018.7 us)
Sparse Core Ops, SparseCore 0:
  16.5 50.5 all-gather.8
  68.7 47.8 all-gather.10
  118.1 34.4 all-gather.20
  241.9 64.8 all-gather.14
  309.1 66.4 all-gather.12
  466.1 54.3 all-gather.16
  522.9 56.5 all-gather.18
  583.0 71.2 reduce-scatter.6
  658.2 71.2 reduce-scatter.10
  732.8 71.2 reduce-scatter.8
  873.2 71.4 reduce-scatter.12
  947.1 44.5 reduce-scatter.16
  1046.6 148.8 all-reduce.5
  1197.9 42.7 reduce-scatter.14

commit v3 on v2

--- a/solution.py
+++ b/solution.py
@@ -92,7 +92,7 @@
             axis=0,
         )
         own = [block, up, far, down]
-        return own + [swap_x(piece) for piece in own]
+        return own + [swap_x(piece) for piece in own], [up, down]
     e_at, s_at = lax.axis_index("expert"), lax.axis_index("seq")
     every = lax.all_gather(block, ("expert", "seq"), axis=0, tiled=False)
     wanted = [
@@ -100,7 +100,7 @@
         for sp in range(2)
         for r in range(count)
     ]
-    return [lax.dynamic_index_in_dim(every, at, 0, keepdims=False) for at in wanted]
+    return [lax.dynamic_index_in_dim(every, at, 0, keepdims=False) for at in wanted], []
 
 
 def group_scatter(own, other):
@@ -382,7 +382,7 @@
             jax.ShapeDtypeStruct(query.shape, BF),
             jax.ShapeDtypeStruct(log_shape, F32),
         ],
-        compiler_params=pltpu.CompilerParams(vmem_limit_bytes=50 << 20),
+        compiler_params=pltpu.CompilerParams(vmem_limit_bytes=60 << 20),
         cost_estimate=pl.CostEstimate(
             flops=flops, bytes_accessed=16 << 20, transcendentals=flops // 512
         ),
@@ -418,7 +418,7 @@
             jax.ShapeDtypeStruct(query.shape, BF),
         ]
         + [jax.ShapeDtypeStruct((total, tokens, width), BF)] * 2,
-        compiler_params=pltpu.CompilerParams(vmem_limit_bytes=50 << 20),
+        compiler_params=pltpu.CompilerParams(vmem_limit_bytes=60 << 20),
         cost_estimate=pl.CostEstimate(
             flops=flops, bytes_accessed=32 << 20, transcendentals=flops // 1280
         ),
@@ -506,7 +506,7 @@
             out_specs=[held_out((rows, 2 * half))] * count,
         ),
         out_shape=[jax.ShapeDtypeStruct((rows, 2 * half), dtype)] * count,
-        compiler_params=pltpu.CompilerParams(vmem_limit_bytes=40 << 20),
+        compiler_params=pltpu.CompilerParams(vmem_limit_bytes=60 << 20),
         cost_estimate=pl.CostEstimate(flops=0, bytes_accessed=4 << 20, transcendentals=0),
     )(s_at[None], *mine, *other)
 
@@ -580,7 +580,7 @@
             jax.ShapeDtypeStruct((total, tok, 2 * half), BF),
             jax.ShapeDtypeStruct((total, cap, half), BF),
         ],
-        compiler_params=pltpu.CompilerParams(vmem_limit_bytes=58 << 20),
+        compiler_params=pltpu.CompilerParams(vmem_limit_bytes=60 << 20),
         cost_estimate=pl.CostEstimate(flops=flops, bytes_accessed=40 << 20, transcendentals=0),
     )(s_at[None], gain, pick, keep, took, *x_parts)
 
@@ -629,7 +629,7 @@
             scratch_shapes=[pltpu.VMEM((blocks * tok, width), BF)],
         ),
         out_shape=[jax.ShapeDtypeStruct((tok, width), BF)] * count,
-        compiler_params=pltpu.CompilerParams(vmem_limit_bytes=58 << 20),
+        compiler_params=pltpu.CompilerParams(vmem_limit_bytes=60 << 20),
         cost_estimate=pl.CostEstimate(
             flops=6 * count * tok * width * half, bytes_accessed=24 << 20, transcendentals=0
         ),
@@ -675,7 +675,7 @@
         out_shape=[jax.ShapeDtypeStruct((every, width), BF)]
         + [jax.ShapeDtypeStruct((every, inner), BF)] * 4
         + [jax.ShapeDtypeStruct((every, 1), F32)],
-        compiler_params=pltpu.CompilerParams(vmem_limit_bytes=58 << 20),
+        compiler_params=pltpu.CompilerParams(vmem_limit_bytes=60 << 20),
         cost_estimate=pl.CostEstimate(
             flops=8 * every * width * inner,
             bytes_accessed=60 << 20,
@@ -758,7 +758,7 @@
             jax.ShapeDtypeStruct((tok, part * count), F32),
         ]
         + [jax.ShapeDtypeStruct((part, width + 128), BF)] * count,
-        compiler_params=pltpu.CompilerParams(vmem_limit_bytes=40 << 20),
+        compiler_params=pltpu.CompilerParams(vmem_limit_bytes=60 << 20),
         cost_estimate=pl.CostEstimate(
             flops=6 * tok * part * count * width, bytes_accessed=10 << 20, transcendentals=0
         ),
@@ -830,7 +830,7 @@
             jax.ShapeDtypeStruct((tok, 128), F32),
         ]
         + [jax.ShapeDtypeStruct((part, width), BF)] * count,
-        compiler_params=pltpu.CompilerParams(vmem_limit_bytes=40 << 20),
+        compiler_params=pltpu.CompilerParams(vmem_limit_bytes=60 << 20),
         cost_estimate=pl.CostEstimate(
             flops=6 * tok * part * count * width, bytes_accessed=12 << 20, transcendentals=0
         ),
@@ -851,7 +851,7 @@
         in_specs=[step_spec((size, width)), held_spec(down_w.shape)],
         out_specs=step_spec((size, inner)),
         out_shape=jax.ShapeDtypeStruct((every, inner), F32),
-        compiler_params=pltpu.CompilerParams(vmem_limit_bytes=40 << 20),
+        compiler_params=pltpu.CompilerParams(vmem_limit_bytes=60 << 20),
         cost_estimate=pl.CostEstimate(
             flops=2 * every * width * inner, bytes_accessed=18 << 20, transcendentals=0
         ),
@@ -912,9 +912,9 @@
     w_keep, w_give = weight_halves(
         s_at, (w_key, w_value, w_query[0]), jnp.concatenate(small, axis=1), dps
     )
-    x_parts = group_gather(x_marked)
+    x_parts, x_near = group_gather(x_marked)
     w_keep = lax.all_gather(w_keep, "dp", axis=0, tiled=True)
-    w_took = lax.all_gather(swap_x(w_give), "dp", axis=0, tiled=True)
+    w_took = lax.all_gather(after(swap_x(w_give), x_near), "dp", axis=0, tiled=True)
     out_w = lax.all_gather(w_out[0], "dp", axis=0, tiled=True)
 
     def feature_rows(first, last):
@@ -1009,21 +1009,22 @@
     in_pairs, out_parts = [], []
     grads = []
     for c in range(2):
-        found = expert_out[c]
+        found, g_part = expert_out[c], g_rows[c]
+        if c == 1:
+            found, g_part = after((found, g_part), in_pairs)
         grads.append(
             [
                 t_dot(found[0][:, :width], found[2]),
                 t_dot(found[0][:, :width], found[3]),
-                t_dot(found[4], g_rows[c]),
+                t_dot(found[4], g_part),
             ]
         )
         if c == 1:
             grads = [low + high for low, high in zip(*grads)]
-        in_sum = square_scatter(found[1])
-        out_parts.append(dot(after(found[5], expert_out[1][1]), down_w).astype(BF))
-        if c == 1:
-            in_sum, grads, out_parts = lax.optimization_barrier((in_sum, grads, out_parts))
-        dots = tiny_scatter(found[6].reshape(dps, seqs, chunk))
+        in_sum = square_scatter(expert_out[c][1])
+        out_parts.append(dot(after(expert_out[c][5], expert_out[1][1]), down_w).astype(BF))
+        in_sum, grads, out_parts = lax.optimization_barrier((in_sum, grads, out_parts))
+        dots = tiny_scatter(expert_out[c][6].reshape(dps, seqs, chunk))
         in_sum = jnp.concatenate([in_sum, in_columns(dots[:, None])], axis=1)
         in_pairs += z_rounds(pieces_of(in_sum), 1)
     grad_gate, grad_up, grad_down = grads
@@ -1056,11 +1057,10 @@
         [jnp.sum(jnp.where(hot, slot_dots, 0.0), axis=1, keepdims=True) for hot in attn_hot], axis=1
     )
     mixed_grad = dot_t(dh_rows, out_w).astype(BF).reshape(total, cap, half)
-    grad_out_w = t_dot(mixed.reshape(total * cap, half), dh_rows).astype(BF)
-    mixed_grad, grad_out_w = lax.optimization_barrier((mixed_grad, grad_out_w))
     mixed_grad = after(mixed_grad, out_sums[0])
-    grad_out_w = lax.psum_scatter(grad_out_w, "dp", scatter_dimension=0, tiled=True)
+    out_pairs = z_rounds(pieces_of(out_sums[0]), 1)
     q_grad, *both_grad = attend_back(index, info, query, both, logs, mixed_grad)
+    both_grad = after(both_grad, out_pairs)
 
     flat_normed = normed_all.reshape(total * tok, width)
     both_dots = [
@@ -1085,15 +1085,16 @@
         both_grads = [
             lax.psum_scatter(dots, "dp", scatter_dimension=0, tiled=False) for dots in both_dots
         ]
-    q_slots = after(q_slots, both_grads)
+    out_pairs += z_rounds(pieces_of(out_sums[1]), 1)
+    both_grads = after(both_grads, query_grads)
+    q_slots = after(q_slots, both_grads, out_pairs)
     in_own = project_back(s_at, both_grad, q_slots, w_keep, w_took, 0, experts, dps)
     one_sum, _ = group_scatter(in_own, in_other)
     shared = lax.psum(jnp.stack(both_grads), "expert")
-
-    out_sums = after(out_sums, both_grads)
-    out_pairs = []
-    for out_sum in out_sums:
-        out_pairs += z_rounds(pieces_of(out_sum), 1)
+    dh_rows = after(dh_rows, in_own)
+    grad_out_w = t_dot(mixed.reshape(total * cap, half), dh_rows).astype(BF)
+    grad_out_w = lax.psum_scatter(grad_out_w, "dp", scatter_dimension=0, tiled=True)
+
     out_pairs = jnp.concatenate(out_pairs, axis=0)
     mlp_high, mlp_low = in_two(mlp_mix)
     output = hidden + dot(mlp_high, out_pairs) + dot(mlp_low, out_pairs)
@@ -1115,6 +1116,7 @@
     input_grad, norm_one_grad = norm_back(x_in, norm_one, normed_one_grad)
     grad_x = (hidden_total + input_grad).astype(BF).reshape(seq_count, stretch, width)
 
+    norm_one_grad = after(norm_one_grad, shared)
     little = little_sum(
         jnp.concatenate(
             [norm_one_grad[None], router_one_grad.T, norm_two_grad, router_two_grad.T], axis=0

time: 1320 us -> 1210 us (0.917)
  local copies, waits for them, and re-layouts: 122 us -> 79.8 us
  starting transfers between devices: 133 us -> 102 us
  waiting for transfers between devices: 550 us -> 521 us
  Pallas kernels: 256 us -> 273 us
    all_gather x4, waiting for transfers between devices: 83.7 us -> 38 us  [square_gather(): return lax.all_gather(piece, ('dp', 'seq'), axis=0, tiled=True)]
    ppermute x5, waiting for transfers between devices: 8.51 us -> 42.6 us  [swap_y(): return lax.ppermute(value, 'dp', flip(4, 2))]
    unnamed x272 -> x260, local copies, waits for them, and re-layouts: 66.8 us -> 33.4 us
    ppermute x33, waiting for transfers between devices: 135 us -> 102 us  [z_rounds(): lax.ppermute(pieces[r], 'expert', ring(count, sign * r))]
    ppermute x1, waiting for transfers between devices: 31.1 us -> 0.01 us  [group_scatter(): from_above = lax.ppermute(down, 'expert', ring(count, -1))]
    reduce_scatter x4, waiting for transfers between devices: 6.54 us -> 34.8 us  [square_scatter(): lax.psum_scatter(parts, ('dp', 'seq'), scatter_dimension=0, tiled=True)]
    ppermute x1, waiting for transfers between devices: 3.87 us -> 21.8 us  [group_scatter(): from_below = lax.ppermute(up, 'expert', ring(count, 1))]
    ppermute x1, waiting for transfers between devices: 15.3 us -> 0.01 us  [group_scatter(): far_down = lax.ppermute(far[1], 'expert', ring(count, -1))]
  transfers between devices with their start and end apart: 86 -> 86, of which waited for: 45 -> 44; matrix products, arithmetic and copies ran while one was open for 23% -> 21% of each run, Pallas kernels for 19% -> 22%
where the time goes in v3:
time: 1210 us; the launch traced here: 1200 us
  waiting for transfers between devices  521 us (43%)
  Pallas kernels  273 us (23%)
  matrix products  165 us (14%)
  starting transfers between devices  102 us (8%)
  local copies, waits for them, and re-layouts  79.8 us (7%)
  other arithmetic  46.2 us (4%)
  between operations  16 us (1%)
    ppermute x19, waiting for transfers between devices, swap_x(): return lax.ppermute(value, 'seq', flip(2, 1))  202 us
    dot_general x11, matrix products, t_dot(): lax.dot_general(left, right, (((0,), (0,)), ((), ())), preferred_element_...  112 us
    ppermute x33, waiting for transfers between devices, z_rounds(): lax.ppermute(pieces[r], 'expert', ring(count, sign * r))  102 us
    pallas_call x2, Pallas kernels, expert_mlp(): pl.pallas_call(expert_kernel, grid=(every // size,), in_specs=[step_spec(...  67.8 us
    ppermute x33, starting transfers between devices, z_rounds(): lax.ppermute(pieces[r], 'expert', ring(count, sign * r))  59.8 us
    pallas_call x1, Pallas kernels, attend_back(): pl.pallas_call(functools.partial(attend_back_kernel, blocks=blocks), grid...  48.5 us
    pallas_call x2, Pallas kernels, project_back(): pl.pallas_call(functools.partial(back_kernel, dps=dps), grid_spec=pltpu.P...  44.8 us
    ppermute x5, waiting for transfers between devices, swap_y(): return lax.ppermute(value, 'dp', flip(4, 2))  42.6 us
  transfers between devices with their start and end apart: 86, of which 44 were waited for; matrix products, arithmetic and copies ran while one was open for 21% of the time, Pallas kernels for 22%

profile of v3, /device:TPU:0, one launch (start us, length us, event | category | flops | bytes accessed | tf_op | source)
XLA Modules:
  0.0 1202.5 jit_solution(5195267743509940177)
XLA Ops:
  20.0 3.7 collective-permute-start.1
  23.7 25.0 %collective-permute-done.1.refs_1_ = bf16[256,2176]{1,0:T(8,128)(2,1)S(1)} collective-permute-done((bf16[256,2176]{1,0:T(8,128)(2,1)S(1)}, bf16[256,2176]{1,0:T(8,128)(2,1)S(1)}, u32[]{:S(2)}, u32[]{:S(2)}) %collective-permute-start.1) | collective-permute-done | bytes 1114144 | tf_op jit(solution)/shard_map/ppermute | solution.py:85
  48.7 23.3 %collective-permute-done.2.refs_3_ = bf16[256,2176]{1,0:T(8,128)(2,1)S(1)} collective-permute-done((bf16[256,2176]{1,0:T(8,128)(2,1)S(1)}, bf16[256,2176]{1,0:T(8,128)(2,1)S(1)}, u32[]{:S(2)}, u32[]{:S(2)}) %collective-permute-start.2) | collective-permute-done | bytes 1114144 | tf_op jit(solution)/shard_map/ppermute | solution.py:86
  91.7 6.8 collective-permute-done.3
  100.4 7.5 collective-permute-done.4
  112.5 12.3 %collective-permute-done.6.refs_5_ = bf16[256,2176]{1,0:T(8,128)(2,1)} collective-permute-done((bf16[256,2176]{1,0:T(8,128)(2,1)}, bf16[256,2176]{1,0:T(8,128)(2,1)}, u32[]{:S(2)}, u32[]{:S(2)}) %collective-permute-start.6) | collective-permute-done | bytes 1114144 | tf_op jit(solution)/shard_map/ppermute | solution.py:44
  125.8 22.9 %collective-permute-done.8.refs_7_ = bf16[256,2176]{1,0:T(8,128)(2,1)} collective-permute-done((bf16[256,2176]{1,0:T(8,128)(2,1)}, bf16[256,2176]{1,0:T(8,128)(2,1)}, u32[]{:S(2)}, u32[]{:S(2)}) %collective-permute-start.8) | collective-permute-done | bytes 1114144 | tf_op jit(solution)/shard_map/ppermute | solution.py:44
  149.7 20.5 %collective-permute-done.7.refs_6_ = bf16[256,2176]{1,0:T(8,128)(2,1)} collective-permute-done((bf16[256,2176]{1,0:T(8,128)(2,1)}, bf16[256,2176]{1,0:T(8,128)(2,1)}, u32[]{:S(2)}, u32[]{:S(2)}) %collective-permute-start.7) | collective-permute-done | bytes 1114144 | tf_op jit(solution)/shard_map/ppermute | solution.py:44
  182.4 36.3 %shard_map.265 = (bf16[8,256,2048]{2,1,0:T(8,128)(2,1)}, bf16[8,256,2048]{2,1,0:T(8,128)(2,1)}, bf16[8,128,1024]{2,1,0:T(8,128)(2,1)}) custom-call(s32[1]{0:T(128)} %bitcast.4.place, f32[1,2048]{1,0:T(1,128)} %bitcast.327, bf16[8,128,256]{2,1,0:T(8,128)(2,1)} %fusion.41.pick, bf16[1024,3200]{1,0:T(8,128)(2,1)} %all-gather.9.cloned.1.call-done.keep, ...), custom_call_target="tpu_custom_call" | custom-call | flops 21474836480 | bytes 41943040 | tf_op jit(solution)/shard_map/pallas_call | solution.py:555
  223.6 27.5 %shard_map.266 = (bf16[8,128,1024]{2,1,0:T(8,128)(2,1)}, f32[8,128,128]{2,1,0:T(8,128)}) custom-call(s32[8]{0:T(128)} %fusion.106.index, s32[8,128,2]{2,1,0:T(8,128)} %copy.214.info, bf16[8,128,1024]{2,1,0:T(8,128)(2,1)} %get-tuple-element.146.query, bf16[8,256,2048]{2,1,0:T(8,128)(2,1)} %get-tuple-element.147.keys.values, ...), custom_call_target="tpu_custom_call" | custom-call | flops 8589934592 | bytes 16777216 | tf_op jit(solution)/shard_map/pallas_call | solution.py:368
  254.2 4.9 fusion.20
  265.1 4.9 fusion.23
  270.1 26.1 %collective-permute-done.9 = bf16[256,2048]{1,0:T(8,128)(2,1)} collective-permute-done((bf16[256,2048]{1,0:T(8,128)(2,1)}, bf16[256,2048]{1,0:T(8,128)(2,1)}, u32[]{:S(2)}, u32[]{:S(2)}) %collective-permute-start.9) | collective-permute-done | bytes 1048608 | tf_op jit(solution)/shard_map/ppermute | solution.py:44
  306.3 25.1 %collective-permute-done.13 = bf16[256,2048]{1,0:T(8,128)(2,1)S(1)} collective-permute-done((bf16[256,2048]{1,0:T(8,128)(2,1)S(1)}, bf16[256,2048]{1,0:T(8,128)(2,1)S(1)}, u32[]{:S(2)}, u32[]{:S(2)}) %collective-permute-start.13) | collective-permute-done | bytes 1048608 | tf_op jit(solution)/shard_map/ppermute | solution.py:44
  337.5 11.4 shard_map.267.act_back
  355.5 11.4 shard_map.268.act_back
  367.9 7.0 shard_map.269
  381.1 4.7 collective-permute-done.20
  385.8 17.5 %collective-permute-done.21 = bf16[64,2176]{1,0:T(8,128)(2,1)S(1)} collective-permute-done((bf16[64,2176]{1,0:T(8,128)(2,1)}, bf16[64,2176]{1,0:T(8,128)(2,1)S(1)}, u32[]{:S(2)}, u32[]{:S(2)}) %collective-permute-start.21) | collective-permute-done | bytes 278560 | tf_op jit(solution)/shard_map/ppermute | solution.py:58
  410.4 5.7 collective-permute-done.25
  416.0 10.7 collective-permute-done.24
  427.9 32.9 %all-gather.19.cloned.1.call-done.rows = bf16[2048,2176]{1,0:T(8,128)(2,1)} async-done(((bf16[256,2176]{1,0:T(8,128)(2,1)}), bf16[2048,2176]{1,0:T(8,128)(2,1)}) %all-gather.19.cloned.1.call-update) | async-done | bytes 8912912 | tf_op jit(solution)/shard_map/all_gather | solution.py:74
  460.7 33.9 %shard_map.271 = (bf16[2048,2048]{1,0:T(8,128)(2,1)}, bf16[2048,704]{1,0:T(8,128)(2,1)}, bf16[2048,704]{1,0:T(8,128)(2,1)}, bf16[2048,704]{1,0:T(8,128)(2,1)}, b...) custom-call(bf16[2048,2176]{1,0:T(8,128)(2,1)} %all-gather.19.cloned.1.call-done.rows, f32[2048,704]{1,0:T(8,128)} %shard_map.267.act_back, ...), custom_call_target="tpu_custom_call" | custom-call | flops 23622320128 | bytes 62914560 | tf_op jit(solution)/shard_map/pallas_call | solution.py:667
  497.8 12.0 fusion.2
  509.8 8.2 fusion
  519.8 33.9 %shard_map.270 = (bf16[2048,2048]{1,0:T(8,128)(2,1)}, bf16[2048,704]{1,0:T(8,128)(2,1)}, bf16[2048,704]{1,0:T(8,128)(2,1)}, bf16[2048,704]{1,0:T(8,128)(2,1)}, b...) custom-call(bf16[2048,2176]{1,0:T(8,128)(2,1)} %all-gather.17.cloned.1.call-done.rows, f32[2048,704]{1,0:T(8,128)} %shard_map.268.act_back, ...), custom_call_target="tpu_custom_call" | custom-call | flops 23622320128 | bytes 62914560 | tf_op jit(solution)/shard_map/pallas_call | solution.py:667
  555.3 11.5 fusion.122
  567.0 10.8 convolution_convert_fusion.1
  577.8 16.8 %reduce-scatter.9.cloned.1.call-done = bf16[256,2048]{1,0:T(8,128)(2,1)} async-done(((bf16[2048,2048]{1,0:T(8,128)(2,1)}), bf16[256,2048]{1,0:T(8,128)(2,1)}) %reduce-scatter.9.cloned.1.call-update) | async-done | bytes 1048592 | tf_op jit(solution)/shard_map/reduce_scatter | solution.py:78
  602.2 11.3 convolution_convert_fusion
  613.5 5.6 collective-permute-done.30.refs_2_
  619.2 12.2 %convolution_add_fusion = f32[704,2048]{1,0:T(8,128)} fusion(f32[704,2048]{1,0:T(8,128)} %fusion.122, bf16[2048,704]{1,0:T(8,128)(2,1)} %get-tuple-element.203, bf16[2048,2048]{1,0:T(8,128)(2,1)} %all-gather.15.cloned.1.call-done.grads), kind=kOutput, calls=%fused_computation.21 | convolution fusion | flops 5907021824 | bytes 22806528 | tf_op jit(solution)/shard_map/dot_general | solution.py:28
  631.5 11.9 fusion.14
  643.4 8.3 fusion.17
  651.8 18.0 %reduce-scatter.7.cloned.1.call-done = bf16[256,2048]{1,0:T(8,128)(2,1)} async-done(((bf16[2048,2048]{1,0:T(8,128)(2,1)}), bf16[256,2048]{1,0:T(8,128)(2,1)}) %reduce-scatter.7.cloned.1.call-update) | async-done | bytes 1048592 | tf_op jit(solution)/shard_map/reduce_scatter | solution.py:78
  687.4 4.5 collective-permute-done.38.refs_5_
  691.9 9.9 collective-permute-done.39.refs_6_
  702.6 9.1 shard_map.272
  711.8 7.4 collective-permute-start.41
  720.9 5.4 collective-permute-done.41
  726.3 16.7 %collective-permute-done.42 = bf16[64,2048]{1,0:T(8,128)(2,1)S(1)} collective-permute-done((bf16[64,2048]{1,0:T(8,128)(2,1)}, bf16[64,2048]{1,0:T(8,128)(2,1)S(1)}, u32[]{:S(2)}, u32[]{:S(2)}) %collective-permute-start.42) | collective-permute-done | bytes 262176 | tf_op jit(solution)/shard_map/ppermute | solution.py:58
  747.0 5.6 collective-permute-done.44
  752.6 15.4 %collective-permute-done.45 = bf16[64,2048]{1,0:T(8,128)(2,1)S(1)} collective-permute-done((bf16[64,2048]{1,0:T(8,128)(2,1)S(1)}, bf16[64,2048]{1,0:T(8,128)(2,1)S(1)}, u32[]{:S(2)}, u32[]{:S(2)}) %collective-permute-start.45) | collective-permute-done | bytes 262176 | tf_op jit(solution)/shard_map/ppermute | solution.py:58
  769.0 23.6 %collective-permute-done.48 = bf16[256,2048]{1,0:T(8,128)(2,1)S(1)} collective-permute-done((bf16[256,2048]{1,0:T(8,128)(2,1)S(1)}, bf16[256,2048]{1,0:T(8,128)(2,1)S(1)}, u32[]{:S(2)}, u32[]{:S(2)}) %collective-permute-start.48) | collective-permute-done | bytes 1048608 | tf_op jit(solution)/shard_map/ppermute | solution.py:44
  794.8 9.4 fusion.34
  811.2 48.5 %shard_map.273 = (bf16[8,128,1024]{2,1,0:T(8,128)(2,1)}, bf16[8,256,1024]{2,1,0:T(8,128)(2,1)}, bf16[8,256,1024]{2,1,0:T(8,128)(2,1)}) custom-call(s32[8]{0:T(128)} %fusion.106.index, s32[8,128,2]{2,1,0:T(8,128)} %copy.214.info, bf16[8,128,1024]{2,1,0:T(8,128)(2,1)} %get-tuple-element.146.query, bf16[8,256,2048]{2,1,0:T(8,128)(2,1)} %get-tuple-element.147.keys.values, ...), custom_call_target="tpu_custom_call" | custom-call | flops 21474836480 | bytes 33554432 | tf_op jit(solution)/shard_map/pallas_call | solution.py:398
  859.8 13.0 %bitcast_convert_fusion.2 = bf16[2048,1024]{1,0:T(8,128)(2,1)S(1)} fusion(bf16[8,256,2048]{2,1,0:T(8,128)(2,1)} %get-tuple-element.145, bf16[8,256,1024]{2,1,0:T(8,128)(2,1)} %get-tuple-element.241.k_grad), kind=kOutput, calls=%fused_computation.2 | convolution fusion | flops 8592031744 | bytes 16777216 | tf_op jit(solution)/shard_map/dot_general | solution.py:28
  877.2 11.7 bitcast_convert_fusion.1
  903.8 12.9 %bitcast_convert_fusion = bf16[2048,1024]{1,0:T(8,128)(2,1)} fusion(bf16[8,256,2048]{2,1,0:T(8,128)(2,1)} %get-tuple-element.145, bf16[8,256,1024]{2,1,0:T(8,128)(2,1)S(1)} %convolution_convert_fusion.4.slots), kind=kOutput, calls=%fused_computation | convolution fusion | flops 8592031744 | bytes 16777216 | tf_op jit(solution)/shard_map/dot_general | solution.py:28
  938.2 22.1 %shard_map.274 = (bf16[256,2048]{1,0:T(8,128)(2,1)}, bf16[256,2048]{1,0:T(8,128)(2,1)}, bf16[256,2048]{1,0:T(8,128)(2,1)}, bf16[256,2048]{1,0:T(8,128)(2,1)}) custom-call(s32[1]{0:T(128)} %bitcast.4.place, bf16[8,256,1024]{2,1,0:T(8,128)(2,1)} %get-tuple-element.241.k_grad, bf16[8,256,1024]{2,1,0:T(8,128)(2,1)} %get-tuple-element.242.v_grad, ...), custom_call_target="tpu_custom_call" | custom-call | flops 12884901888 | bytes 25165824 | tf_op jit(solution)/shard_map/pallas_call | solution.py:616
  960.3 19.6 %collective-permute-done.54 = bf16[512,1024]{1,0:T(8,128)(2,1)} collective-permute-done((bf16[512,1024]{1,0:T(8,128)(2,1)}, bf16[512,1024]{1,0:T(8,128)(2,1)}, u32[]{:S(2)}, u32[]{:S(2)}) %collective-permute-start.54) | collective-permute-done | bytes 1048608 | tf_op jit(solution)/shard_map/ppermute | solution.py:52
  982.6 19.0 %collective-permute-done.55 = bf16[512,1024]{1,0:T(8,128)(2,1)} collective-permute-done((bf16[512,1024]{1,0:T(8,128)(2,1)}, bf16[512,1024]{1,0:T(8,128)(2,1)}, u32[]{:S(2)}, u32[]{:S(2)}) %collective-permute-start.55) | collective-permute-done | bytes 1048608 | tf_op jit(solution)/shard_map/ppermute | solution.py:52
  1005.7 22.8 %shard_map.275 = (bf16[256,2048]{1,0:T(8,128)(2,1)}, bf16[256,2048]{1,0:T(8,128)(2,1)}, bf16[256,2048]{1,0:T(8,128)(2,1)}, bf16[256,2048]{1,0:T(8,128)(2,1)}) custom-call(s32[1]{0:T(128)} %bitcast.4.place, bf16[8,256,1024]{2,1,0:T(8,128)(2,1)} %get-tuple-element.241.k_grad, bf16[8,256,1024]{2,1,0:T(8,128)(2,1)} %get-tuple-element.242.v_grad, ...), custom_call_target="tpu_custom_call" | custom-call | flops 12884901888 | bytes 25165824 | tf_op jit(solution)/shard_map/pallas_call | solution.py:616
  1028.5 8.3 convolution_convert_fusion.2
  1047.8 19.5 %collective-permute-done.58 = bf16[256,2048]{1,0:T(8,128)(2,1)S(1)} collective-permute-done((bf16[256,2048]{1,0:T(8,128)(2,1)S(1)}, bf16[256,2048]{1,0:T(8,128)(2,1)S(1)}, u32[]{:S(2)}, u32[]{:S(2)}) %collective-permute-start.58) | collective-permute-done | bytes 1048608 | tf_op jit(solution)/shard_map/ppermute | solution.py:44
  1067.4 20.8 %collective-permute-done.57 = bf16[256,2048]{1,0:T(8,128)(2,1)S(1)} collective-permute-done((bf16[256,2048]{1,0:T(8,128)(2,1)S(1)}, bf16[256,2048]{1,0:T(8,128)(2,1)S(1)}, u32[]{:S(2)}, u32[]{:S(2)}) %collective-permute-start.57) | collective-permute-done | bytes 1048608 | tf_op jit(solution)/shard_map/ppermute | solution.py:44
  1090.2 3.8 collective-permute-start.63
  1094.0 11.3 collective-permute-done.60
  1113.2 10.1 collective-permute-done.71.refs_1_
  1126.7 21.8 %collective-permute-done.61 = bf16[256,2048]{1,0:T(8,128)(2,1)} collective-permute-done((bf16[256,2048]{1,0:T(8,128)(2,1)}, bf16[256,2048]{1,0:T(8,128)(2,1)}, u32[]{:S(2)}, u32[]{:S(2)}) %collective-permute-start.61) | collective-permute-done | bytes 1048608 | tf_op jit(solution)/shard_map/ppermute | solution.py:142
  1148.5 4.4 multiply_reduce_fusion
  1172.6 6.2 collective-permute-done.69.refs_2_
  1178.8 9.5 collective-permute-done.70.refs_3_
  1189.1 3.8 shard_map.276
  (592 shorter events, 247.7 us)
Async XLA Ops:
  7.2 171.5 %all-gather.9.cloned.1.call-start = ((), (), s32[]{:S(2)}) async-start(), calls=%async_computation.6 | async-start | bytes 8192000 | tf_op jit(solution)/shard_map/all_gather | solution.py:916
  16.4 163.4 %all-gather.11.cloned.1.call-start = ((), (), s32[]{:S(2)}) async-start(), calls=%async_computation.7 | async-start | bytes 8192000 | tf_op jit(solution)/shard_map/all_gather | solution.py:917
  16.4 56.6 %collective-permute-start = (bf16[256,3200]{1,0:T(8,128)(2,1)S(1)}, bf16[256,3200]{1,0:T(8,128)(2,1)}, u32[]{:S(2)}, u32[]{:S(2)}) collective-permute-start(bf16[256,3200]{1,0:T(8,128)(2,1)S(1)} %get-tuple-element.143), channel_id=1, source_target_pairs={{0,1},{1,0},{2,3},{3,2},{4,5},{5,4},{6,7},{7,6},{8,9},{9,8},{10,11... | collective-permute-start | bytes 4915208 | tf_op jit(solution)/shard_map/ppermute | solution.py:44
  20.0 28.7 %collective-permute-start.1 = (bf16[256,2176]{1,0:T(8,128)(2,1)S(1)}, bf16[256,2176]{1,0:T(8,128)(2,1)S(1)}, u32[]{:S(2)}, u32[]{:S(2)}) collective-permute-start(bf16[256,2176]{1,0:T(8,128)(2,1)S(1)} %pad_maximum_fusion.2.refs_0_), channel_id=1, source_target_pairs={{0,6},{2,0},{4,2},{6,4},{1,7},{3,1},{5,3},{7,5},{8,14},{10,8},{12,... | collective-permute-start | bytes 3342344 | tf_op jit(solution)/shard_map/ppermute | solution.py:85
  23.7 48.3 %collective-permute-start.2 = (bf16[256,2176]{1,0:T(8,128)(2,1)S(1)}, bf16[256,2176]{1,0:T(8,128)(2,1)S(1)}, u32[]{:S(2)}, u32[]{:S(2)}) collective-permute-start(bf16[256,2176]{1,0:T(8,128)(2,1)S(1)} %pad_maximum_fusion.2.refs_0_), channel_id=1, source_target_pairs={{0,2},{2,4},{4,6},{6,0},{1,3},{3,5},{5,7},{7,1},{8,10},{10,12},{12... | collective-permute-start | bytes 3342344 | tf_op jit(solution)/shard_map/ppermute | solution.py:86
  73.0 181.2 %all-gather.21.cloned.1.call-start = ((), (), s32[]{:S(2)}) async-start(), calls=%async_computation.19 | async-start | bytes 5242880 | tf_op jit(solution)/shard_map/all_gather | solution.py:918
  73.1 37.5 %collective-permute-start.5 = (bf16[256,2176]{1,0:T(8,128)(2,1)}, bf16[256,2176]{1,0:T(8,128)(2,1)}, u32[]{:S(2)}, u32[]{:S(2)}) collective-permute-start(bf16[256,2176]{1,0:T(8,128)(2,1)} %copy-done.30), channel_id=1, source_target_pairs={{0,1},{1,0},{2,3},{3,2},{4,5},{5,4},{6,7},{7,6},{8,9},{9,8},{10,11... | collective-permute-start | bytes 3342344 | tf_op jit(solution)/shard_map/ppermute | solution.py:44
  74.1 263.4 %all-gather.13.cloned.1.call-start = ((), (), s32[]{:S(2)}) async-start(), calls=%async_computation.8 | async-start | bytes 9437184 | tf_op jit(solution)/shard_map/all_gather | solution.py:74
  86.4 21.5 %collective-permute-start.4 = (bf16[128,2176]{1,0:T(8,128)(2,1)}, bf16[128,2176]{1,0:T(8,128)(2,1)S(1)}, u32[]{:S(2)}, u32[]{:S(2)}) collective-permute-start(bf16[128,2176]{1,0:T(8,128)(2,1)} %slice.388), channel_id=1, source_target_pairs={{0,6},{2,0},{4,2},{6,4},{1,7},{3,1},{5,3},{7,5},{8,14},{10,8},{12,... | collective-permute-start | bytes 1671176 | tf_op jit(solution)/shard_map/ppermute | solution.py:90
  89.6 35.2 %collective-permute-start.6 = (bf16[256,2176]{1,0:T(8,128)(2,1)}, bf16[256,2176]{1,0:T(8,128)(2,1)}, u32[]{:S(2)}, u32[]{:S(2)}) collective-permute-start(bf16[256,2176]{1,0:T(8,128)(2,1)} %copy-done.44), channel_id=1, source_target_pairs={{0,1},{1,0},{2,3},{3,2},{4,5},{5,4},{6,7},{7,6},{8,9},{9,8},{10,11... | collective-permute-start | bytes 3342344 | tf_op jit(solution)/shard_map/ppermute | solution.py:44
  90.8 57.9 %collective-permute-start.8 = (bf16[256,2176]{1,0:T(8,128)(2,1)}, bf16[256,2176]{1,0:T(8,128)(2,1)}, u32[]{:S(2)}, u32[]{:S(2)}) collective-permute-start(bf16[256,2176]{1,0:T(8,128)(2,1)} %copy-done.45), channel_id=1, source_target_pairs={{0,1},{1,0},{2,3},{3,2},{4,5},{5,4},{6,7},{7,6},{8,9},{9,8},{10,11... | collective-permute-start | bytes 3342344 | tf_op jit(solution)/shard_map/ppermute | solution.py:44
  108.8 61.4 %collective-permute-start.7 = (bf16[256,2176]{1,0:T(8,128)(2,1)}, bf16[256,2176]{1,0:T(8,128)(2,1)}, u32[]{:S(2)}, u32[]{:S(2)}) collective-permute-start(bf16[256,2176]{1,0:T(8,128)(2,1)} %constant_dynamic-update-slice_fusion.refs_2_), channel_id=1, source_target_pairs={{0,1},{1,0},{2,3},{3,2},{4,5},{5,4},{6,7},{7,6},{8,9},{9,8},{10,11... | collective-permute-start | bytes 3342344 | tf_op jit(solution)/shard_map/ppermute | solution.py:44
  172.4 46.3 %collective-permute-start.17 = (bf16[2,64,2048]{2,1,0:T(8,128)(2,1)}, bf16[2,64,2048]{2,1,0:T(8,128)(2,1)S(1)}, u32[]{:S(2)}, u32[]{:S(2)}) collective-permute-start(bf16[2,64,2048]{2,1,0:T(8,128)(2,1)} %get-tuple-element.314), channel_id=1, source_target_pairs={{0,6},{2,0},{4,2},{6,4},{1,7},{3,1},{5,3},{7,5},{8,14},{10,8},{12,... | collective-permute-start | bytes 1572872 | tf_op jit(solution)/shard_map/ppermute | solution.py:58
  175.3 43.7 %collective-permute-start.18 = (bf16[2,64,2048]{2,1,0:T(8,128)(2,1)}, bf16[2,64,2048]{2,1,0:T(8,128)(2,1)S(1)}, u32[]{:S(2)}, u32[]{:S(2)}) collective-permute-start(bf16[2,64,2048]{2,1,0:T(8,128)(2,1)} %get-tuple-element.313), channel_id=1, source_target_pairs={{0,4},{2,6},{4,0},{6,2},{1,5},{3,7},{5,1},{7,3},{8,12},{10,14},{12... | collective-permute-start | bytes 1572872 | tf_op jit(solution)/shard_map/ppermute | solution.py:58
  175.6 43.5 %collective-permute-start.19 = (bf16[2,64,2048]{2,1,0:T(8,128)(2,1)S(1)}, bf16[2,64,2048]{2,1,0:T(8,128)(2,1)S(1)}, u32[]{:S(2)}, u32[]{:S(2)}) collective-permute-start(bf16[2,64,2048]{2,1,0:T(8,128)(2,1)S(1)} %get-tuple-element.312), channel_id=1, source_target_pairs={{0,2},{2,4},{4,6},{6,0},{1,3},{3,5},{5,7},{7,1},{8,10},{10,12},{12... | collective-permute-start | bytes 1572872 | tf_op jit(solution)/shard_map/ppermute | solution.py:58
  220.8 134.8 %all-gather.15.cloned.1.call-start = ((), (), s32[]{:S(2)}) async-start(), calls=%async_computation.9 | async-start | bytes 9437184 | tf_op jit(solution)/shard_map/all_gather | solution.py:74
  221.4 239.4 %all-gather.19.cloned.1.call-start = ((), (), s32[]{:S(2)}) async-start(), calls=%async_computation.12 | async-start | bytes 10027008 | tf_op jit(solution)/shard_map/all_gather | solution.py:74
  260.1 36.0 %collective-permute-start.9 = (bf16[256,2048]{1,0:T(8,128)(2,1)}, bf16[256,2048]{1,0:T(8,128)(2,1)}, u32[]{:S(2)}, u32[]{:S(2)}) collective-permute-start(bf16[256,2048]{1,0:T(8,128)(2,1)} %slice.407), channel_id=1, source_target_pairs={{0,1},{1,0},{2,3},{3,2},{4,5},{5,4},{6,7},{7,6},{8,9},{9,8},{10,11... | collective-permute-start | bytes 3145736 | tf_op jit(solution)/shard_map/ppermute | solution.py:44
  296.1 35.3 %collective-permute-start.13 = (bf16[256,2048]{1,0:T(8,128)(2,1)S(1)}, bf16[256,2048]{1,0:T(8,128)(2,1)S(1)}, u32[]{:S(2)}, u32[]{:S(2)}) collective-permute-start(bf16[256,2048]{1,0:T(8,128)(2,1)S(1)} %slice.417), channel_id=1, source_target_pairs={{0,1},{1,0},{2,3},{3,2},{4,5},{5,4},{6,7},{7,6},{8,9},{9,8},{10,11... | collective-permute-start | bytes 3145736 | tf_op jit(solution)/shard_map/ppermute | solution.py:44
  300.8 48.2 %collective-permute-start.10 = (bf16[64,2048]{1,0:T(8,128)(2,1)S(1)}, bf16[64,2048]{1,0:T(8,128)(2,1)S(1)}, u32[]{:S(2)}, u32[]{:S(2)}) collective-permute-start(bf16[64,2048]{1,0:T(8,128)(2,1)S(1)} %get-tuple-element.300), channel_id=1, source_target_pairs={{0,2},{2,4},{4,6},{6,0},{1,3},{3,5},{5,7},{7,1},{8,10},{10,12},{12... | collective-permute-start | bytes 786440 | tf_op jit(solution)/shard_map/ppermute | solution.py:58
  302.5 64.4 %collective-permute-start.11 = (bf16[64,2048]{1,0:T(8,128)(2,1)S(1)}, bf16[64,2048]{1,0:T(8,128)(2,1)S(1)}, u32[]{:S(2)}, u32[]{:S(2)}) collective-permute-start(bf16[64,2048]{1,0:T(8,128)(2,1)S(1)} %get-tuple-element.299), channel_id=1, source_target_pairs={{0,4},{2,6},{4,0},{6,2},{1,5},{3,7},{5,1},{7,3},{8,12},{10,14},{12... | collective-permute-start | bytes 786440 | tf_op jit(solution)/shard_map/ppermute | solution.py:58
  304.9 62.0 %collective-permute-start.12 = (bf16[64,2048]{1,0:T(8,128)(2,1)S(1)}, bf16[64,2048]{1,0:T(8,128)(2,1)S(1)}, u32[]{:S(2)}, u32[]{:S(2)}) collective-permute-start(bf16[64,2048]{1,0:T(8,128)(2,1)S(1)} %get-tuple-element.298), channel_id=1, source_target_pairs={{0,6},{2,0},{4,2},{6,4},{1,7},{3,1},{5,3},{7,5},{8,14},{10,8},{12,... | collective-permute-start | bytes 786440 | tf_op jit(solution)/shard_map/ppermute | solution.py:58
  332.5 34.4 %collective-permute-start.14 = (bf16[64,2048]{1,0:T(8,128)(2,1)S(1)}, bf16[64,2048]{1,0:T(8,128)(2,1)S(1)}, u32[]{:S(2)}, u32[]{:S(2)}) collective-permute-start(bf16[64,2048]{1,0:T(8,128)(2,1)S(1)} %get-tuple-element.296), channel_id=1, source_target_pairs={{0,2},{2,4},{4,6},{6,0},{1,3},{3,5},{5,7},{7,1},{8,10},{10,12},{12... | collective-permute-start | bytes 786440 | tf_op jit(solution)/shard_map/ppermute | solution.py:58
  335.0 32.0 %collective-permute-start.15 = (bf16[64,2048]{1,0:T(8,128)(2,1)S(1)}, bf16[64,2048]{1,0:T(8,128)(2,1)S(1)}, u32[]{:S(2)}, u32[]{:S(2)}) collective-permute-start(bf16[64,2048]{1,0:T(8,128)(2,1)S(1)} %get-tuple-element.295), channel_id=1, source_target_pairs={{0,4},{2,6},{4,0},{6,2},{1,5},{3,7},{5,1},{7,3},{8,12},{10,14},{12... | collective-permute-start | bytes 786440 | tf_op jit(solution)/shard_map/ppermute | solution.py:58
  348.9 18.1 %collective-permute-start.16 = (bf16[64,2048]{1,0:T(8,128)(2,1)S(1)}, bf16[64,2048]{1,0:T(8,128)(2,1)S(1)}, u32[]{:S(2)}, u32[]{:S(2)}) collective-permute-start(bf16[64,2048]{1,0:T(8,128)(2,1)S(1)} %get-tuple-element.294), channel_id=1, source_target_pairs={{0,6},{2,0},{4,2},{6,4},{1,7},{3,1},{5,3},{7,5},{8,14},{10,8},{12,... | collective-permute-start | bytes 786440 | tf_op jit(solution)/shard_map/ppermute | solution.py:58
  378.4 24.9 %collective-permute-start.21 = (bf16[64,2176]{1,0:T(8,128)(2,1)}, bf16[64,2176]{1,0:T(8,128)(2,1)S(1)}, u32[]{:S(2)}, u32[]{:S(2)}) collective-permute-start(bf16[64,2176]{1,0:T(8,128)(2,1)} %get-tuple-element.175), channel_id=1, source_target_pairs={{0,4},{2,6},{4,0},{6,2},{1,5},{3,7},{5,1},{7,3},{8,12},{10,14},{12... | collective-permute-start | bytes 835592 | tf_op jit(solution)/shard_map/ppermute | solution.py:58
  378.4 25.0 %collective-permute-start.22 = (bf16[64,2176]{1,0:T(8,128)(2,1)}, bf16[64,2176]{1,0:T(8,128)(2,1)S(1)}, u32[]{:S(2)}, u32[]{:S(2)}) collective-permute-start(bf16[64,2176]{1,0:T(8,128)(2,1)} %get-tuple-element.176), channel_id=1, source_target_pairs={{0,2},{2,4},{4,6},{6,0},{1,3},{3,5},{5,7},{7,1},{8,10},{10,12},{12... | collective-permute-start | bytes 835592 | tf_op jit(solution)/shard_map/ppermute | solution.py:58
  404.4 115.4 %all-gather.17.cloned.1.call-start = ((), (), s32[]{:S(2)}) async-start(), calls=%async_computation.10 | async-start | bytes 10027008 | tf_op jit(solution)/shard_map/all_gather | solution.py:74
  405.6 21.1 %collective-permute-start.24 = (bf16[64,2176]{1,0:T(8,128)(2,1)S(1)}, bf16[64,2176]{1,0:T(8,128)(2,1)S(1)}, u32[]{:S(2)}, u32[]{:S(2)}) collective-permute-start(bf16[64,2176]{1,0:T(8,128)(2,1)S(1)} %copy-done.98), channel_id=1, source_target_pairs={{0,4},{2,6},{4,0},{6,2},{1,5},{3,7},{5,1},{7,3},{8,12},{10,14},{12... | collective-permute-start | bytes 835592 | tf_op jit(solution)/shard_map/ppermute | solution.py:58
  407.5 19.2 %collective-permute-start.23 = (bf16[64,2176]{1,0:T(8,128)(2,1)S(1)}, bf16[64,2176]{1,0:T(8,128)(2,1)S(1)}, u32[]{:S(2)}, u32[]{:S(2)}) collective-permute-start(bf16[64,2176]{1,0:T(8,128)(2,1)S(1)} %copy-done.97), channel_id=1, source_target_pairs={{0,6},{2,0},{4,2},{6,4},{1,7},{3,1},{5,3},{7,5},{8,14},{10,8},{12,... | collective-permute-start | bytes 835592 | tf_op jit(solution)/shard_map/ppermute | solution.py:58
  427.8 166.8 %reduce-scatter.9.cloned.1.call-start = ((), (), s32[]{:S(2)}) async-start(), calls=%async_computation.13 | async-start | bytes 9437184 | tf_op jit(solution)/shard_map/reduce_scatter | solution.py:78
  494.7 175.1 %reduce-scatter.7.cloned.1.call-start = ((), (), s32[]{:S(2)}) async-start(), calls=%async_computation.11 | async-start | bytes 9437184 | tf_op jit(solution)/shard_map/reduce_scatter | solution.py:78
  496.2 21.8 %collective-permute-start.26 = (f32[4,256]{1,0:T(4,128)S(1)}, f32[4,256]{1,0:T(4,128)S(1)}, u32[]{:S(2)}, u32[]{:S(2)}) collective-permute-start(f32[4,256]{1,0:T(4,128)S(1)} %bitcast.340), channel_id=1, source_target_pairs={{0,1},{1,0},{2,3},{3,2},{4,5},{5,4},{6,7},{7,6},{8,9},{9,8},{10,11... | collective-permute-start | bytes 12296 | tf_op jit(solution)/shard_map/ppermute | solution.py:44
  518.0 36.0 %collective-permute-start.27 = (f32[2,256]{1,0:T(2,128)S(1)}, f32[2,256]{1,0:T(2,128)S(1)}, u32[]{:S(2)}, u32[]{:S(2)}) collective-permute-start(f32[2,256]{1,0:T(2,128)S(1)} %bitcast.346), channel_id=1, source_target_pairs={{0,8},{8,0},{16,24},{24,16},{1,9},{9,1},{17,25},{25,17},{2,10},{10... | collective-permute-start | bytes 6152 | tf_op jit(solution)/shard_map/ppermute | solution.py:48
  553.8 250.4 %reduce-scatter.11.cloned.1.call-start = ((), (), s32[]{:S(2)}) async-start(), calls=%async_computation.14 | async-start | bytes 9437184 | tf_op jit(solution)/shard_map/reduce_scatter | solution.py:78
  598.4 20.8 %collective-permute-start.30 = (bf16[64,2176]{1,0:T(8,128)(2,1)S(1)}, bf16[64,2176]{1,0:T(8,128)(2,1)S(1)}, u32[]{:S(2)}, u32[]{:S(2)}) collective-permute-start(bf16[64,2176]{1,0:T(8,128)(2,1)S(1)} %get-tuple-element.323), channel_id=1, source_target_pairs={{0,4},{2,6},{4,0},{6,2},{1,5},{3,7},{5,1},{7,3},{8,12},{10,14},{12... | collective-permute-start | bytes 835592 | tf_op jit(solution)/shard_map/ppermute | solution.py:58
  600.8 18.4 %collective-permute-start.31 = (bf16[64,2176]{1,0:T(8,128)(2,1)S(1)}, bf16[64,2176]{1,0:T(8,128)(2,1)S(1)}, u32[]{:S(2)}, u32[]{:S(2)}) collective-permute-start(bf16[64,2176]{1,0:T(8,128)(2,1)S(1)} %get-tuple-element.322), channel_id=1, source_target_pairs={{0,6},{2,0},{4,2},{6,4},{1,7},{3,1},{5,3},{7,5},{8,14},{10,8},{12,... | collective-permute-start | bytes 835592 | tf_op jit(solution)/shard_map/ppermute | solution.py:58
  669.8 229.2 %reduce-scatter.13.cloned.1.call-start = ((), (), s32[]{:S(2)}) async-start(), calls=%async_computation.15 | async-start | bytes 9437184 | tf_op jit(solution)/shard_map/reduce_scatter | solution.py:78
  681.9 20.0 %collective-permute-start.39 = (bf16[64,2176]{1,0:T(8,128)(2,1)S(1)}, bf16[64,2176]{1,0:T(8,128)(2,1)S(1)}, u32[]{:S(2)}, u32[]{:S(2)}) collective-permute-start(bf16[64,2176]{1,0:T(8,128)(2,1)S(1)} %get-tuple-element.319), channel_id=1, source_target_pairs={{0,4},{2,6},{4,0},{6,2},{1,5},{3,7},{5,1},{7,3},{8,12},{10,14},{12... | collective-permute-start | bytes 835592 | tf_op jit(solution)/shard_map/ppermute | solution.py:58
  719.2 23.8 %collective-permute-start.42 = (bf16[64,2048]{1,0:T(8,128)(2,1)}, bf16[64,2048]{1,0:T(8,128)(2,1)S(1)}, u32[]{:S(2)}, u32[]{:S(2)}) collective-permute-start(bf16[64,2048]{1,0:T(8,128)(2,1)} %get-tuple-element.218), channel_id=1, source_target_pairs={{0,4},{2,6},{4,0},{6,2},{1,5},{3,7},{5,1},{7,3},{8,12},{10,14},{12... | collective-permute-start | bytes 786440 | tf_op jit(solution)/shard_map/ppermute | solution.py:58
  720.6 22.5 %collective-permute-start.43 = (bf16[64,2048]{1,0:T(8,128)(2,1)}, bf16[64,2048]{1,0:T(8,128)(2,1)S(1)}, u32[]{:S(2)}, u32[]{:S(2)}) collective-permute-start(bf16[64,2048]{1,0:T(8,128)(2,1)} %get-tuple-element.219), channel_id=1, source_target_pairs={{0,2},{2,4},{4,6},{6,0},{1,3},{3,5},{5,7},{7,1},{8,10},{10,12},{12... | collective-permute-start | bytes 786440 | tf_op jit(solution)/shard_map/ppermute | solution.py:58
  743.1 25.0 %collective-permute-start.47 = (bf16[256,2048]{1,0:T(8,128)(2,1)S(1)}, bf16[256,2048]{1,0:T(8,128)(2,1)S(1)}, u32[]{:S(2)}, u32[]{:S(2)}) collective-permute-start(bf16[256,2048]{1,0:T(8,128)(2,1)S(1)} %constant_dynamic-update-slice_fusion.6), channel_id=1, source_target_pairs={{0,1},{1,0},{2,3},{3,2},{4,5},{5,4},{6,7},{7,6},{8,9},{9,8},{10,11... | collective-permute-start | bytes 3145736 | tf_op jit(solution)/shard_map/ppermute | solution.py:44
  744.5 23.6 %collective-permute-start.45 = (bf16[64,2048]{1,0:T(8,128)(2,1)S(1)}, bf16[64,2048]{1,0:T(8,128)(2,1)S(1)}, u32[]{:S(2)}, u32[]{:S(2)}) collective-permute-start(bf16[64,2048]{1,0:T(8,128)(2,1)S(1)} %copy-done.101), channel_id=1, source_target_pairs={{0,4},{2,6},{4,0},{6,2},{1,5},{3,7},{5,1},{7,3},{8,12},{10,14},{12... | collective-permute-start | bytes 786440 | tf_op jit(solution)/shard_map/ppermute | solution.py:58
  745.0 23.1 %collective-permute-start.46 = (bf16[64,2048]{1,0:T(8,128)(2,1)S(1)}, bf16[64,2048]{1,0:T(8,128)(2,1)S(1)}, u32[]{:S(2)}, u32[]{:S(2)}) collective-permute-start(bf16[64,2048]{1,0:T(8,128)(2,1)S(1)} %copy-done.100), channel_id=1, source_target_pairs={{0,2},{2,4},{4,6},{6,0},{1,3},{3,5},{5,7},{7,1},{8,10},{10,12},{12... | collective-permute-start | bytes 786440 | tf_op jit(solution)/shard_map/ppermute | solution.py:58
  768.2 24.4 %collective-permute-start.48 = (bf16[256,2048]{1,0:T(8,128)(2,1)S(1)}, bf16[256,2048]{1,0:T(8,128)(2,1)S(1)}, u32[]{:S(2)}, u32[]{:S(2)}) collective-permute-start(bf16[256,2048]{1,0:T(8,128)(2,1)S(1)} %constant_dynamic-update-slice_fusion.10), channel_id=1, source_target_pairs={{0,1},{1,0},{2,3},{3,2},{4,5},{5,4},{6,7},{7,6},{8,9},{9,8},{10,11... | collective-permute-start | bytes 3145736 | tf_op jit(solution)/shard_map/ppermute | solution.py:44
  794.7 209.4 %reduce-scatter.15.cloned.1.call-start = ((), (), s32[]{:S(2)}) async-start(), calls=%async_computation.16 | async-start | bytes 5242880 | tf_op jit(solution)/shard_map/reduce_scatter | solution.py:1079
  805.6 54.1 %collective-permute-start.32 = (bf16[64,2048]{1,0:T(8,128)(2,1)S(1)}, bf16[64,2048]{1,0:T(8,128)(2,1)S(1)}, u32[]{:S(2)}, u32[]{:S(2)}) collective-permute-start(bf16[64,2048]{1,0:T(8,128)(2,1)S(1)} %get-tuple-element.336), channel_id=1, source_target_pairs={{0,2},{2,4},{4,6},{6,0},{1,3},{3,5},{5,7},{7,1},{8,10},{10,12},{12... | collective-permute-start | bytes 786440 | tf_op jit(solution)/shard_map/ppermute | solution.py:58
  806.3 53.4 %collective-permute-start.33 = (bf16[64,2048]{1,0:T(8,128)(2,1)S(1)}, bf16[64,2048]{1,0:T(8,128)(2,1)S(1)}, u32[]{:S(2)}, u32[]{:S(2)}) collective-permute-start(bf16[64,2048]{1,0:T(8,128)(2,1)S(1)} %get-tuple-element.335), channel_id=1, source_target_pairs={{0,4},{2,6},{4,0},{6,2},{1,5},{3,7},{5,1},{7,3},{8,12},{10,14},{12... | collective-permute-start | bytes 786440 | tf_op jit(solution)/shard_map/ppermute | solution.py:58
  808.2 51.5 %collective-permute-start.34 = (bf16[64,2048]{1,0:T(8,128)(2,1)S(1)}, bf16[64,2048]{1,0:T(8,128)(2,1)S(1)}, u32[]{:S(2)}, u32[]{:S(2)}) collective-permute-start(bf16[64,2048]{1,0:T(8,128)(2,1)S(1)} %get-tuple-element.334), channel_id=1, source_target_pairs={{0,6},{2,0},{4,2},{6,4},{1,7},{3,1},{5,3},{7,5},{8,14},{10,8},{12,... | collective-permute-start | bytes 786440 | tf_op jit(solution)/shard_map/ppermute | solution.py:58
  916.7 236.2 %all-reduce.6.cloned.1.call-start = ((), (), s32[]{:S(2)}) async-start(), calls=%async_computation.17 | async-start | bytes 4194304 | tf_op jit(solution)/shard_map/psum | solution.py:1093
  931.2 48.6 %collective-permute-start.54 = (bf16[512,1024]{1,0:T(8,128)(2,1)}, bf16[512,1024]{1,0:T(8,128)(2,1)}, u32[]{:S(2)}, u32[]{:S(2)}) collective-permute-start(bf16[512,1024]{1,0:T(8,128)(2,1)} %fusion.33), channel_id=1, source_target_pairs={{0,16},{8,24},{16,0},{24,8},{1,17},{9,25},{17,1},{25,9},{2,18},{10... | collective-permute-start | bytes 3145736 | tf_op jit(solution)/shard_map/ppermute | solution.py:52
  931.8 69.8 %collective-permute-start.55 = (bf16[512,1024]{1,0:T(8,128)(2,1)}, bf16[512,1024]{1,0:T(8,128)(2,1)}, u32[]{:S(2)}, u32[]{:S(2)}) collective-permute-start(bf16[512,1024]{1,0:T(8,128)(2,1)} %fusion.32), channel_id=1, source_target_pairs={{0,16},{8,24},{16,0},{24,8},{1,17},{9,25},{17,1},{25,9},{2,18},{10... | collective-permute-start | bytes 3145736 | tf_op jit(solution)/shard_map/ppermute | solution.py:52
  934.3 69.8 %collective-permute-start.49 = (bf16[64,2048]{1,0:T(8,128)(2,1)}, bf16[64,2048]{1,0:T(8,128)(2,1)}, u32[]{:S(2)}, u32[]{:S(2)}) collective-permute-start(bf16[64,2048]{1,0:T(8,128)(2,1)} %get-tuple-element.339), channel_id=1, source_target_pairs={{0,2},{2,4},{4,6},{6,0},{1,3},{3,5},{5,7},{7,1},{8,10},{10,12},{12... | collective-permute-start | bytes 786440 | tf_op jit(solution)/shard_map/ppermute | solution.py:58
  934.3 69.8 %collective-permute-start.50 = (bf16[64,2048]{1,0:T(8,128)(2,1)}, bf16[64,2048]{1,0:T(8,128)(2,1)}, u32[]{:S(2)}, u32[]{:S(2)}) collective-permute-start(bf16[64,2048]{1,0:T(8,128)(2,1)} %get-tuple-element.338), channel_id=1, source_target_pairs={{0,4},{2,6},{4,0},{6,2},{1,5},{3,7},{5,1},{7,3},{8,12},{10,14},{12... | collective-permute-start | bytes 786440 | tf_op jit(solution)/shard_map/ppermute | solution.py:58
  935.1 69.1 %collective-permute-start.51 = (bf16[64,2048]{1,0:T(8,128)(2,1)}, bf16[64,2048]{1,0:T(8,128)(2,1)S(1)}, u32[]{:S(2)}, u32[]{:S(2)}) collective-permute-start(bf16[64,2048]{1,0:T(8,128)(2,1)} %get-tuple-element.337), channel_id=1, source_target_pairs={{0,6},{2,0},{4,2},{6,4},{1,7},{3,1},{5,3},{7,5},{8,14},{10,8},{12,... | collective-permute-start | bytes 786440 | tf_op jit(solution)/shard_map/ppermute | solution.py:58
  979.8 61.4 %collective-permute-start.56 = (bf16[256,2048]{1,0:T(8,128)(2,1)}, bf16[256,2048]{1,0:T(8,128)(2,1)}, u32[]{:S(2)}, u32[]{:S(2)}) collective-permute-start(bf16[256,2048]{1,0:T(8,128)(2,1)} %get-tuple-element.247), channel_id=1, source_target_pairs={{0,1},{1,0},{2,3},{3,2},{4,5},{5,4},{6,7},{7,6},{8,9},{9,8},{10,11... | collective-permute-start | bytes 3145736 | tf_op jit(solution)/shard_map/ppermute | solution.py:44
  1005.7 187.3 %reduce-scatter.17.cloned.1.call-start = ((), (), s32[]{:S(2)}) async-start(), calls=%async_computation.18 | async-start | bytes 5242880 | tf_op jit(solution)/shard_map/reduce_scatter | solution.py:1096
  1041.2 26.2 %collective-permute-start.58 = (bf16[256,2048]{1,0:T(8,128)(2,1)S(1)}, bf16[256,2048]{1,0:T(8,128)(2,1)S(1)}, u32[]{:S(2)}, u32[]{:S(2)}) collective-permute-start(bf16[256,2048]{1,0:T(8,128)(2,1)S(1)} %copy-done.96), channel_id=1, source_target_pairs={{0,1},{1,0},{2,3},{3,2},{4,5},{5,4},{6,7},{7,6},{8,9},{9,8},{10,11... | collective-permute-start | bytes 3145736 | tf_op jit(solution)/shard_map/ppermute | solution.py:44
  1041.9 46.3 %collective-permute-start.57 = (bf16[256,2048]{1,0:T(8,128)(2,1)S(1)}, bf16[256,2048]{1,0:T(8,128)(2,1)S(1)}, u32[]{:S(2)}, u32[]{:S(2)}) collective-permute-start(bf16[256,2048]{1,0:T(8,128)(2,1)S(1)} %copy-done.95), channel_id=1, source_target_pairs={{0,1},{1,0},{2,3},{3,2},{4,5},{5,4},{6,7},{7,6},{8,9},{9,8},{10,11... | collective-permute-start | bytes 3145736 | tf_op jit(solution)/shard_map/ppermute | solution.py:44
  1044.9 43.8 %collective-permute-start.62 = (bf16[128,2048]{1,0:T(8,128)(2,1)S(1)}, bf16[128,2048]{1,0:T(8,128)(2,1)S(1)}, u32[]{:S(2)}, u32[]{:S(2)}) collective-permute-start(bf16[128,2048]{1,0:T(8,128)(2,1)S(1)} %get-tuple-element.307), channel_id=1, source_target_pairs={{0,6},{2,0},{4,2},{6,4},{1,7},{3,1},{5,3},{7,5},{8,14},{10,8},{12,... | collective-permute-start | bytes 1572872 | tf_op jit(solution)/shard_map/ppermute | solution.py:127
  1088.2 38.5 %collective-permute-start.59 = (bf16[256,2048]{1,0:T(8,128)(2,1)}, bf16[256,2048]{1,0:T(8,128)(2,1)}, u32[]{:S(2)}, u32[]{:S(2)}) collective-permute-start(bf16[256,2048]{1,0:T(8,128)(2,1)} %get-tuple-element.257), channel_id=1, source_target_pairs={{0,1},{1,0},{2,3},{3,2},{4,5},{5,4},{6,7},{7,6},{8,9},{9,8},{10,11... | collective-permute-start | bytes 3145736 | tf_op jit(solution)/shard_map/ppermute | solution.py:44
  1090.2 36.5 %collective-permute-start.63 = (bf16[256,2048]{1,0:T(8,128)(2,1)}, bf16[256,2048]{1,0:T(8,128)(2,1)}, u32[]{:S(2)}, u32[]{:S(2)}) collective-permute-start(bf16[256,2048]{1,0:T(8,128)(2,1)} %pad_maximum_fusion.5), channel_id=1, source_target_pairs={{0,6},{2,0},{4,2},{6,4},{1,7},{3,1},{5,3},{7,5},{8,14},{10,8},{12,... | collective-permute-start | bytes 3145736 | tf_op jit(solution)/shard_map/ppermute | solution.py:143
  1106.9 41.6 %collective-permute-start.61 = (bf16[256,2048]{1,0:T(8,128)(2,1)}, bf16[256,2048]{1,0:T(8,128)(2,1)}, u32[]{:S(2)}, u32[]{:S(2)}) collective-permute-start(bf16[256,2048]{1,0:T(8,128)(2,1)} %pad_maximum_fusion.4), channel_id=1, source_target_pairs={{0,2},{2,4},{4,6},{6,0},{1,3},{3,5},{5,7},{7,1},{8,10},{10,12},{12... | collective-permute-start | bytes 3145736 | tf_op jit(solution)/shard_map/ppermute | solution.py:142
  1164.9 23.4 %collective-permute-start.70 = (bf16[256,1024]{1,0:T(8,128)(2,1)S(1)}, bf16[256,1024]{1,0:T(8,128)(2,1)S(1)}, u32[]{:S(2)}, u32[]{:S(2)}) collective-permute-start(bf16[256,1024]{1,0:T(8,128)(2,1)S(1)} %get-tuple-element.328), channel_id=1, source_target_pairs={{0,1},{1,0},{2,3},{3,2},{4,5},{5,4},{6,7},{7,6},{8,9},{9,8},{10,11... | collective-permute-start | bytes 1572872 | tf_op jit(solution)/shard_map/ppermute | solution.py:44
  (137 other events, 2312.7 us)
Sparse Core Ops, SparseCore 0:
  16.5 50.5 all-gather.8
  73.1 47.4 all-gather.10
  122.2 34.4 all-gather.20
  220.9 66.7 all-gather.12
  290.0 65.5 all-gather.14
  404.5 56.1 all-gather.18
  463.2 56.5 all-gather.16
  523.3 71.2 reduce-scatter.8
  598.5 71.2 reduce-scatter.6
  673.1 71.2 reduce-scatter.10
  794.8 70.4 reduce-scatter.12
  916.8 64.2 reduce-scatter.14
  1005.8 85.9 all-reduce.5
  1094.2 45.0 reduce-scatter.16

commit v4 on v3

--- a/solution.py
+++ b/solution.py
@@ -103,7 +103,11 @@
     return [lax.dynamic_index_in_dim(every, at, 0, keepdims=False) for at in wanted], []
 
 
-def group_scatter(own, other):
+def far_swap(other):
+    return swap_x(other[2]) if is_small() else None
+
+
+def group_scatter(own, other, far_took):
     count = lax.axis_size("expert")
     if not is_small():
         e_at, s_at = lax.axis_index("expert"), lax.axis_index("seq")
@@ -119,7 +123,6 @@
         return total.astype(F32), []
     half = own[0].shape[0] // 2
     halves = (slice(0, half), slice(half, 2 * half))
-    far_took = swap_x(other[2])
     near_took = [swap_x(after(other[1], far_took)), swap_x(after(other[3], far_took))]
     own_took = swap_x(after(other[0], *near_took))
     far = [add_low(own[2][rows], far_took[rows]) for rows in halves]
@@ -1073,24 +1076,24 @@
     if is_small():
         firsts = [dp_first(dots) for dots in both_dots]
         q_grad, both_grad = after((q_grad, both_grad), [far for _, far in firsts])
+    out_pairs += z_rounds(pieces_of(out_sums[1]), 1)
+    q_grad = after(q_grad, out_pairs)
     q_slots = jnp.einsum("bct,bch->bth", pick, q_grad, preferred_element_type=F32).astype(BF)
-    query_grads = t_dot(flat_normed, q_slots.reshape(total * tok, half)).astype(BF)
-    q_slots = after(q_slots, query_grads)
-    query_grads = lax.psum_scatter(query_grads, "dp", scatter_dimension=0, tiled=True)
 
     in_other = project_back(s_at, both_grad, q_slots, w_keep, w_took, experts, experts, dps)
+    far_took = far_swap(in_other)
     if is_small():
-        both_grads = [after(add_low(mine, swap_y(far)), in_other) for mine, far in firsts]
+        both_grads = [add_low(mine, after(swap_y(far), in_other)) for mine, far in firsts]
     else:
         both_grads = [
             lax.psum_scatter(dots, "dp", scatter_dimension=0, tiled=False) for dots in both_dots
         ]
-    out_pairs += z_rounds(pieces_of(out_sums[1]), 1)
-    both_grads = after(both_grads, query_grads)
-    q_slots = after(q_slots, both_grads, out_pairs)
+    q_slots = after(q_slots, both_grads, far_took)
     in_own = project_back(s_at, both_grad, q_slots, w_keep, w_took, 0, experts, dps)
-    one_sum, _ = group_scatter(in_own, in_other)
+    one_sum, _ = group_scatter(in_own, in_other, far_took)
     shared = lax.psum(jnp.stack(both_grads), "expert")
+    query_grads = t_dot(flat_normed, after(q_slots, in_own).reshape(total * tok, half)).astype(BF)
+    query_grads = lax.psum_scatter(query_grads, "dp", scatter_dimension=0, tiled=True)
     dh_rows = after(dh_rows, in_own)
     grad_out_w = t_dot(mixed.reshape(total * cap, half), dh_rows).astype(BF)
     grad_out_w = lax.psum_scatter(grad_out_w, "dp", scatter_dimension=0, tiled=True)
@@ -1100,14 +1103,17 @@
     output = hidden + dot(mlp_high, out_pairs) + dot(mlp_low, out_pairs)
     result_out = output.astype(BF).reshape(seq_count, stretch, width)
 
-    def joined(arrays):
+    def both_halves(arrays):
         arrays = [array.reshape(seqs, rows_own, half) for array in arrays]
         mine = [lax.dynamic_index_in_dim(array, s_at, 0, keepdims=False) for array in arrays]
         give = [lax.dynamic_index_in_dim(array, 1 - s_at, 0, keepdims=False) for array in arrays]
-        return join_columns(s_at, mine, [swap_x(array) for array in give], dps, F32)
-
-    (grad_query,) = joined([query_grads])
-    shared_grads = joined([shared[0], shared[1]])
+        return mine, [swap_x(array) for array in give]
+
+    shared_mine, shared_took = both_halves([shared[0], shared[1]])
+    one_sum = after(one_sum, shared_took)
+    shared_grads = join_columns(s_at, shared_mine, shared_took, dps, F32)
+    query_mine, query_took = both_halves([query_grads])
+    (grad_query,) = join_columns(s_at, query_mine, query_took, dps, F32)
 
     router_one_grad, router_one_input = gate_grads(
         normed_one, route_one, attn_idx, attn_gates, attn_gate_grad
@@ -1116,7 +1122,7 @@
     input_grad, norm_one_grad = norm_back(x_in, norm_one, normed_one_grad)
     grad_x = (hidden_total + input_grad).astype(BF).reshape(seq_count, stretch, width)
 
-    norm_one_grad = after(norm_one_grad, shared)
+    norm_one_grad = after(norm_one_grad, query_took)
     little = little_sum(
         jnp.concatenate(
             [norm_one_grad[None], router_one_grad.T, norm_two_grad, router_two_grad.T], axis=0

time: 1210 us -> 1180 us (0.975)
  waiting for transfers between devices: 521 us -> 471 us
  starting transfers between devices: 102 us -> 116 us
    ppermute x19, waiting for transfers between devices: 202 us -> 170 us  [swap_x(): return lax.ppermute(value, 'seq', flip(2, 1))]
    ppermute x5, waiting for transfers between devices: 42.6 us -> 12 us  [swap_y(): return lax.ppermute(value, 'dp', flip(4, 2))]
    ppermute x1, waiting for transfers between devices: 21.8 us -> 4.08 us  [group_scatter(): from_below = lax.ppermute(up, 'expert', ring(count, 1))]
    ppermute x1, waiting for transfers between devices: 0.01 us -> 13.9 us  [group_scatter(): far_down = lax.ppermute(far[1], 'expert', ring(count, -1))]
    reduce_scatter x1, waiting for transfers between devices: 0.02 us -> 13.7 us  [body(): lax.psum_scatter(query_grads, 'dp', scatter_dimension=0, tiled=True)]
    unnamed x260 -> x222, local copies, waits for them, and re-layouts: 33.4 us -> 29.6 us
  transfers between devices with their start and end apart: 86 -> 86, of which waited for: 44 -> 43; matrix products, arithmetic and copies ran while one was open for 21% -> 24% of each run, Pallas kernels for 22% -> 23%
where the time goes in v4:
time: 1180 us; the launch traced here: 1170 us
  waiting for transfers between devices  471 us (40%)
  Pallas kernels  272 us (23%)
  matrix products  172 us (15%)
  starting transfers between devices  116 us (10%)
  local copies, waits for them, and re-layouts  77.6 us (7%)
  other arithmetic  44.4 us (4%)
  between operations  15.8 us (1%)
    ppermute x19, waiting for transfers between devices, swap_x(): return lax.ppermute(value, 'seq', flip(2, 1))  170 us
    dot_general x11, matrix products, t_dot(): lax.dot_general(left, right, (((0,), (0,)), ((), ())), preferred_element_...  114 us
    ppermute x33, waiting for transfers between devices, z_rounds(): lax.ppermute(pieces[r], 'expert', ring(count, sign * r))  112 us
    pallas_call x2, Pallas kernels, expert_mlp(): pl.pallas_call(expert_kernel, grid=(every // size,), in_specs=[step_spec(...  67.8 us
    ppermute x33, starting transfers between devices, z_rounds(): lax.ppermute(pieces[r], 'expert', ring(count, sign * r))  59.7 us
    pallas_call x1, Pallas kernels, attend_back(): pl.pallas_call(functools.partial(attend_back_kernel, blocks=blocks), grid...  48.5 us
    pallas_call x2, Pallas kernels, project_back(): pl.pallas_call(functools.partial(back_kernel, dps=dps), grid_spec=pltpu.P...  44.5 us
    dot_general x7, matrix products, dot(): return jnp.dot(left, right, preferred_element_type=F32)  39.6 us
  transfers between devices with their start and end apart: 86, of which 43 were waited for; matrix products, arithmetic and copies ran while one was open for 24% of the time, Pallas kernels for 23%

profile of v4, /device:TPU:0, one launch (start us, length us, event | category | flops | bytes accessed | tf_op | source)
XLA Modules:
  0.0 1169.5 jit_solution(14458252673773614650)
XLA Ops:
  23.7 25.0 %collective-permute-done.1.refs_1_ = bf16[256,2176]{1,0:T(8,128)(2,1)S(1)} collective-permute-done((bf16[256,2176]{1,0:T(8,128)(2,1)S(1)}, bf16[256,2176]{1,0:T(8,128)(2,1)S(1)}, u32[]{:S(2)}, u32[]{:S(2)}) %collective-permute-start.1) | collective-permute-done | bytes 1114144 | tf_op jit(solution)/shard_map/ppermute | solution.py:85
  48.7 23.3 %collective-permute-done.2.refs_3_ = bf16[256,2176]{1,0:T(8,128)(2,1)S(1)} collective-permute-done((bf16[256,2176]{1,0:T(8,128)(2,1)S(1)}, bf16[256,2176]{1,0:T(8,128)(2,1)S(1)}, u32[]{:S(2)}, u32[]{:S(2)}) %collective-permute-start.2) | collective-permute-done | bytes 1114144 | tf_op jit(solution)/shard_map/ppermute | solution.py:86
  91.7 6.8 collective-permute-done.3
  100.4 7.5 collective-permute-done.4
  112.5 12.3 %collective-permute-done.6.refs_5_ = bf16[256,2176]{1,0:T(8,128)(2,1)} collective-permute-done((bf16[256,2176]{1,0:T(8,128)(2,1)}, bf16[256,2176]{1,0:T(8,128)(2,1)}, u32[]{:S(2)}, u32[]{:S(2)}) %collective-permute-start.6) | collective-permute-done | bytes 1114144 | tf_op jit(solution)/shard_map/ppermute | solution.py:44
  125.8 22.9 %collective-permute-done.8.refs_7_ = bf16[256,2176]{1,0:T(8,128)(2,1)} collective-permute-done((bf16[256,2176]{1,0:T(8,128)(2,1)}, bf16[256,2176]{1,0:T(8,128)(2,1)}, u32[]{:S(2)}, u32[]{:S(2)}) %collective-permute-start.8) | collective-permute-done | bytes 1114144 | tf_op jit(solution)/shard_map/ppermute | solution.py:44
  149.7 20.5 %collective-permute-done.7.refs_6_ = bf16[256,2176]{1,0:T(8,128)(2,1)} collective-permute-done((bf16[256,2176]{1,0:T(8,128)(2,1)}, bf16[256,2176]{1,0:T(8,128)(2,1)}, u32[]{:S(2)}, u32[]{:S(2)}) %collective-permute-start.7) | collective-permute-done | bytes 1114144 | tf_op jit(solution)/shard_map/ppermute | solution.py:44
  182.4 36.3 %shard_map.265 = (bf16[8,256,2048]{2,1,0:T(8,128)(2,1)}, bf16[8,256,2048]{2,1,0:T(8,128)(2,1)}, bf16[8,128,1024]{2,1,0:T(8,128)(2,1)}) custom-call(s32[1]{0:T(128)} %bitcast.4.place, f32[1,2048]{1,0:T(1,128)} %bitcast.327, bf16[8,128,256]{2,1,0:T(8,128)(2,1)} %fusion.41.pick, bf16[1024,3200]{1,0:T(8,128)(2,1)} %all-gather.9.cloned.1.call-done.keep, ...), custom_call_target="tpu_custom_call" | custom-call | flops 21474836480 | bytes 41943040 | tf_op jit(solution)/shard_map/pallas_call | solution.py:558
  223.6 27.5 %shard_map.266 = (bf16[8,128,1024]{2,1,0:T(8,128)(2,1)}, f32[8,128,128]{2,1,0:T(8,128)}) custom-call(s32[8]{0:T(128)} %fusion.106.index, s32[8,128,2]{2,1,0:T(8,128)} %copy.214.info, bf16[8,128,1024]{2,1,0:T(8,128)(2,1)} %get-tuple-element.146.query, bf16[8,256,2048]{2,1,0:T(8,128)(2,1)} %get-tuple-element.147.keys.values, ...), custom_call_target="tpu_custom_call" | custom-call | flops 8589934592 | bytes 16777216 | tf_op jit(solution)/shard_map/pallas_call | solution.py:371
  254.2 4.9 fusion.20
  265.1 4.9 fusion.23
  270.1 26.1 %collective-permute-done.9 = bf16[256,2048]{1,0:T(8,128)(2,1)} collective-permute-done((bf16[256,2048]{1,0:T(8,128)(2,1)}, bf16[256,2048]{1,0:T(8,128)(2,1)}, u32[]{:S(2)}, u32[]{:S(2)}) %collective-permute-start.9) | collective-permute-done | bytes 1048608 | tf_op jit(solution)/shard_map/ppermute | solution.py:44
  306.4 25.0 %collective-permute-done.13 = bf16[256,2048]{1,0:T(8,128)(2,1)S(1)} collective-permute-done((bf16[256,2048]{1,0:T(8,128)(2,1)S(1)}, bf16[256,2048]{1,0:T(8,128)(2,1)S(1)}, u32[]{:S(2)}, u32[]{:S(2)}) %collective-permute-start.13) | collective-permute-done | bytes 1048608 | tf_op jit(solution)/shard_map/ppermute | solution.py:44
  337.5 11.4 shard_map.267.act_back
  355.6 11.4 shard_map.268.act_back
  368.0 7.0 shard_map.269
  381.2 4.7 collective-permute-done.20
  385.9 17.5 %collective-permute-done.21 = bf16[64,2176]{1,0:T(8,128)(2,1)S(1)} collective-permute-done((bf16[64,2176]{1,0:T(8,128)(2,1)}, bf16[64,2176]{1,0:T(8,128)(2,1)S(1)}, u32[]{:S(2)}, u32[]{:S(2)}) %collective-permute-start.21) | collective-permute-done | bytes 278560 | tf_op jit(solution)/shard_map/ppermute | solution.py:58
  410.5 5.7 collective-permute-done.25
  416.1 10.7 collective-permute-done.24
  427.9 32.9 %all-gather.19.cloned.1.call-done.rows = bf16[2048,2176]{1,0:T(8,128)(2,1)} async-done(((bf16[256,2176]{1,0:T(8,128)(2,1)}), bf16[2048,2176]{1,0:T(8,128)(2,1)}) %all-gather.19.cloned.1.call-update) | async-done | bytes 8912912 | tf_op jit(solution)/shard_map/all_gather | solution.py:74
  460.8 33.9 %shard_map.271 = (bf16[2048,2048]{1,0:T(8,128)(2,1)}, bf16[2048,704]{1,0:T(8,128)(2,1)}, bf16[2048,704]{1,0:T(8,128)(2,1)}, bf16[2048,704]{1,0:T(8,128)(2,1)}, b...) custom-call(bf16[2048,2176]{1,0:T(8,128)(2,1)} %all-gather.19.cloned.1.call-done.rows, f32[2048,704]{1,0:T(8,128)} %shard_map.267.act_back, ...), custom_call_target="tpu_custom_call" | custom-call | flops 23622320128 | bytes 62914560 | tf_op jit(solution)/shard_map/pallas_call | solution.py:670
  497.9 12.0 %fusion.2 = f32[2048,704]{0,1:T(8,128)} fusion(bf16[2048,704]{1,0:T(8,128)(2,1)} %get-tuple-element.185, bf16[2048,2176]{1,0:T(8,128)(2,1)} %all-gather.19.cloned.1.call-done.rows), kind=kOutput, calls=%fused_computation.7 | convolution fusion | flops 5905580032 | bytes 17301504 | tf_op jit(solution)/shard_map/dot_general | solution.py:28
  509.9 8.3 fusion
  519.9 33.9 %shard_map.270 = (bf16[2048,2048]{1,0:T(8,128)(2,1)}, bf16[2048,704]{1,0:T(8,128)(2,1)}, bf16[2048,704]{1,0:T(8,128)(2,1)}, bf16[2048,704]{1,0:T(8,128)(2,1)}, b...) custom-call(bf16[2048,2176]{1,0:T(8,128)(2,1)} %all-gather.17.cloned.1.call-done.rows, f32[2048,704]{1,0:T(8,128)} %shard_map.268.act_back, ...), custom_call_target="tpu_custom_call" | custom-call | flops 23622320128 | bytes 62914560 | tf_op jit(solution)/shard_map/pallas_call | solution.py:670
  555.4 11.5 fusion.122
  567.1 10.8 convolution_convert_fusion.1
  578.0 16.7 %reduce-scatter.9.cloned.1.call-done = bf16[256,2048]{1,0:T(8,128)(2,1)} async-done(((bf16[2048,2048]{1,0:T(8,128)(2,1)}), bf16[256,2048]{1,0:T(8,128)(2,1)}) %reduce-scatter.9.cloned.1.call-update) | async-done | bytes 1048592 | tf_op jit(solution)/shard_map/reduce_scatter | solution.py:78
  602.3 11.3 convolution_convert_fusion
  613.6 5.7 collective-permute-done.30.refs_2_
  619.3 12.2 %convolution_add_fusion = f32[704,2048]{1,0:T(8,128)} fusion(f32[704,2048]{1,0:T(8,128)} %fusion.122, bf16[2048,704]{1,0:T(8,128)(2,1)} %get-tuple-element.203, bf16[2048,2048]{1,0:T(8,128)(2,1)} %all-gather.15.cloned.1.call-done.grads), kind=kOutput, calls=%fused_computation.21 | convolution fusion | flops 5907021824 | bytes 22806528 | tf_op jit(solution)/shard_map/dot_general | solution.py:28
  631.5 11.9 %fusion.14 = f32[2048,704]{0,1:T(8,128)} fusion(f32[2048,704]{0,1:T(8,128)} %fusion.2, bf16[2048,704]{1,0:T(8,128)(2,1)S(1)} %copy-done.86, bf16[2048,2176]{1,0:T(8,128)(2,1)} %all-gather.17.cloned.1.call-done.rows), kind=kOutput, calls=%fused_computation.22 | convolution fusion | flops 5907021824 | bytes 22806528 | tf_op jit(solution)/shard_map/dot_general | solution.py:28
  643.5 8.3 fusion.17
  651.8 18.0 %reduce-scatter.7.cloned.1.call-done = bf16[256,2048]{1,0:T(8,128)(2,1)} async-done(((bf16[2048,2048]{1,0:T(8,128)(2,1)}), bf16[256,2048]{1,0:T(8,128)(2,1)}) %reduce-scatter.7.cloned.1.call-update) | async-done | bytes 1048592 | tf_op jit(solution)/shard_map/reduce_scatter | solution.py:78
  687.5 4.5 collective-permute-done.38.refs_5_
  692.0 9.9 collective-permute-done.39.refs_6_
  702.7 9.2 shard_map.272
  711.9 7.4 collective-permute-start.41
  721.0 5.4 collective-permute-done.41
  726.4 16.7 %collective-permute-done.42 = bf16[64,2048]{1,0:T(8,128)(2,1)S(1)} collective-permute-done((bf16[64,2048]{1,0:T(8,128)(2,1)}, bf16[64,2048]{1,0:T(8,128)(2,1)S(1)}, u32[]{:S(2)}, u32[]{:S(2)}) %collective-permute-start.42) | collective-permute-done | bytes 262176 | tf_op jit(solution)/shard_map/ppermute | solution.py:58
  747.2 5.5 collective-permute-done.44
  752.8 15.5 %collective-permute-done.45 = bf16[64,2048]{1,0:T(8,128)(2,1)S(1)} collective-permute-done((bf16[64,2048]{1,0:T(8,128)(2,1)S(1)}, bf16[64,2048]{1,0:T(8,128)(2,1)S(1)}, u32[]{:S(2)}, u32[]{:S(2)}) %collective-permute-start.45) | collective-permute-done | bytes 262176 | tf_op jit(solution)/shard_map/ppermute | solution.py:58
  769.1 23.6 %collective-permute-done.48 = bf16[256,2048]{1,0:T(8,128)(2,1)S(1)} collective-permute-done((bf16[256,2048]{1,0:T(8,128)(2,1)S(1)}, bf16[256,2048]{1,0:T(8,128)(2,1)S(1)}, u32[]{:S(2)}, u32[]{:S(2)}) %collective-permute-start.48) | collective-permute-done | bytes 1048608 | tf_op jit(solution)/shard_map/ppermute | solution.py:44
  795.0 9.3 fusion.34
  812.0 48.5 %shard_map.273 = (bf16[8,128,1024]{2,1,0:T(8,128)(2,1)}, bf16[8,256,1024]{2,1,0:T(8,128)(2,1)}, bf16[8,256,1024]{2,1,0:T(8,128)(2,1)}) custom-call(s32[8]{0:T(128)} %fusion.106.index, s32[8,128,2]{2,1,0:T(8,128)} %copy.214.info, bf16[8,128,1024]{2,1,0:T(8,128)(2,1)} %get-tuple-element.146.query, bf16[8,256,2048]{2,1,0:T(8,128)(2,1)} %get-tuple-element.147.keys.values, ...), custom_call_target="tpu_custom_call" | custom-call | flops 21474836480 | bytes 33554432 | tf_op jit(solution)/shard_map/pallas_call | solution.py:401
  860.6 12.8 %bitcast_convert_fusion.2 = bf16[2048,1024]{1,0:T(8,128)(2,1)S(1)} fusion(bf16[8,256,2048]{2,1,0:T(8,128)(2,1)} %get-tuple-element.145, bf16[8,256,1024]{2,1,0:T(8,128)(2,1)} %get-tuple-element.241.k_grad), kind=kOutput, calls=%fused_computation.2 | convolution fusion | flops 8592031744 | bytes 16777216 | tf_op jit(solution)/shard_map/dot_general | solution.py:28
  877.7 11.7 %bitcast_convert_fusion.1 = bf16[2048,1024]{1,0:T(8,128)(2,1)S(1)} fusion(bf16[8,256,2048]{2,1,0:T(8,128)(2,1)} %get-tuple-element.145, bf16[8,256,1024]{2,1,0:T(8,128)(2,1)S(1)} %copy-done.84), kind=kOutput, calls=%fused_computation.1 | convolution fusion | flops 8592031744 | bytes 16777216 | tf_op jit(solution)/shard_map/dot_general | solution.py:28
  907.8 10.0 collective-permute-done.50
  921.1 22.0 %shard_map.274 = (bf16[256,2048]{1,0:T(8,128)(2,1)}, bf16[256,2048]{1,0:T(8,128)(2,1)}, bf16[256,2048]{1,0:T(8,128)(2,1)}, bf16[256,2048]{1,0:T(8,128)(2,1)}) custom-call(s32[1]{0:T(128)} %bitcast.4.place, bf16[8,256,1024]{2,1,0:T(8,128)(2,1)} %get-tuple-element.241.k_grad, bf16[8,256,1024]{2,1,0:T(8,128)(2,1)} %get-tuple-element.242.v_grad, ...), custom_call_target="tpu_custom_call" | custom-call | flops 12884901888 | bytes 25165824 | tf_op jit(solution)/shard_map/pallas_call | solution.py:619
  943.8 6.9 collective-permute-done.55
  956.9 10.9 collective-permute-done.56
  967.7 22.5 %shard_map.275 = (bf16[256,2048]{1,0:T(8,128)(2,1)}, bf16[256,2048]{1,0:T(8,128)(2,1)}, bf16[256,2048]{1,0:T(8,128)(2,1)}, bf16[256,2048]{1,0:T(8,128)(2,1)}) custom-call(s32[1]{0:T(128)} %bitcast.4.place, bf16[8,256,1024]{2,1,0:T(8,128)(2,1)} %get-tuple-element.241.k_grad, bf16[8,256,1024]{2,1,0:T(8,128)(2,1)} %get-tuple-element.242.v_grad, ...), custom_call_target="tpu_custom_call" | custom-call | flops 12884901888 | bytes 25165824 | tf_op jit(solution)/shard_map/pallas_call | solution.py:619
  990.2 14.0 %bitcast_convert_fusion = bf16[2048,1024]{1,0:T(8,128)(2,1)} fusion(bf16[8,256,2048]{2,1,0:T(8,128)(2,1)} %get-tuple-element.145, bf16[8,256,1024]{2,1,0:T(8,128)(2,1)} %convolution_convert_fusion.4.slots), kind=kOutput, calls=%fused_computation | convolution fusion | flops 8592031744 | bytes 16777216 | tf_op jit(solution)/shard_map/dot_general | solution.py:28
  1012.4 9.4 convolution_convert_fusion.2
  1027.5 6.1 collective-permute-start.62
  1037.7 13.9 %collective-permute-done.62 = bf16[128,2048]{1,0:T(8,128)(2,1)S(1)} collective-permute-done((bf16[128,2048]{1,0:T(8,128)(2,1)S(1)}, bf16[128,2048]{1,0:T(8,128)(2,1)S(1)}, u32[]{:S(2)}, u32[]{:S(2)}) %collective-permute-start.62) | collective-permute-done | bytes 524320 | tf_op jit(solution)/shard_map/ppermute | solution.py:130
  1052.2 5.8 collective-permute-start.63
  1058.0 7.5 collective-permute-done.60
  1065.5 5.7 collective-permute-done.57
  1071.8 6.8 collective-permute-start.61
  1088.4 13.7 %reduce-scatter.15.cloned.1.call-done = bf16[512,1024]{1,0:T(8,128)(2,1)} async-done(((bf16[2048,1024]{1,0:T(8,128)(2,1)}), bf16[512,1024]{1,0:T(8,128)(2,1)}) %reduce-scatter.15.cloned.1.call-update) | async-done | bytes 1048592 | tf_op jit(solution)/shard_map/reduce_scatter | solution.py:1096
  1105.7 4.1 collective-permute-done.61
  1116.2 11.2 collective-permute-done.65.refs_3_
  1130.6 5.0 collective-permute-done.66.refs_1_
  (554 shorter events, 259.4 us)
Async XLA Ops:
  7.2 171.5 %all-gather.9.cloned.1.call-start = ((), (), s32[]{:S(2)}) async-start(), calls=%async_computation.6 | async-start | bytes 8192000 | tf_op jit(solution)/shard_map/all_gather | solution.py:919
  16.4 163.4 %all-gather.11.cloned.1.call-start = ((), (), s32[]{:S(2)}) async-start(), calls=%async_computation.7 | async-start | bytes 8192000 | tf_op jit(solution)/shard_map/all_gather | solution.py:920
  16.4 56.6 %collective-permute-start = (bf16[256,3200]{1,0:T(8,128)(2,1)S(1)}, bf16[256,3200]{1,0:T(8,128)(2,1)}, u32[]{:S(2)}, u32[]{:S(2)}) collective-permute-start(bf16[256,3200]{1,0:T(8,128)(2,1)S(1)} %get-tuple-element.143), channel_id=1, source_target_pairs={{0,1},{1,0},{2,3},{3,2},{4,5},{5,4},{6,7},{7,6},{8,9},{9,8},{10,11... | collective-permute-start | bytes 4915208 | tf_op jit(solution)/shard_map/ppermute | solution.py:44
  20.0 28.7 %collective-permute-start.1 = (bf16[256,2176]{1,0:T(8,128)(2,1)S(1)}, bf16[256,2176]{1,0:T(8,128)(2,1)S(1)}, u32[]{:S(2)}, u32[]{:S(2)}) collective-permute-start(bf16[256,2176]{1,0:T(8,128)(2,1)S(1)} %pad_maximum_fusion.2.refs_0_), channel_id=1, source_target_pairs={{0,6},{2,0},{4,2},{6,4},{1,7},{3,1},{5,3},{7,5},{8,14},{10,8},{12,... | collective-permute-start | bytes 3342344 | tf_op jit(solution)/shard_map/ppermute | solution.py:85
  23.7 48.3 %collective-permute-start.2 = (bf16[256,2176]{1,0:T(8,128)(2,1)S(1)}, bf16[256,2176]{1,0:T(8,128)(2,1)S(1)}, u32[]{:S(2)}, u32[]{:S(2)}) collective-permute-start(bf16[256,2176]{1,0:T(8,128)(2,1)S(1)} %pad_maximum_fusion.2.refs_0_), channel_id=1, source_target_pairs={{0,2},{2,4},{4,6},{6,0},{1,3},{3,5},{5,7},{7,1},{8,10},{10,12},{12... | collective-permute-start | bytes 3342344 | tf_op jit(solution)/shard_map/ppermute | solution.py:86
  73.0 181.2 %all-gather.21.cloned.1.call-start = ((), (), s32[]{:S(2)}) async-start(), calls=%async_computation.19 | async-start | bytes 5242880 | tf_op jit(solution)/shard_map/all_gather | solution.py:921
  73.1 37.5 %collective-permute-start.5 = (bf16[256,2176]{1,0:T(8,128)(2,1)}, bf16[256,2176]{1,0:T(8,128)(2,1)}, u32[]{:S(2)}, u32[]{:S(2)}) collective-permute-start(bf16[256,2176]{1,0:T(8,128)(2,1)} %copy-done.23), channel_id=1, source_target_pairs={{0,1},{1,0},{2,3},{3,2},{4,5},{5,4},{6,7},{7,6},{8,9},{9,8},{10,11... | collective-permute-start | bytes 3342344 | tf_op jit(solution)/shard_map/ppermute | solution.py:44
  74.1 263.4 %all-gather.13.cloned.1.call-start = ((), (), s32[]{:S(2)}) async-start(), calls=%async_computation.8 | async-start | bytes 9437184 | tf_op jit(solution)/shard_map/all_gather | solution.py:74
  86.4 21.5 %collective-permute-start.4 = (bf16[128,2176]{1,0:T(8,128)(2,1)}, bf16[128,2176]{1,0:T(8,128)(2,1)S(1)}, u32[]{:S(2)}, u32[]{:S(2)}) collective-permute-start(bf16[128,2176]{1,0:T(8,128)(2,1)} %slice.388), channel_id=1, source_target_pairs={{0,6},{2,0},{4,2},{6,4},{1,7},{3,1},{5,3},{7,5},{8,14},{10,8},{12,... | collective-permute-start | bytes 1671176 | tf_op jit(solution)/shard_map/ppermute | solution.py:90
  89.6 35.2 %collective-permute-start.6 = (bf16[256,2176]{1,0:T(8,128)(2,1)}, bf16[256,2176]{1,0:T(8,128)(2,1)}, u32[]{:S(2)}, u32[]{:S(2)}) collective-permute-start(bf16[256,2176]{1,0:T(8,128)(2,1)} %copy-done.34), channel_id=1, source_target_pairs={{0,1},{1,0},{2,3},{3,2},{4,5},{5,4},{6,7},{7,6},{8,9},{9,8},{10,11... | collective-permute-start | bytes 3342344 | tf_op jit(solution)/shard_map/ppermute | solution.py:44
  90.8 57.9 %collective-permute-start.8 = (bf16[256,2176]{1,0:T(8,128)(2,1)}, bf16[256,2176]{1,0:T(8,128)(2,1)}, u32[]{:S(2)}, u32[]{:S(2)}) collective-permute-start(bf16[256,2176]{1,0:T(8,128)(2,1)} %copy-done.35), channel_id=1, source_target_pairs={{0,1},{1,0},{2,3},{3,2},{4,5},{5,4},{6,7},{7,6},{8,9},{9,8},{10,11... | collective-permute-start | bytes 3342344 | tf_op jit(solution)/shard_map/ppermute | solution.py:44
  108.8 61.4 %collective-permute-start.7 = (bf16[256,2176]{1,0:T(8,128)(2,1)}, bf16[256,2176]{1,0:T(8,128)(2,1)}, u32[]{:S(2)}, u32[]{:S(2)}) collective-permute-start(bf16[256,2176]{1,0:T(8,128)(2,1)} %constant_dynamic-update-slice_fusion.refs_2_), channel_id=1, source_target_pairs={{0,1},{1,0},{2,3},{3,2},{4,5},{5,4},{6,7},{7,6},{8,9},{9,8},{10,11... | collective-permute-start | bytes 3342344 | tf_op jit(solution)/shard_map/ppermute | solution.py:44
  172.4 46.3 %collective-permute-start.17 = (bf16[2,64,2048]{2,1,0:T(8,128)(2,1)}, bf16[2,64,2048]{2,1,0:T(8,128)(2,1)S(1)}, u32[]{:S(2)}, u32[]{:S(2)}) collective-permute-start(bf16[2,64,2048]{2,1,0:T(8,128)(2,1)} %get-tuple-element.313), channel_id=1, source_target_pairs={{0,6},{2,0},{4,2},{6,4},{1,7},{3,1},{5,3},{7,5},{8,14},{10,8},{12,... | collective-permute-start | bytes 1572872 | tf_op jit(solution)/shard_map/ppermute | solution.py:58
  175.3 43.7 %collective-permute-start.18 = (bf16[2,64,2048]{2,1,0:T(8,128)(2,1)}, bf16[2,64,2048]{2,1,0:T(8,128)(2,1)S(1)}, u32[]{:S(2)}, u32[]{:S(2)}) collective-permute-start(bf16[2,64,2048]{2,1,0:T(8,128)(2,1)} %get-tuple-element.312), channel_id=1, source_target_pairs={{0,4},{2,6},{4,0},{6,2},{1,5},{3,7},{5,1},{7,3},{8,12},{10,14},{12... | collective-permute-start | bytes 1572872 | tf_op jit(solution)/shard_map/ppermute | solution.py:58
  175.6 43.5 %collective-permute-start.19 = (bf16[2,64,2048]{2,1,0:T(8,128)(2,1)S(1)}, bf16[2,64,2048]{2,1,0:T(8,128)(2,1)S(1)}, u32[]{:S(2)}, u32[]{:S(2)}) collective-permute-start(bf16[2,64,2048]{2,1,0:T(8,128)(2,1)S(1)} %get-tuple-element.311), channel_id=1, source_target_pairs={{0,2},{2,4},{4,6},{6,0},{1,3},{3,5},{5,7},{7,1},{8,10},{10,12},{12... | collective-permute-start | bytes 1572872 | tf_op jit(solution)/shard_map/ppermute | solution.py:58
  220.8 134.8 %all-gather.15.cloned.1.call-start = ((), (), s32[]{:S(2)}) async-start(), calls=%async_computation.9 | async-start | bytes 9437184 | tf_op jit(solution)/shard_map/all_gather | solution.py:74
  221.4 239.5 %all-gather.19.cloned.1.call-start = ((), (), s32[]{:S(2)}) async-start(), calls=%async_computation.12 | async-start | bytes 10027008 | tf_op jit(solution)/shard_map/all_gather | solution.py:74
  260.2 36.0 %collective-permute-start.9 = (bf16[256,2048]{1,0:T(8,128)(2,1)}, bf16[256,2048]{1,0:T(8,128)(2,1)}, u32[]{:S(2)}, u32[]{:S(2)}) collective-permute-start(bf16[256,2048]{1,0:T(8,128)(2,1)} %slice.407), channel_id=1, source_target_pairs={{0,1},{1,0},{2,3},{3,2},{4,5},{5,4},{6,7},{7,6},{8,9},{9,8},{10,11... | collective-permute-start | bytes 3145736 | tf_op jit(solution)/shard_map/ppermute | solution.py:44
  296.2 35.3 %collective-permute-start.13 = (bf16[256,2048]{1,0:T(8,128)(2,1)S(1)}, bf16[256,2048]{1,0:T(8,128)(2,1)S(1)}, u32[]{:S(2)}, u32[]{:S(2)}) collective-permute-start(bf16[256,2048]{1,0:T(8,128)(2,1)S(1)} %slice.417), channel_id=1, source_target_pairs={{0,1},{1,0},{2,3},{3,2},{4,5},{5,4},{6,7},{7,6},{8,9},{9,8},{10,11... | collective-permute-start | bytes 3145736 | tf_op jit(solution)/shard_map/ppermute | solution.py:44
  300.8 48.0 %collective-permute-start.10 = (bf16[64,2048]{1,0:T(8,128)(2,1)S(1)}, bf16[64,2048]{1,0:T(8,128)(2,1)S(1)}, u32[]{:S(2)}, u32[]{:S(2)}) collective-permute-start(bf16[64,2048]{1,0:T(8,128)(2,1)S(1)} %get-tuple-element.299), channel_id=1, source_target_pairs={{0,2},{2,4},{4,6},{6,0},{1,3},{3,5},{5,7},{7,1},{8,10},{10,12},{12... | collective-permute-start | bytes 786440 | tf_op jit(solution)/shard_map/ppermute | solution.py:58
  302.6 64.4 %collective-permute-start.11 = (bf16[64,2048]{1,0:T(8,128)(2,1)S(1)}, bf16[64,2048]{1,0:T(8,128)(2,1)S(1)}, u32[]{:S(2)}, u32[]{:S(2)}) collective-permute-start(bf16[64,2048]{1,0:T(8,128)(2,1)S(1)} %get-tuple-element.298), channel_id=1, source_target_pairs={{0,4},{2,6},{4,0},{6,2},{1,5},{3,7},{5,1},{7,3},{8,12},{10,14},{12... | collective-permute-start | bytes 786440 | tf_op jit(solution)/shard_map/ppermute | solution.py:58
  305.0 62.0 %collective-permute-start.12 = (bf16[64,2048]{1,0:T(8,128)(2,1)S(1)}, bf16[64,2048]{1,0:T(8,128)(2,1)S(1)}, u32[]{:S(2)}, u32[]{:S(2)}) collective-permute-start(bf16[64,2048]{1,0:T(8,128)(2,1)S(1)} %get-tuple-element.297), channel_id=1, source_target_pairs={{0,6},{2,0},{4,2},{6,4},{1,7},{3,1},{5,3},{7,5},{8,14},{10,8},{12,... | collective-permute-start | bytes 786440 | tf_op jit(solution)/shard_map/ppermute | solution.py:58
  332.5 34.5 %collective-permute-start.14 = (bf16[64,2048]{1,0:T(8,128)(2,1)S(1)}, bf16[64,2048]{1,0:T(8,128)(2,1)S(1)}, u32[]{:S(2)}, u32[]{:S(2)}) collective-permute-start(bf16[64,2048]{1,0:T(8,128)(2,1)S(1)} %get-tuple-element.295), channel_id=1, source_target_pairs={{0,2},{2,4},{4,6},{6,0},{1,3},{3,5},{5,7},{7,1},{8,10},{10,12},{12... | collective-permute-start | bytes 786440 | tf_op jit(solution)/shard_map/ppermute | solution.py:58
  335.0 32.0 %collective-permute-start.15 = (bf16[64,2048]{1,0:T(8,128)(2,1)S(1)}, bf16[64,2048]{1,0:T(8,128)(2,1)S(1)}, u32[]{:S(2)}, u32[]{:S(2)}) collective-permute-start(bf16[64,2048]{1,0:T(8,128)(2,1)S(1)} %get-tuple-element.294), channel_id=1, source_target_pairs={{0,4},{2,6},{4,0},{6,2},{1,5},{3,7},{5,1},{7,3},{8,12},{10,14},{12... | collective-permute-start | bytes 786440 | tf_op jit(solution)/shard_map/ppermute | solution.py:58
  378.5 24.9 %collective-permute-start.21 = (bf16[64,2176]{1,0:T(8,128)(2,1)}, bf16[64,2176]{1,0:T(8,128)(2,1)S(1)}, u32[]{:S(2)}, u32[]{:S(2)}) collective-permute-start(bf16[64,2176]{1,0:T(8,128)(2,1)} %get-tuple-element.175), channel_id=1, source_target_pairs={{0,4},{2,6},{4,0},{6,2},{1,5},{3,7},{5,1},{7,3},{8,12},{10,14},{12... | collective-permute-start | bytes 835592 | tf_op jit(solution)/shard_map/ppermute | solution.py:58
  378.5 25.0 %collective-permute-start.22 = (bf16[64,2176]{1,0:T(8,128)(2,1)}, bf16[64,2176]{1,0:T(8,128)(2,1)S(1)}, u32[]{:S(2)}, u32[]{:S(2)}) collective-permute-start(bf16[64,2176]{1,0:T(8,128)(2,1)} %get-tuple-element.176), channel_id=1, source_target_pairs={{0,2},{2,4},{4,6},{6,0},{1,3},{3,5},{5,7},{7,1},{8,10},{10,12},{12... | collective-permute-start | bytes 835592 | tf_op jit(solution)/shard_map/ppermute | solution.py:58
  404.5 115.4 %all-gather.17.cloned.1.call-start = ((), (), s32[]{:S(2)}) async-start(), calls=%async_computation.10 | async-start | bytes 10027008 | tf_op jit(solution)/shard_map/all_gather | solution.py:74
  405.7 21.1 %collective-permute-start.24 = (bf16[64,2176]{1,0:T(8,128)(2,1)S(1)}, bf16[64,2176]{1,0:T(8,128)(2,1)S(1)}, u32[]{:S(2)}, u32[]{:S(2)}) collective-permute-start(bf16[64,2176]{1,0:T(8,128)(2,1)S(1)} %copy-done.79), channel_id=1, source_target_pairs={{0,4},{2,6},{4,0},{6,2},{1,5},{3,7},{5,1},{7,3},{8,12},{10,14},{12... | collective-permute-start | bytes 835592 | tf_op jit(solution)/shard_map/ppermute | solution.py:58
  427.9 166.8 %reduce-scatter.9.cloned.1.call-start = ((), (), s32[]{:S(2)}) async-start(), calls=%async_computation.13 | async-start | bytes 9437184 | tf_op jit(solution)/shard_map/reduce_scatter | solution.py:78
  494.8 175.1 %reduce-scatter.7.cloned.1.call-start = ((), (), s32[]{:S(2)}) async-start(), calls=%async_computation.11 | async-start | bytes 9437184 | tf_op jit(solution)/shard_map/reduce_scatter | solution.py:78
  496.3 21.8 %collective-permute-start.26 = (f32[4,256]{1,0:T(4,128)S(1)}, f32[4,256]{1,0:T(4,128)S(1)}, u32[]{:S(2)}, u32[]{:S(2)}) collective-permute-start(f32[4,256]{1,0:T(4,128)S(1)} %bitcast.340), channel_id=1, source_target_pairs={{0,1},{1,0},{2,3},{3,2},{4,5},{5,4},{6,7},{7,6},{8,9},{9,8},{10,11... | collective-permute-start | bytes 12296 | tf_op jit(solution)/shard_map/ppermute | solution.py:44
  518.2 35.9 %collective-permute-start.27 = (f32[2,256]{1,0:T(2,128)S(1)}, f32[2,256]{1,0:T(2,128)S(1)}, u32[]{:S(2)}, u32[]{:S(2)}) collective-permute-start(f32[2,256]{1,0:T(2,128)S(1)} %bitcast.346), channel_id=1, source_target_pairs={{0,8},{8,0},{16,24},{24,16},{1,9},{9,1},{17,25},{25,17},{2,10},{10... | collective-permute-start | bytes 6152 | tf_op jit(solution)/shard_map/ppermute | solution.py:48
  553.9 250.4 %reduce-scatter.11.cloned.1.call-start = ((), (), s32[]{:S(2)}) async-start(), calls=%async_computation.14 | async-start | bytes 9437184 | tf_op jit(solution)/shard_map/reduce_scatter | solution.py:78
  598.4 20.8 %collective-permute-start.30 = (bf16[64,2176]{1,0:T(8,128)(2,1)S(1)}, bf16[64,2176]{1,0:T(8,128)(2,1)S(1)}, u32[]{:S(2)}, u32[]{:S(2)}) collective-permute-start(bf16[64,2176]{1,0:T(8,128)(2,1)S(1)} %get-tuple-element.322), channel_id=1, source_target_pairs={{0,4},{2,6},{4,0},{6,2},{1,5},{3,7},{5,1},{7,3},{8,12},{10,14},{12... | collective-permute-start | bytes 835592 | tf_op jit(solution)/shard_map/ppermute | solution.py:58
  669.9 224.6 %reduce-scatter.13.cloned.1.call-start = ((), (), s32[]{:S(2)}) async-start(), calls=%async_computation.15 | async-start | bytes 9437184 | tf_op jit(solution)/shard_map/reduce_scatter | solution.py:78
  681.9 20.0 %collective-permute-start.39 = (bf16[64,2176]{1,0:T(8,128)(2,1)S(1)}, bf16[64,2176]{1,0:T(8,128)(2,1)S(1)}, u32[]{:S(2)}, u32[]{:S(2)}) collective-permute-start(bf16[64,2176]{1,0:T(8,128)(2,1)S(1)} %get-tuple-element.318), channel_id=1, source_target_pairs={{0,4},{2,6},{4,0},{6,2},{1,5},{3,7},{5,1},{7,3},{8,12},{10,14},{12... | collective-permute-start | bytes 835592 | tf_op jit(solution)/shard_map/ppermute | solution.py:58
  719.3 23.8 %collective-permute-start.42 = (bf16[64,2048]{1,0:T(8,128)(2,1)}, bf16[64,2048]{1,0:T(8,128)(2,1)S(1)}, u32[]{:S(2)}, u32[]{:S(2)}) collective-permute-start(bf16[64,2048]{1,0:T(8,128)(2,1)} %get-tuple-element.218), channel_id=1, source_target_pairs={{0,4},{2,6},{4,0},{6,2},{1,5},{3,7},{5,1},{7,3},{8,12},{10,14},{12... | collective-permute-start | bytes 786440 | tf_op jit(solution)/shard_map/ppermute | solution.py:58
  720.7 22.5 %collective-permute-start.43 = (bf16[64,2048]{1,0:T(8,128)(2,1)}, bf16[64,2048]{1,0:T(8,128)(2,1)S(1)}, u32[]{:S(2)}, u32[]{:S(2)}) collective-permute-start(bf16[64,2048]{1,0:T(8,128)(2,1)} %get-tuple-element.219), channel_id=1, source_target_pairs={{0,2},{2,4},{4,6},{6,0},{1,3},{3,5},{5,7},{7,1},{8,10},{10,12},{12... | collective-permute-start | bytes 786440 | tf_op jit(solution)/shard_map/ppermute | solution.py:58
  743.2 25.1 %collective-permute-start.47 = (bf16[256,2048]{1,0:T(8,128)(2,1)S(1)}, bf16[256,2048]{1,0:T(8,128)(2,1)S(1)}, u32[]{:S(2)}, u32[]{:S(2)}) collective-permute-start(bf16[256,2048]{1,0:T(8,128)(2,1)S(1)} %constant_dynamic-update-slice_fusion.6), channel_id=1, source_target_pairs={{0,1},{1,0},{2,3},{3,2},{4,5},{5,4},{6,7},{7,6},{8,9},{9,8},{10,11... | collective-permute-start | bytes 3145736 | tf_op jit(solution)/shard_map/ppermute | solution.py:44
  744.7 23.6 %collective-permute-start.45 = (bf16[64,2048]{1,0:T(8,128)(2,1)S(1)}, bf16[64,2048]{1,0:T(8,128)(2,1)S(1)}, u32[]{:S(2)}, u32[]{:S(2)}) collective-permute-start(bf16[64,2048]{1,0:T(8,128)(2,1)S(1)} %copy-done.82), channel_id=1, source_target_pairs={{0,4},{2,6},{4,0},{6,2},{1,5},{3,7},{5,1},{7,3},{8,12},{10,14},{12... | collective-permute-start | bytes 786440 | tf_op jit(solution)/shard_map/ppermute | solution.py:58
  745.2 23.1 %collective-permute-start.46 = (bf16[64,2048]{1,0:T(8,128)(2,1)S(1)}, bf16[64,2048]{1,0:T(8,128)(2,1)S(1)}, u32[]{:S(2)}, u32[]{:S(2)}) collective-permute-start(bf16[64,2048]{1,0:T(8,128)(2,1)S(1)} %copy-done.81), channel_id=1, source_target_pairs={{0,2},{2,4},{4,6},{6,0},{1,3},{3,5},{5,7},{7,1},{8,10},{10,12},{12... | collective-permute-start | bytes 786440 | tf_op jit(solution)/shard_map/ppermute | solution.py:58
  768.3 24.4 %collective-permute-start.48 = (bf16[256,2048]{1,0:T(8,128)(2,1)S(1)}, bf16[256,2048]{1,0:T(8,128)(2,1)S(1)}, u32[]{:S(2)}, u32[]{:S(2)}) collective-permute-start(bf16[256,2048]{1,0:T(8,128)(2,1)S(1)} %constant_dynamic-update-slice_fusion.10), channel_id=1, source_target_pairs={{0,1},{1,0},{2,3},{3,2},{4,5},{5,4},{6,7},{7,6},{8,9},{9,8},{10,11... | collective-permute-start | bytes 3145736 | tf_op jit(solution)/shard_map/ppermute | solution.py:44
  794.9 287.6 %all-reduce.6.cloned.1.call-start = ((), (), s32[]{:S(2)}) async-start(), calls=%async_computation.16 | async-start | bytes 4194304 | tf_op jit(solution)/shard_map/psum | solution.py:1094
  806.5 54.0 %collective-permute-start.32 = (bf16[64,2048]{1,0:T(8,128)(2,1)S(1)}, bf16[64,2048]{1,0:T(8,128)(2,1)S(1)}, u32[]{:S(2)}, u32[]{:S(2)}) collective-permute-start(bf16[64,2048]{1,0:T(8,128)(2,1)S(1)} %get-tuple-element.335), channel_id=1, source_target_pairs={{0,2},{2,4},{4,6},{6,0},{1,3},{3,5},{5,7},{7,1},{8,10},{10,12},{12... | collective-permute-start | bytes 786440 | tf_op jit(solution)/shard_map/ppermute | solution.py:58
  807.1 53.4 %collective-permute-start.33 = (bf16[64,2048]{1,0:T(8,128)(2,1)S(1)}, bf16[64,2048]{1,0:T(8,128)(2,1)S(1)}, u32[]{:S(2)}, u32[]{:S(2)}) collective-permute-start(bf16[64,2048]{1,0:T(8,128)(2,1)S(1)} %get-tuple-element.334), channel_id=1, source_target_pairs={{0,4},{2,6},{4,0},{6,2},{1,5},{3,7},{5,1},{7,3},{8,12},{10,14},{12... | collective-permute-start | bytes 786440 | tf_op jit(solution)/shard_map/ppermute | solution.py:58
  808.9 51.6 %collective-permute-start.34 = (bf16[64,2048]{1,0:T(8,128)(2,1)S(1)}, bf16[64,2048]{1,0:T(8,128)(2,1)S(1)}, u32[]{:S(2)}, u32[]{:S(2)}) collective-permute-start(bf16[64,2048]{1,0:T(8,128)(2,1)S(1)} %get-tuple-element.333), channel_id=1, source_target_pairs={{0,6},{2,0},{4,2},{6,4},{1,7},{3,1},{5,3},{7,5},{8,14},{10,8},{12,... | collective-permute-start | bytes 786440 | tf_op jit(solution)/shard_map/ppermute | solution.py:58
  876.5 23.8 %collective-permute-start.52 = (bf16[2,512,1024]{2,1,0:T(8,128)(2,1)}, bf16[2,512,1024]{2,1,0:T(8,128)(2,1)S(1)}, u32[]{:S(2)}, u32[]{:S(2)}) collective-permute-start(bf16[2,512,1024]{2,1,0:T(8,128)(2,1)} %dynamic-slice_bitcast_fusion.1), channel_id=1, source_target_pairs={{0,8},{8,0},{16,24},{24,16},{1,9},{9,1},{17,25},{25,17},{2,10},{10... | collective-permute-start | bytes 6291464 | tf_op jit(solution)/shard_map/ppermute | solution.py:48
  896.4 21.4 %collective-permute-start.50 = (bf16[64,2048]{1,0:T(8,128)(2,1)S(1)}, bf16[64,2048]{1,0:T(8,128)(2,1)}, u32[]{:S(2)}, u32[]{:S(2)}) collective-permute-start(bf16[64,2048]{1,0:T(8,128)(2,1)S(1)} %get-tuple-element.337), channel_id=1, source_target_pairs={{0,4},{2,6},{4,0},{6,2},{1,5},{3,7},{5,1},{7,3},{8,12},{10,14},{12... | collective-permute-start | bytes 786440 | tf_op jit(solution)/shard_map/ppermute | solution.py:58
  897.2 20.6 %collective-permute-start.51 = (bf16[64,2048]{1,0:T(8,128)(2,1)S(1)}, bf16[64,2048]{1,0:T(8,128)(2,1)}, u32[]{:S(2)}, u32[]{:S(2)}) collective-permute-start(bf16[64,2048]{1,0:T(8,128)(2,1)S(1)} %get-tuple-element.336), channel_id=1, source_target_pairs={{0,6},{2,0},{4,2},{6,4},{1,7},{3,1},{5,3},{7,5},{8,14},{10,8},{12,... | collective-permute-start | bytes 786440 | tf_op jit(solution)/shard_map/ppermute | solution.py:58
  902.8 40.9 %collective-permute-start.54 = (bf16[512,1024]{1,0:T(8,128)(2,1)}, bf16[512,1024]{1,0:T(8,128)(2,1)}, u32[]{:S(2)}, u32[]{:S(2)}) collective-permute-start(bf16[512,1024]{1,0:T(8,128)(2,1)} %fusion.33), channel_id=1, source_target_pairs={{0,16},{8,24},{16,0},{24,8},{1,17},{9,25},{17,1},{25,9},{2,18},{10... | collective-permute-start | bytes 3145736 | tf_op jit(solution)/shard_map/ppermute | solution.py:52
  906.4 44.2 %collective-permute-start.55 = (bf16[512,1024]{1,0:T(8,128)(2,1)}, bf16[512,1024]{1,0:T(8,128)(2,1)}, u32[]{:S(2)}, u32[]{:S(2)}) collective-permute-start(bf16[512,1024]{1,0:T(8,128)(2,1)} %fusion.32), channel_id=1, source_target_pairs={{0,16},{8,24},{16,0},{24,8},{1,17},{9,25},{17,1},{25,9},{2,18},{10... | collective-permute-start | bytes 3145736 | tf_op jit(solution)/shard_map/ppermute | solution.py:52
  943.1 24.6 %collective-permute-start.56 = (bf16[256,2048]{1,0:T(8,128)(2,1)}, bf16[256,2048]{1,0:T(8,128)(2,1)S(1)}, u32[]{:S(2)}, u32[]{:S(2)}) collective-permute-start(bf16[256,2048]{1,0:T(8,128)(2,1)} %get-tuple-element.247), channel_id=1, source_target_pairs={{0,1},{1,0},{2,3},{3,2},{4,5},{5,4},{6,7},{7,6},{8,9},{9,8},{10,11... | collective-permute-start | bytes 3145736 | tf_op jit(solution)/shard_map/ppermute | solution.py:44
  956.8 145.2 %reduce-scatter.15.cloned.1.call-start = ((), (), s32[]{:S(2)}) async-start(), calls=%async_computation.17 | async-start | bytes 5242880 | tf_op jit(solution)/shard_map/reduce_scatter | solution.py:1096
  1004.3 151.9 %reduce-scatter.17.cloned.1.call-start = ((), (), s32[]{:S(2)}) async-start(), calls=%async_computation.18 | async-start | bytes 5242880 | tf_op jit(solution)/shard_map/reduce_scatter | solution.py:1099
  1024.8 26.8 %collective-permute-start.58 = (bf16[256,2048]{1,0:T(8,128)(2,1)}, bf16[256,2048]{1,0:T(8,128)(2,1)S(1)}, u32[]{:S(2)}, u32[]{:S(2)}) collective-permute-start(bf16[256,2048]{1,0:T(8,128)(2,1)} %get-tuple-element.254), channel_id=1, source_target_pairs={{0,1},{1,0},{2,3},{3,2},{4,5},{5,4},{6,7},{7,6},{8,9},{9,8},{10,11... | collective-permute-start | bytes 3145736 | tf_op jit(solution)/shard_map/ppermute | solution.py:44
  1027.5 24.1 %collective-permute-start.62 = (bf16[128,2048]{1,0:T(8,128)(2,1)S(1)}, bf16[128,2048]{1,0:T(8,128)(2,1)S(1)}, u32[]{:S(2)}, u32[]{:S(2)}) collective-permute-start(bf16[128,2048]{1,0:T(8,128)(2,1)S(1)} %get-tuple-element.306), channel_id=1, source_target_pairs={{0,6},{2,0},{4,2},{6,4},{1,7},{3,1},{5,3},{7,5},{8,14},{10,8},{12,... | collective-permute-start | bytes 1572872 | tf_op jit(solution)/shard_map/ppermute | solution.py:130
  1033.7 37.5 %collective-permute-start.57 = (bf16[256,2048]{1,0:T(8,128)(2,1)S(1)}, bf16[256,2048]{1,0:T(8,128)(2,1)S(1)}, u32[]{:S(2)}, u32[]{:S(2)}) collective-permute-start(bf16[256,2048]{1,0:T(8,128)(2,1)S(1)} %copy-done.77), channel_id=1, source_target_pairs={{0,1},{1,0},{2,3},{3,2},{4,5},{5,4},{6,7},{7,6},{8,9},{9,8},{10,11... | collective-permute-start | bytes 3145736 | tf_op jit(solution)/shard_map/ppermute | solution.py:44
  1037.7 27.8 %collective-permute-start.60 = (bf16[128,2048]{1,0:T(8,128)(2,1)S(1)}, bf16[128,2048]{1,0:T(8,128)(2,1)S(1)}, u32[]{:S(2)}, u32[]{:S(2)}) collective-permute-start(bf16[128,2048]{1,0:T(8,128)(2,1)S(1)} %get-tuple-element.305), channel_id=1, source_target_pairs={{0,2},{2,4},{4,6},{6,0},{1,3},{3,5},{5,7},{7,1},{8,10},{10,12},{12... | collective-permute-start | bytes 1572872 | tf_op jit(solution)/shard_map/ppermute | solution.py:129
  1052.2 52.0 %collective-permute-start.63 = (bf16[256,2048]{1,0:T(8,128)(2,1)S(1)}, bf16[256,2048]{1,0:T(8,128)(2,1)}, u32[]{:S(2)}, u32[]{:S(2)}) collective-permute-start(bf16[256,2048]{1,0:T(8,128)(2,1)S(1)} %pad_maximum_fusion.5), channel_id=1, source_target_pairs={{0,6},{2,0},{4,2},{6,4},{1,7},{3,1},{5,3},{7,5},{8,14},{10,8},{12,... | collective-permute-start | bytes 3145736 | tf_op jit(solution)/shard_map/ppermute | solution.py:146
  1071.8 38.0 %collective-permute-start.61 = (bf16[256,2048]{1,0:T(8,128)(2,1)S(1)}, bf16[256,2048]{1,0:T(8,128)(2,1)}, u32[]{:S(2)}, u32[]{:S(2)}) collective-permute-start(bf16[256,2048]{1,0:T(8,128)(2,1)S(1)} %pad_maximum_fusion.4), channel_id=1, source_target_pairs={{0,2},{2,4},{4,6},{6,0},{1,3},{3,5},{5,7},{7,1},{8,10},{10,12},{12... | collective-permute-start | bytes 3145736 | tf_op jit(solution)/shard_map/ppermute | solution.py:145
  1078.5 31.3 %collective-permute-start.59 = (bf16[256,2048]{1,0:T(8,128)(2,1)}, bf16[256,2048]{1,0:T(8,128)(2,1)}, u32[]{:S(2)}, u32[]{:S(2)}) collective-permute-start(bf16[256,2048]{1,0:T(8,128)(2,1)} %get-tuple-element.255), channel_id=1, source_target_pairs={{0,1},{1,0},{2,3},{3,2},{4,5},{5,4},{6,7},{7,6},{8,9},{9,8},{10,11... | collective-permute-start | bytes 3145736 | tf_op jit(solution)/shard_map/ppermute | solution.py:44
  1085.3 30.9 %collective-permute-start.64 = (bf16[256,1024]{1,0:T(8,128)(2,1)}, bf16[256,1024]{1,0:T(8,128)(2,1)}, u32[]{:S(2)}, u32[]{:S(2)}) collective-permute-start(bf16[256,1024]{1,0:T(8,128)(2,1)} %get-tuple-element.330), channel_id=1, source_target_pairs={{0,1},{1,0},{2,3},{3,2},{4,5},{5,4},{6,7},{7,6},{8,9},{9,8},{10,11... | collective-permute-start | bytes 1572872 | tf_op jit(solution)/shard_map/ppermute | solution.py:44
  1087.7 39.7 %collective-permute-start.65 = (bf16[256,1024]{1,0:T(8,128)(2,1)}, bf16[256,1024]{1,0:T(8,128)(2,1)}, u32[]{:S(2)}, u32[]{:S(2)}) collective-permute-start(bf16[256,1024]{1,0:T(8,128)(2,1)} %get-tuple-element.328), channel_id=1, source_target_pairs={{0,1},{1,0},{2,3},{3,2},{4,5},{5,4},{6,7},{7,6},{8,9},{9,8},{10,11... | collective-permute-start | bytes 1572872 | tf_op jit(solution)/shard_map/ppermute | solution.py:44
  1104.2 31.3 %collective-permute-start.66 = (bf16[256,1024]{1,0:T(8,128)(2,1)S(1)}, bf16[256,1024]{1,0:T(8,128)(2,1)S(1)}, u32[]{:S(2)}, u32[]{:S(2)}) collective-permute-start(bf16[256,1024]{1,0:T(8,128)(2,1)S(1)} %get-tuple-element.326), channel_id=1, source_target_pairs={{0,1},{1,0},{2,3},{3,2},{4,5},{5,4},{6,7},{7,6},{8,9},{9,8},{10,11... | collective-permute-start | bytes 1572872 | tf_op jit(solution)/shard_map/ppermute | solution.py:44
  (118 other events, 2223.0 us)
Sparse Core Ops, SparseCore 0:
  16.5 50.5 all-gather.8
  73.1 47.4 all-gather.10
  122.2 34.4 all-gather.20
  220.9 66.7 all-gather.12
  290.0 65.4 all-gather.14
  404.6 56.1 all-gather.18
  463.3 56.5 all-gather.16
  523.4 71.2 reduce-scatter.8
  598.6 71.2 reduce-scatter.6
  673.2 71.2 reduce-scatter.10
  795.0 70.4 reduce-scatter.12
  956.9 87.1 all-reduce.5
  1046.8 55.2 reduce-scatter.14
  1104.4 44.5 reduce-scatter.16
